TPU v7x, 128 devices: a whole 4x4x4 slice. The times are simulated.
128 devices in a mesh: row: 32 (over z, y, core), col: 4 (over x).
Axes of the slice: x: 4, y: 4, z: 4, core: 2. Of those that a mesh axis runs over, the one named last changes fastest.
Arguments:
- latent: bfloat16 [32, 4, 512, 256], P('row', 'col'), may hold values from -6 to 6
- cotangent: bfloat16 [32, 4, 512, 256], P('row', 'col'), may hold values from -6 to 6
- fine_w1: bfloat16 [512, 512], replicated, may hold values from -0.25 to 0.25
- fine_w2: bfloat16 [512, 256], replicated, may hold values from -0.25 to 0.25
- fine_gain: float32 [256], replicated, may hold values from 0.1 to 1.9
- coarse_w1: bfloat16 [512, 512], replicated, may hold values from -0.25 to 0.25
- coarse_w2: bfloat16 [512, 256], replicated, may hold values from -0.25 to 0.25
- coarse_gain: float32 [256], replicated, may hold values from 0.1 to 1.9
- fine_src: int32 [32, 4, 2048], P('row', 'col'), may hold values from 0 to 1023
- fine_dst: int32 [32, 4, 2048], P('row', 'col'), may hold values from 0 to 511
- live_blocks: int32 [32, 4], P('row', 'col'), may hold values from 8 to 16, as said below
- export_rows: int32 [32, 4, 128], P('row', 'col'), may hold values from 0 to 511
- pool_assign: int32 [32, 4, 512], P('row', 'col'), may hold values from 0 to 511
- coarse_src: int32 [32, 3072], P('row'), may hold values from 0 to 511
- coarse_dst: int32 [32, 3072], P('row'), may hold values from 0 to 511
Outputs:
- grad_latent: float32 [32, 4, 512, 256], P('row', 'col')
- grad_fine_w1: float32 [512, 512], replicated
- grad_fine_w2: float32 [512, 256], replicated
- grad_coarse_w1: float32 [512, 512], replicated
- grad_coarse_w2: float32 [512, 256], replicated
Inputs may be any that keep to these rules, and one draw needn't show every extreme that they name: `live_blocks`: some partition has all 16 blocks live.
All inputs are finite; a program needn't handle non-finite values.
Results may differ from a plain program's by a relative error of at most 0.0075.
Values may be sent and summed in bfloat16 or wider, within the bound.
No kernel may reach another device: no remote copies, remote signals or barrier semaphores. Data moves between devices by JAX's collectives and lax.ppermute only.
A program may use at most 128 MiB of HBM per device.

v0:
```python
import functools
import math

import jax
import jax.numpy as jnp
from jax import lax
from jax.experimental import pallas as pl
from jax.experimental.pallas import tpu as pltpu
from jax.sharding import Mesh
from jax.sharding import PartitionSpec as P

EPS = 1e-05
CNODE = 512
CHUNK = 1024
LIMITS = (20, 20, 36, 22)
BF = jnp.bfloat16
F32 = jnp.float32


def dot(left, right):
    return lax.dot_general(left, right, (((1,), (0,)), ((), ())), preferred_element_type=F32)


def dot_rt(left, right):
    return lax.dot_general(left, right, (((1,), (1,)), ((), ())), preferred_element_type=F32)


def dot_lt(left, right):
    return lax.dot_general(left, right, (((0,), (0,)), ((), ())), preferred_element_type=F32)


def halves(value):
    high = value.astype(BF)
    return high, (value - high.astype(F32)).astype(BF)


def spread_row(row):
    count = row.shape[1]
    return jnp.concatenate(
        [
            jnp.broadcast_to(row[:, at : at + 128], (128, 128)).T
            for at in range(0, count, 128)
        ],
        axis=0,
    )


def pick_matrix(row, width):
    column = spread_row(row)
    wide = jnp.concatenate([column] * (width // 128), axis=1)
    hit = wide == lax.broadcasted_iota(jnp.int32, wide.shape, 1)
    return jnp.where(hit, 1.0, 0.0).astype(BF)


def sum_matrix(row, width):
    shape = (width, row.shape[1])
    hit = lax.broadcasted_iota(jnp.int32, shape, 0) == row
    return jnp.where(hit, 1.0, 0.0).astype(BF)


def receivers_of(dst_ref, live_ref, at):
    row = dst_ref[:, at : at + CHUNK]
    slot = lax.broadcasted_iota(jnp.int32, row.shape, 1) + at
    return jnp.where(slot < 128 * live_ref[0, 0], row, -1)


def norm_of(summed):
    inverse = lax.rsqrt(jnp.mean(summed * summed, axis=-1, keepdims=True) + EPS)
    return inverse, summed * inverse


def summed_grad(grad_new, gain, summed):
    inverse, normed = norm_of(summed)
    grad_normed = grad_new * gain
    mean = jnp.mean(grad_normed * normed, axis=-1, keepdims=True)
    return (inverse * (grad_normed - normed * mean)).astype(BF)


def activations(preact):
    sig = jax.nn.sigmoid(preact)
    return (preact * sig).astype(BF), sig * (1.0 + preact * (1.0 - sig))


def start_kernel(own_ref, export_ref, cot_ref, assign_ref, rim_ref, pack_ref):
    rim_count = export_ref.shape[1]
    rim = dot(pick_matrix(export_ref[...], own_ref.shape[0]), own_ref[...]).astype(BF)
    rim_ref[...] = rim
    pack_ref[0:rim_count, :] = rim
    pool = sum_matrix(assign_ref[...], CNODE)
    pack_ref[rim_count : rim_count + CNODE, :] = dot(pool, cot_ref[...]).astype(BF)
    count = dot_rt(jnp.ones((16, pool.shape[1]), BF), pool)
    coarse_part = jnp.floor(count * (1.0 / 256.0)) * 256.0
    upper = lax.broadcasted_iota(jnp.int32, count.shape, 0) < 8
    packed = jnp.where(upper, coarse_part, count - coarse_part).astype(BF)
    at = rim_count + CNODE
    pack_ref[at : at + 16, :] = packed[:, :256]
    pack_ref[at + 16 : at + 32, :] = packed[:, 256:]


def own_kernel(own_ref, src_ref, dst_ref, live_ref, w1_ref, part_ref):
    nodes, feature = own_ref.shape
    for at in range(0, src_ref.shape[1], CHUNK):
        here = slice(at, at + CHUNK)
        left = dot(pick_matrix(src_ref[:, here], nodes), own_ref[...]).astype(BF)
        target = receivers_of(dst_ref, live_ref, at)
        right = dot(pick_matrix(target, nodes), own_ref[...]).astype(BF)
        part_ref[here, :] = dot(left, w1_ref[0:feature, :]) + dot(right, w1_ref[feature:, :])


def fine_forward_kernel(
    part_ref, own_ref, ra, rb, rw, re, src_ref, dst_ref, live_ref, core_ref, col_ref,
    w1_ref, w2_ref, gain_ref, assign_ref, slope_ref, acc_out, summed_ref, pooled_ref, table, acc,
):
    nodes, feature = own_ref.shape
    rim = ra.shape[0]
    core, col = core_ref[0], col_ref[0]
    table[0:nodes, :] = own_ref[...]
    table[pl.ds(pl.multiple_of(nodes + rim * (1 - core), rim), rim), :] = ra[...]
    table[pl.ds(pl.multiple_of(nodes + rim * core, rim), rim), :] = rb[...]
    west = rw[0:rim, :].astype(F32) * jnp.where(col > 0, 1.0, 0.0)
    east = re[0:rim, :].astype(F32) * jnp.where(col < 3, 1.0, 0.0)
    table[nodes + 2 * rim : nodes + 3 * rim, :] = west.astype(BF)
    table[nodes + 3 * rim :, :] = east.astype(BF)
    for at in range(0, src_ref.shape[1], CHUNK):
        here = slice(at, at + CHUNK)
        picks = pick_matrix(src_ref[:, here] - nodes, 4 * rim)
        left = dot(picks, table[nodes:, :]).astype(BF)
        preact = part_ref[here, :] + dot(left, w1_ref[0:feature, :])
        hidden, slope = activations(preact)
        slope_ref[here, :] = slope
        part = dot(sum_matrix(receivers_of(dst_ref, live_ref, at), nodes), hidden)
        if at == 0:
            acc[...] = part
        else:
            acc[...] += part
    high, low = halves(acc[...])
    acc_out[...] = high
    summed = dot(high, w2_ref[...]) + dot(low, w2_ref[...])
    summed_ref[...] = summed
    _, normed = norm_of(summed)
    fine_new = own_ref[...].astype(F32) + normed * gain_ref[...]
    high, low = halves(fine_new)
    pool = sum_matrix(assign_ref[...], CNODE)
    pooled_ref[...] = (dot(pool, high) + dot(pool, low)).astype(BF)


def coarse_kernel(
    p0, p1, p2, p3, p4, g0, g1, g2, g3, src_ref, dst_ref, w1_ref, w2_ref, gain_ref, cot_ref,
    assign_ref, col_ref, grad_fine_ref, pack_ref,
    table, slope, pick_t, sum_t, acc, by_src, by_dst,
):
    feature = p0.shape[1]
    edges = src_ref.shape[1]
    grads = []
    count = None
    for ref in (g0, g1, g2, g3):
        skip = ref.shape[0] - CNODE - 32
        grads.append(ref[skip : skip + CNODE, :].astype(F32))
        tail = ref[skip + CNODE :, :].astype(F32)
        tail = [tail[at : at + 1, :] + tail[at + 8 : at + 9, :] for at in (0, 16)]
        tail = jnp.concatenate(tail, axis=1)
        count = tail if count is None else count + tail
    grad_c1 = (grads[0] + grads[1]) + (grads[2] + grads[3])
    weight = spread_row(1.0 / jnp.maximum(count, 1.0))
    weight = jnp.concatenate([weight] * (feature // 128), axis=1)
    across = jnp.concatenate([p3[...].astype(F32), p4[...].astype(F32)], axis=0)
    pooled = (p0[...].astype(F32) + p1[...].astype(F32)) + (p2[...].astype(F32) + across)
    table[...] = (pooled * weight).astype(BF)
    for at in range(0, edges, CHUNK):
        here = slice(at, at + CHUNK)
        left = dot(pick_matrix(src_ref[:, here], CNODE), table[...]).astype(BF)
        pick = pick_matrix(dst_ref[:, here], CNODE)
        pick_t[here, :] = pick
        right = dot(pick, table[...]).astype(BF)
        preact = dot(left, w1_ref[0:feature, :]) + dot(right, w1_ref[feature:, :])
        hidden, slope[here, :] = activations(preact)
        adds = sum_matrix(dst_ref[:, here], CNODE)
        sum_t[:, here] = adds
        part = dot(adds, hidden)
        if at == 0:
            acc[...] = part
        else:
            acc[...] += part
    high, low = halves(acc[...])
    summed = dot(high, w2_ref[...]) + dot(low, w2_ref[...])
    grad_summed = summed_grad(grad_c1, gain_ref[...], summed)
    for at in range(0, edges, CHUNK):
        here = slice(at, at + CHUNK)
        grad_message = dot(pick_t[here, :], grad_summed).astype(BF)
        grad_preact = (dot_rt(grad_message, w2_ref[...]) * slope[here, :]).astype(BF)
        part_src = dot(sum_matrix(src_ref[:, here], CNODE), grad_preact)
        part_dst = dot(sum_t[:, here], grad_preact)
        if at == 0:
            by_src[...] = part_src
            by_dst[...] = part_dst
        else:
            by_src[...] += part_src
            by_dst[...] += part_dst
    grad_c0 = (
        grad_c1
        + dot_rt(by_src[...].astype(BF), w1_ref[0:feature, :])
        + dot_rt(by_dst[...].astype(BF), w1_ref[feature:, :])
    )
    high, low = halves(grad_c0 * weight)
    spread = pick_matrix(assign_ref[...], CNODE)
    grad_fine_ref[...] = cot_ref[...].astype(F32) + dot(spread, high) + dot(spread, low)
    own = pl.ds(pl.multiple_of(col_ref[0] * 128, 128), 128)
    for half, rows in enumerate((by_src, by_dst)):
        pack_ref[half, 0:256, :] = dot_lt(table[...], rows[:, own].astype(BF))
    second = dot_lt(acc[:, own].astype(BF), grad_summed)
    for half in range(2):
        for k in range(2):
            pack_ref[half, 256 + 64 * k : 320 + 64 * k, :] = second[
                64 * half : 64 * half + 64, 128 * k : 128 * k + 128
            ]


def fine_backward_kernel(
    grad_fine_ref, summed_ref, slope_ref, acc_ref, table_ref, src_ref, dst_ref,
    live_ref, core_ref, w1_ref, w2_ref, gain_ref, coarse_ref,
    local_ref, give_ref, keep_ref, ghost_b, ghost_w, ghost_e, by_src, by_dst, ghost,
):
    nodes, feature = grad_fine_ref.shape
    rim = ghost_b.shape[0]
    core = core_ref[0]
    grad_fine = grad_fine_ref[...]
    grad_summed = summed_grad(grad_fine, gain_ref[...], summed_ref[...])
    for at in range(0, src_ref.shape[1], CHUNK):
        here = slice(at, at + CHUNK)
        target = receivers_of(dst_ref, live_ref, at)
        grad_message = dot(pick_matrix(target, nodes), grad_summed).astype(BF)
        grad_preact = (dot_rt(grad_message, w2_ref[...]) * slope_ref[here, :]).astype(BF)
        part_src = dot(sum_matrix(src_ref[:, here], table_ref.shape[0]), grad_preact)
        part_dst = dot(sum_matrix(target, nodes), grad_preact)
        if at == 0:
            by_src[...] = part_src
            by_dst[...] = part_dst
        else:
            by_src[...] += part_src
            by_dst[...] += part_dst
    grad_table = dot_rt(by_src[...].astype(BF), w1_ref[0:feature, :])
    local_ref[...] = (
        grad_fine
        + grad_table[0:nodes, :]
        + dot_rt(by_dst[...].astype(BF), w1_ref[feature:, :])
    )
    ghost[...] = grad_table[nodes:, :].astype(BF)
    to_core = ghost[pl.ds(pl.multiple_of(rim * (1 - core), rim), rim), :]
    give_ref[1920 : 1920 + rim, :] = to_core[:, 0:128]
    give_ref[1920 + rim :, :] = to_core[:, 128:256]
    ghost_b[...] = ghost[pl.ds(pl.multiple_of(rim * core, rim), rim), :]
    for out, at in ((ghost_w, 2 * rim), (ghost_e, 3 * rim)):
        out[0:rim, :] = ghost[at : at + rim, 0:128]
        out[rim:, :] = ghost[at : at + rim, 128:256]
    for out, half in ((give_ref, 1 - core), (keep_ref, core)):
        part = pl.ds(pl.multiple_of(half * 256, 256), 256)
        first = dot_lt(table_ref[...], by_src[:, part].astype(BF)).astype(out.dtype)
        second = dot_lt(table_ref[0:nodes, :], by_dst[:, part].astype(BF)).astype(out.dtype)
        third = dot_lt(acc_ref[:, part], grad_summed).astype(out.dtype)
        for k in range(2):
            lanes = slice(128 * k, 128 * k + 128)
            out[512 * k : 512 * k + 256, :] = first[:, lanes]
            out[512 * k + 256 : 512 * k + 512, :] = second[:, lanes]
            out[1024 + 256 * k : 1280 + 256 * k, :] = third[:, lanes]
        out[1536:1920, :] = coarse_ref[half].astype(out.dtype)


def split_kernel(keep_ref, got_ref, ghost_w, ghost_e, col_ref, total_ref, coarse_ref, *sends):
    col = col_ref[0]

    def block(step):
        rows = pl.ds(pl.multiple_of(lax.rem(col + step, 4) * 384, 384), 384)
        return keep_ref[rows, :] + got_ref[rows, :].astype(F32)

    total_ref[...] = block(0)
    coarse_ref[...] = keep_ref[1536:1920, :] + got_ref[1536:1920, :].astype(F32)
    for step, out in enumerate(sends, 1):
        out[0:384, :] = block(step).astype(BF)
    sends[0][384:, :] = ghost_e[...]
    sends[2][384:, :] = ghost_w[...]


def return_kernel(local_ref, from_core, from_b, from_west, from_east, export_ref, col_ref, out_ref):
    rim = export_ref.shape[1]
    adds = sum_matrix(export_ref[...], local_ref.shape[0])
    col = col_ref[0]

    def wide(ref):
        at = ref.shape[0] - 2 * rim
        rows = ref[at:, :].astype(F32)
        return jnp.concatenate([rows[0:rim, :], rows[rim:, :]], axis=1)

    west = wide(from_west) * jnp.where(col > 0, 1.0, 0.0)
    east = wide(from_east) * jnp.where(col < 3, 1.0, 0.0)
    arrived = (wide(from_core) + from_b[...].astype(F32)) + (west + east)
    high, low = halves(arrived)
    out_ref[...] = local_ref[...] + dot(adds, high) + dot(adds, low)


def unpack_kernel(
    mine_ref, other_ref, core_ref, fine1_ref, fine2_ref, coarse1_ref, coarse2_ref,
    *, fine_scale, coarse_scale,
):
    for ref, half in ((mine_ref, core_ref[0]), (other_ref, 1 - core_ref[0])):
        for plane in range(16):
            for x in range(4):
                values = ref[plane * 4 + x].astype(F32)
                for at in range(0, 24, 8):
                    row = x * 384 + plane * 24 + at
                    piece = values[at : at + 8, :] * fine_scale
                    if row < 1024:
                        lanes = pl.ds(pl.multiple_of(half * 256 + row // 512 * 128, 128), 128)
                        fine1_ref[row % 512 : row % 512 + 8, lanes] = piece
                    else:
                        start = pl.multiple_of(half * 256 + row % 256, 8)
                        lane = (row - 1024) // 256 * 128
                        fine2_ref[pl.ds(start, 8), lane : lane + 128] = piece
                    row = plane * 24 + at
                    piece = values[24 + at : 32 + at, :] * coarse_scale
                    if row < 256:
                        start = pl.multiple_of(half * 256 + row, 8)
                        coarse1_ref[pl.ds(start, 8), x * 128 : x * 128 + 128] = piece
                    else:
                        start = pl.multiple_of(half * 64 + x * 128 + row % 64, 8)
                        lane = (row - 256) // 64 * 128
                        coarse2_ref[pl.ds(start, 8), lane : lane + 128] = piece


class Late:
    def __init__(self, source, held, sem):
        self.held = held
        self.shape = held.shape
        self.copy = pltpu.make_async_copy(source, held, sem)
        self.copy.start()

    def __getitem__(self, index):
        if self.copy is not None:
            self.copy.wait()
            self.copy = None
        return self.held[index]

    def finish(self):
        if self.copy is not None:
            self.copy.wait()
            self.copy = None


def run(kernel, outs, operands, scratch=(), scalars=(), late=(), inner=(), ahead=(), limit=16):
    size = sum(math.prod(x.shape) * x.dtype.itemsize for x in [*operands, *ahead]) + sum(
        math.prod(shape) * jnp.dtype(kind).itemsize for shape, kind in outs
    )
    shapes = [
        (pltpu.VMEM if i in inner else jax.ShapeDtypeStruct)(shape, kind)
        for i, (shape, kind) in enumerate(outs)
    ] + [pltpu.VMEM(x.shape, x.dtype) for x in ahead]
    operands = [
        pltpu.with_memory_space_constraint(x, pltpu.HBM) if i in late else x
        for i, x in enumerate(operands)
    ] + [pltpu.with_memory_space_constraint(x, pltpu.HBM) for x in ahead]
    count = len(operands) - len(ahead)
    first_out = len(operands)
    first_ahead = first_out + len(outs)
    first_scratch = first_ahead + len(ahead)
    first_held = first_scratch + len(scratch)

    def space(i):
        return pltpu.SMEM if i in scalars else pltpu.HBM if i in late or i >= count else pltpu.VMEM

    def body(*refs):
        sems = refs[-1]
        inputs = list(refs[:count])
        for k, i in enumerate(late):
            inputs[i] = Late(refs[i], refs[first_held + k], sems.at[k])
        fetched = [
            Late(refs[count + k], refs[first_ahead + k], sems.at[len(late) + k])
            for k in range(len(ahead))
        ]
        kernel(*inputs, *refs[first_out:first_ahead], *refs[first_scratch:first_held])
        for copy in [inputs[i] for i in late] + fetched:
            copy.finish()

    copies = len(late) + len(ahead)
    return pl.pallas_call(
        body if copies else kernel,
        out_shape=shapes,
        in_specs=[pl.BlockSpec(memory_space=space(i)) for i in range(first_out)],
        out_specs=[pl.BlockSpec(memory_space=pltpu.VMEM)] * len(shapes),
        scratch_shapes=[pltpu.VMEM(shape, kind) for shape, kind in scratch]
        + [pltpu.VMEM(operands[i].shape, operands[i].dtype) for i in late]
        + ([pltpu.SemaphoreType.DMA((copies,))] if copies else []),
        compiler_params=pltpu.CompilerParams(vmem_limit_bytes=limit * 1024 * 1024),
        cost_estimate=pl.CostEstimate(flops=0, bytes_accessed=size, transcendentals=0),
    )(*operands)


ROW = ("z", "y", "core")
PLANE = ("z", "y")
CHIPS = ("z", "y", "x")


def send(value, axis, step):
    size = lax.axis_size(axis)
    return lax.ppermute(value, axis, [(i, (i + step) % size) for i in range(size)])


def shards(
    latent, cotangent, fine_w1, fine_w2, fine_gain, coarse_w1, coarse_w2, coarse_gain,
    fine_src, fine_dst, live_blocks, export_rows, pool_assign, coarse_src, coarse_dst,
):
    own = latent[0, 0]
    cot = cotangent[0, 0]
    nodes, feature = own.shape
    export = export_rows[0]
    assign = pool_assign[0]
    src, dst = fine_src[0], fine_dst[0]
    rim_count = export.shape[1]
    hidden = fine_w1.shape[1]
    edges, coarse_edges = src.shape[1], coarse_src.shape[1]
    rows, cols = lax.axis_size(ROW), lax.axis_size("x")
    fine_gain = fine_gain[None, :]
    coarse_gain = coarse_gain[None, :]
    between = [(i, i + 1) for i in range(1, rows - 1, 2)]
    between = between + [(target, source) for source, target in between]
    column = lax.axis_index("x").astype(jnp.int32)[None]
    core = lax.axis_index("core").astype(jnp.int32)[None]
    own, column, core = lax.optimization_barrier((own, column, core))
    wide = 2 * feature

    rim, pack, own_in, src_in, dst_in, w1_in, w2_in, gain_in, assign_in, export_in = run(
        start_kernel,
        [((rim_count, feature), BF), ((rim_count + CNODE + 32, feature), BF)],
        [own, export, cot, assign],
        late=(0, 1, 2, 3),
        inner=(0, 1),
        ahead=[own, src, dst, fine_w1, fine_w2, fine_gain, assign, export],
    )
    from_a = send(rim, "core", 1)
    from_b = lax.ppermute(rim, ROW, between)
    packs = [pack, send(pack, "x", 1), send(pack, "x", 3), send(pack[rim_count:], "x", 2)]
    part, csrc_in, cdst_in, cw1_in, cw2_in, cgain_in, cot_in = run(
        own_kernel,
        [((edges, hidden), F32)],
        [own_in, src_in, dst_in, live_blocks, w1_in],
        scalars=(3,),
        inner=(0,),
        ahead=[coarse_src, coarse_dst, coarse_w1, coarse_w2, coarse_gain, cot],
        limit=LIMITS[0],
    )
    slope, acc, summed, pooled, table = run(
        fine_forward_kernel,
        [
            ((edges, hidden), F32),
            ((nodes, hidden), BF),
            ((nodes, feature), F32),
            ((CNODE, feature), BF),
            ((nodes + 4 * rim_count, feature), BF),
        ],
        [
            part, own_in, from_a, from_b, packs[1], packs[2], src_in, dst_in, live_blocks, core,
            column, w1_in, w2_in, gain_in, assign_in,
        ],
        [((nodes, hidden), F32)],
        scalars=(8, 9, 10),
        inner=(0, 1, 2, 3, 4),
        limit=LIMITS[1],
    )
    half_rows = CNODE // 2
    left, right = send(pooled, "x", 1), send(pooled, "x", 3)
    across = [send(left[:half_rows], "x", 1), send(right[half_rows:], "x", 3)]

    grad_fine, coarse_pack = run(
        coarse_kernel,
        [((nodes, feature), F32), ((2, 384, 128), F32)],
        [
            pooled, left, right, *across, *packs, csrc_in, cdst_in, cw1_in, cw2_in, cgain_in,
            cot_in, assign_in, column,
        ],
        [
            ((CNODE, feature), BF),
            ((coarse_edges, hidden), F32),
            ((coarse_edges, CNODE), BF),
            ((CNODE, coarse_edges), BF),
            ((CNODE, hidden), F32),
            ((CNODE, hidden), F32),
            ((CNODE, hidden), F32),
        ],
        scalars=(16,),
        inner=(0, 1),
        limit=LIMITS[2],
    )

    local, give, keep, ghost_b, ghost_w, ghost_e = run(
        fine_backward_kernel,
        [
            ((nodes, feature), F32),
            ((1920 + 2 * rim_count, 128), BF),
            ((1920, 128), F32),
            ((rim_count, feature), BF),
            ((2 * rim_count, 128), BF),
            ((2 * rim_count, 128), BF),
        ],
        [
            grad_fine, summed, slope, acc, table, src_in, dst_in, live_blocks, core,
            w1_in, w2_in, gain_in, coarse_pack,
        ],
        [
            ((nodes + 4 * rim_count, hidden), F32),
            ((nodes, hidden), F32),
            ((4 * rim_count, feature), BF),
        ],
        scalars=(7, 8),
        inner=(0, 1, 2, 3, 4, 5),
        limit=LIMITS[3],
    )
    from_core = send(give, "core", 1)
    from_b = lax.ppermute(ghost_b, ROW, between)
    total, coarse_total, to_east, to_cross, to_west = run(
        split_kernel,
        [
            ((384, 128), F32),
            ((384, 128), F32),
            ((384 + 2 * rim_count, 128), BF),
            ((384, 128), BF),
            ((384 + 2 * rim_count, 128), BF),
        ],
        [keep, from_core, ghost_w, ghost_e, column],
        scalars=(4,),
        inner=(0, 1, 2, 3, 4),
    )
    from_west = send(to_east, "x", 1)
    from_cross = send(to_cross, "x", 2)
    from_east = send(to_west, "x", 3)
    total = (
        total
        + from_west[0:384].astype(F32)
        + from_cross.astype(F32)
        + from_east[0:384].astype(F32)
    )
    both = jnp.concatenate(
        [total.reshape(16, 24, 128), coarse_total.reshape(16, 24, 128)], axis=1
    ).astype(BF)
    both = lax.all_to_all(both, PLANE, 0, 0, tiled=True)
    both = jnp.sum(both.astype(F32), axis=0).astype(BF)
    copies = jnp.broadcast_to(both[None], (64,) + both.shape)
    mine = lax.all_to_all(copies, CHIPS, 0, 0, tiled=True)
    mine, local = lax.optimization_barrier((mine, local))
    other = send(mine, "core", 1)
    (grad_latent,) = run(
        return_kernel,
        [((nodes, feature), F32)],
        [local, from_core, from_b, from_west, from_east, export_in, column],
        scalars=(6,),
    )
    unpack = functools.partial(
        unpack_kernel,
        fine_scale=1.0 / math.sqrt(edges * rows * cols),
        coarse_scale=1.0 / math.sqrt(coarse_edges * rows),
    )
    weight_grads = run(
        unpack,
        [
            ((2 * feature, hidden), F32),
            ((hidden, feature), F32),
            ((2 * feature, hidden), F32),
            ((hidden, feature), F32),
        ],
        [mine, other, core],
        scalars=(2,),
    )
    return (grad_latent[None, None], *weight_grads)


def solution(mesh):
    shape = (4, 4, 2, 4)
    inner = Mesh(mesh.devices.reshape(shape), ("z", "y", "core", "x"))
    node_sharded = P(ROW, "x", None, None)
    index_sharded = P(ROW, "x", None)
    placed = (
        node_sharded,
        node_sharded,
        P(),
        P(),
        P(),
        P(),
        P(),
        P(),
        index_sharded,
        index_sharded,
        P(ROW, "x"),
        index_sharded,
        index_sharded,
        P(ROW, None),
        P(ROW, None),
    )
    return jax.shard_map(
        shards,
        mesh=inner,
        in_specs=placed,
        out_specs=(node_sharded, P(), P(), P(), P()),
        check_vma=False,
    )
```

profile of v0, /device:TPU:1, one launch (start us, length us, event | category | flops | bytes accessed | tf_op | source)
XLA Modules:
  0.0 119.3 jit_solution(4375469999429975944)
XLA Ops:
  0.6 1.9 %shard_map.182 = (bf16[128,256]{1,0:T(8,128)(2,1)S(1)}, bf16[672,256]{1,0:T(8,128)(2,1)S(1)}, bf16[512,256]{1,0:T(8,128)(2,1)S(1)}, s32[1,2048]{1,0:T(1,128)S(1)...) custom-call(bf16[512,256]{1,0:T(8,128)(2,1)} %bitcast.13, ...), custom_call_target="tpu_custom_call" | custom-call | bytes 2004992 | tf_op jit(solution)/shard_map/pallas_call | solution.py:383
  2.5 2.1 %collective-permute-start.2 = (bf16[672,256]{1,0:T(8,128)(2,1)S(1)}, bf16[672,256]{1,0:T(8,128)(2,1)S(1)}, u32[]{:S(2)}, u32[]{:S(2)}) collective-permute-start(bf16[672,256]{1,0:T(8,128)(2,1)S(1)} %get-tuple-element.56.g0), channel_id=1, source_target_pairs={{0,1},{1,2},{2,3},{3,0},{4,5},{5,6},{6,7},{7,4},{8,9},{9,10},{10,1... | collective-permute-start | bytes 1032200 | tf_op jit(solution)/shard_map/ppermute | solution.py:403
  4.6 1.4 %collective-permute-start.3 = (bf16[672,256]{1,0:T(8,128)(2,1)S(1)}, bf16[672,256]{1,0:T(8,128)(2,1)S(1)}, u32[]{:S(2)}, u32[]{:S(2)}) collective-permute-start(bf16[672,256]{1,0:T(8,128)(2,1)S(1)} %get-tuple-element.56.g0), channel_id=1, source_target_pairs={{0,3},{1,0},{2,1},{3,2},{4,7},{5,4},{6,5},{7,6},{8,11},{9,8},{10,9... | collective-permute-start | bytes 1032200 | tf_op jit(solution)/shard_map/ppermute | solution.py:403
  6.0 1.3 %collective-permute-start = (bf16[128,256]{1,0:T(8,128)(2,1)S(1)}, bf16[128,256]{1,0:T(8,128)(2,1)S(1)}, u32[]{:S(2)}, u32[]{:S(2)}) collective-permute-start(bf16[128,256]{1,0:T(8,128)(2,1)S(1)} %get-tuple-element.55), channel_id=1, source_target_pairs={{0,4},{4,0},{1,5},{5,1},{2,6},{6,2},{3,7},{7,3},{8,12},{12,8},{9,1... | collective-permute-start | bytes 196616 | tf_op jit(solution)/shard_map/ppermute | solution.py:403
  7.2 3.2 %collective-permute-start.1 = (bf16[128,256]{1,0:T(8,128)(2,1)S(1)}, bf16[128,256]{1,0:T(8,128)(2,1)S(1)}, u32[]{:S(2)}, u32[]{:S(2)}) collective-permute-start(bf16[128,256]{1,0:T(8,128)(2,1)S(1)} %get-tuple-element.55), channel_id=1, source_target_pairs={{4,8},{12,16},{20,24},{28,32},{36,40},{44,48},{52,56},{60,64},{68,... | collective-permute-start | bytes 196616 | tf_op jit(solution)/shard_map/ppermute | solution.py:438
  11.1 3.2 %shard_map.183 = (f32[2048,512]{1,0:T(8,128)S(1)}, s32[1,3072]{1,0:T(1,128)S(1)}, s32[1,3072]{1,0:T(1,128)S(1)}, bf16[512,512]{1,0:T(8,128)(2,1)S(1)}, bf16[512,...) custom-call(bf16[512,256]{1,0:T(8,128)(2,1)S(1)} %get-tuple-element.50.refs_0_.own_ref, ...), custom_call_target="tpu_custom_call" | custom-call | bytes 6071300 | tf_op jit(solution)/shard_map/pallas_call | solution.py:383
  14.3 0.0 collective-permute-done.ra
  14.3 0.0 collective-permute-done.1.rb
  14.3 0.0 collective-permute-done.2.rw.g1
  14.3 0.0 collective-permute-done.3.re.g2
  14.3 4.6 %shard_map.184 = (f32[2048,512]{1,0:T(8,128)S(1)}, bf16[512,512]{1,0:T(8,128)(2,1)S(1)}, f32[512,256]{1,0:T(8,128)S(1)}, bf16[512,256]{1,0:T(8,128)(2,1)S(1)}, bf16[1024,256]{1,0:T(8,128)(2,1)S(1)}) custom-call(f32[2048,512]{1,0:T(8,128)S(1)} %get-tuple-element.54.part_ref, bf16[512,256]{1,0:T(8,128)(2,1)S(1)} %get-tuple-element.50.refs_0_.own_ref, ...), custom_call_target="tpu_custom_call" | custom-call | bytes 12110860 | tf_op jit(solution)/shard_map/pallas_call | solution.py:383
  18.9 0.2 collective-permute-start.4
  19.1 2.6 %collective-permute-start.5 = (bf16[512,256]{1,0:T(8,128)(2,1)S(1)}, bf16[512,256]{1,0:T(8,128)(2,1)S(1)}, u32[]{:S(2)}, u32[]{:S(2)}) collective-permute-start(bf16[512,256]{1,0:T(8,128)(2,1)S(1)} %get-tuple-element.62.p0), channel_id=1, source_target_pairs={{0,3},{1,0},{2,1},{3,2},{4,7},{5,4},{6,5},{7,6},{8,11},{9,8},{10,9... | collective-permute-start | bytes 786440 | tf_op jit(solution)/shard_map/ppermute | solution.py:403
  21.7 0.4 collective-permute-start.8
  22.1 6.5 %collective-permute-done.4.p1 = bf16[512,256]{1,0:T(8,128)(2,1)S(1)} collective-permute-done((bf16[512,256]{1,0:T(8,128)(2,1)S(1)}, bf16[512,256]{1,0:T(8,128)(2,1)S(1)}, u32[]{:S(2)}, u32[]{:S(2)}) %collective-permute-start.4) | collective-permute-done | bytes 262176 | tf_op jit(solution)/shard_map/ppermute | solution.py:403
  28.6 0.1 collective-permute-start.6
  28.7 0.0 collective-permute-done.5.p2
  28.7 3.7 %collective-permute-start.7 = (bf16[256,256]{1,0:T(8,128)(2,1)S(1)}, bf16[256,256]{1,0:T(8,128)(2,1)S(1)}, u32[]{:S(2)}, u32[]{:S(2)}) collective-permute-start(bf16[256,256]{1,0:T(8,128)(2,1)S(1)} %slice.21), channel_id=1, source_target_pairs={{0,3},{1,0},{2,1},{3,2},{4,7},{5,4},{6,5},{7,6},{8,11},{9,8},{10,9... | collective-permute-start | bytes 393224 | tf_op jit(solution)/shard_map/ppermute | solution.py:403
  32.4 0.0 collective-permute-done.8.g3
  32.4 3.9 %collective-permute-done.6.p3 = bf16[256,256]{1,0:T(8,128)(2,1)S(1)} collective-permute-done((bf16[256,256]{1,0:T(8,128)(2,1)S(1)}, bf16[256,256]{1,0:T(8,128)(2,1)S(1)}, u32[]{:S(2)}, u32[]{:S(2)}) %collective-permute-start.6) | collective-permute-done | bytes 131104 | tf_op jit(solution)/shard_map/ppermute | solution.py:403
  36.3 0.0 collective-permute-done.7.p4
  36.3 13.5 %shard_map.185 = (f32[512,256]{1,0:T(8,128)S(1)}, f32[2,384,128]{2,1,0:T(8,128)S(1)}) custom-call(bf16[512,256]{1,0:T(8,128)(2,1)S(1)} %get-tuple-element.62.p0, bf16[512,256]{1,0:T(8,128)(2,1)S(1)} %collective-permute-done.4.p1, bf16[512,256]{1,0:T(8,128)(2,1)S(1)} %collective-permute-done.5.p2, bf16[256,256]{1,0:T(8,128)(2,1)S(1)} %collective-permute-done.6.p3, ...), custom_call_target="tpu_custom_call" | custom-call | bytes 4353028 | tf_op jit(solution)/shard_map/pallas_call | solution.py:383
  49.8 6.3 %shard_map.186 = (f32[512,256]{1,0:T(8,128)S(1)}, bf16[2176,128]{1,0:T(8,128)(2,1)S(1)}, f32[1920,128]{1,0:T(8,128)S(1)}, bf16[128,256]{1,0:T(8,128)(2,1)S(1)}, ...) custom-call(f32[512,256]{1,0:T(8,128)S(1)} %get-tuple-element.69.grad_fine_ref, ...), custom_call_target="tpu_custom_call" | custom-call | bytes 9749512 | tf_op jit(solution)/shard_map/pallas_call | solution.py:383
  56.1 4.6 %collective-permute-start.9 = (bf16[2176,128]{1,0:T(8,128)(2,1)S(1)}, bf16[2176,128]{1,0:T(8,128)(2,1)S(1)}, u32[]{:S(2)}, u32[]{:S(2)}) collective-permute-start(bf16[2176,128]{1,0:T(8,128)(2,1)S(1)} %get-tuple-element.76), channel_id=1, source_target_pairs={{0,4},{4,0},{1,5},{5,1},{2,6},{6,2},{3,7},{7,3},{8,12},{12,8},{9,1... | collective-permute-start | bytes 1671176 | tf_op jit(solution)/shard_map/ppermute | solution.py:403
  60.8 1.6 %collective-permute-done.9.got_ref.from_core = bf16[2176,128]{1,0:T(8,128)(2,1)S(1)} collective-permute-done((bf16[2176,128]{1,0:T(8,128)(2,1)S(1)}, bf16[2176,128]{1,0:T(8,128)(2,1)S(1)}, u32[]{:S(2)}, u32[]{:S(2)}) %collective-permute-start.9) | collective-permute-done | bytes 557088 | tf_op jit(solution)/shard_map/ppermute | solution.py:403
  62.4 0.1 shard_map.187
  62.5 0.1 collective-permute-start.10
  62.6 3.5 %collective-permute-start.12 = (bf16[640,128]{1,0:T(8,128)(2,1)S(1)}, bf16[640,128]{1,0:T(8,128)(2,1)S(1)}, u32[]{:S(2)}, u32[]{:S(2)}) collective-permute-start(bf16[640,128]{1,0:T(8,128)(2,1)S(1)} %get-tuple-element.82), channel_id=1, source_target_pairs={{0,3},{1,0},{2,1},{3,2},{4,7},{5,4},{6,5},{7,6},{8,11},{9,8},{10,9... | collective-permute-start | bytes 491528 | tf_op jit(solution)/shard_map/ppermute | solution.py:403
  66.0 1.1 collective-permute-start.11
  67.1 6.0 %collective-permute-done.11 = bf16[384,128]{1,0:T(8,128)(2,1)S(1)} collective-permute-done((bf16[384,128]{1,0:T(8,128)(2,1)S(1)}, bf16[384,128]{1,0:T(8,128)(2,1)S(1)}, u32[]{:S(2)}, u32[]{:S(2)}) %collective-permute-start.11) | collective-permute-done | bytes 98336 | tf_op jit(solution)/shard_map/ppermute | solution.py:403
  73.2 0.0 collective-permute-done.10.from_west
  73.2 0.0 collective-permute-done.12.from_east
  73.2 0.1 add_convert_fusion
  73.3 15.0 %all_to_all.10 = bf16[16,48,128]{2,1,0:T(8,128)(2,1)S(1)} all-to-all(bf16[16,48,128]{2,1,0:T(8,128)(2,1)S(1)} %pad_maximum_fusion), channel_id=1, replica_groups=mesh['z'=4,'y'=4,'core'=2,'x'=4] {'z','y'}, dimensions={0} | all-to-all | bytes 393216 | tf_op jit(solution)/shard_map/all_to_all | solution.py:542
  88.3 0.1 broadcast_in_dim.25
  88.4 18.6 %all_to_all.11.mine_ref = bf16[64,48,128]{2,1,0:T(8,128)(2,1)S(1)} all-to-all(bf16[64,48,128]{2,1,0:T(8,128)(2,1)S(1)} %broadcast_in_dim.25), channel_id=1, replica_groups=mesh['z'=4,'y'=4,'core'=2,'x'=4] {'z','y','x'}, dimensions={0} | all-to-all | bytes 1572864 | tf_op jit(solution)/shard_map/all_to_all | solution.py:545
  106.9 3.7 %collective-permute-start.14 = (bf16[64,48,128]{2,1,0:T(8,128)(2,1)S(1)}, bf16[64,48,128]{2,1,0:T(8,128)(2,1)S(1)}, u32[]{:S(2)}, u32[]{:S(2)}) collective-permute-start(bf16[64,48,128]{2,1,0:T(8,128)(2,1)S(1)} %all_to_all.11.mine_ref), channel_id=1, source_target_pairs={{0,4},{4,0},{1,5},{5,1},{2,6},{6,2},{3,7},{7,3},{8,12},{12,8},{9,1... | collective-permute-start | bytes 2359304 | tf_op jit(solution)/shard_map/ppermute | solution.py:403
  110.6 2.1 %collective-permute-start.13 = (bf16[128,256]{1,0:T(8,128)(2,1)S(1)}, bf16[128,256]{1,0:T(8,128)(2,1)S(1)}, u32[]{:S(2)}, u32[]{:S(2)}) collective-permute-start(bf16[128,256]{1,0:T(8,128)(2,1)S(1)} %get-tuple-element.86), channel_id=1, source_target_pairs={{4,8},{12,16},{20,24},{28,32},{36,40},{44,48},{52,56},{60,64},{68,... | collective-permute-start | bytes 196616 | tf_op jit(solution)/shard_map/ppermute | solution.py:516
  112.7 3.5 %collective-permute-done.13.from_b = bf16[128,256]{1,0:T(8,128)(2,1)S(1)} collective-permute-done((bf16[128,256]{1,0:T(8,128)(2,1)S(1)}, bf16[128,256]{1,0:T(8,128)(2,1)S(1)}, u32[]{:S(2)}, u32[]{:S(2)}) %collective-permute-start.13) | collective-permute-done | bytes 65568 | tf_op jit(solution)/shard_map/ppermute | solution.py:516
  116.2 1.1 shard_map.188
  117.3 0.0 collective-permute-done.14.other_ref
  117.3 2.0 %shard_map.189 = (f32[512,512]{1,0:T(8,128)}, f32[512,256]{1,0:T(8,128)}, f32[512,512]{1,0:T(8,128)}, f32[512,256]{1,0:T(8,128)}) custom-call(bf16[64,48,128]{2,1,0:T(8,128)(2,1)S(1)} %all_to_all.11.mine_ref, bf16[64,48,128]{2,1,0:T(8,128)(2,1)S(1)} %collective-permute-done.14.other_ref, s32[1]{0:T(128)} %bitcast.2.core_ref), custom_call_target="tpu_custom_call" | custom-call | bytes 4718596 | tf_op jit(solution)/shard_map/pallas_call | solution.py:383
  (6 shorter events, 0.1 us)
Async XLA Ops:
  2.5 11.8 %collective-permute-start.2 = (bf16[672,256]{1,0:T(8,128)(2,1)S(1)}, bf16[672,256]{1,0:T(8,128)(2,1)S(1)}, u32[]{:S(2)}, u32[]{:S(2)}) collective-permute-start(bf16[672,256]{1,0:T(8,128)(2,1)S(1)} %get-tuple-element.56.g0), channel_id=1, source_target_pairs={{0,1},{1,2},{2,3},{3,0},{4,5},{5,6},{6,7},{7,4},{8,9},{9,10},{10,1... | collective-permute-start | bytes 1032200 | tf_op jit(solution)/shard_map/ppermute | solution.py:403
  4.6 9.7 %collective-permute-start.3 = (bf16[672,256]{1,0:T(8,128)(2,1)S(1)}, bf16[672,256]{1,0:T(8,128)(2,1)S(1)}, u32[]{:S(2)}, u32[]{:S(2)}) collective-permute-start(bf16[672,256]{1,0:T(8,128)(2,1)S(1)} %get-tuple-element.56.g0), channel_id=1, source_target_pairs={{0,3},{1,0},{2,1},{3,2},{4,7},{5,4},{6,5},{7,6},{8,11},{9,8},{10,9... | collective-permute-start | bytes 1032200 | tf_op jit(solution)/shard_map/ppermute | solution.py:403
  6.0 8.3 %collective-permute-start = (bf16[128,256]{1,0:T(8,128)(2,1)S(1)}, bf16[128,256]{1,0:T(8,128)(2,1)S(1)}, u32[]{:S(2)}, u32[]{:S(2)}) collective-permute-start(bf16[128,256]{1,0:T(8,128)(2,1)S(1)} %get-tuple-element.55), channel_id=1, source_target_pairs={{0,4},{4,0},{1,5},{5,1},{2,6},{6,2},{3,7},{7,3},{8,12},{12,8},{9,1... | collective-permute-start | bytes 196616 | tf_op jit(solution)/shard_map/ppermute | solution.py:403
  7.2 7.1 %collective-permute-start.1 = (bf16[128,256]{1,0:T(8,128)(2,1)S(1)}, bf16[128,256]{1,0:T(8,128)(2,1)S(1)}, u32[]{:S(2)}, u32[]{:S(2)}) collective-permute-start(bf16[128,256]{1,0:T(8,128)(2,1)S(1)} %get-tuple-element.55), channel_id=1, source_target_pairs={{4,8},{12,16},{20,24},{28,32},{36,40},{44,48},{52,56},{60,64},{68,... | collective-permute-start | bytes 196616 | tf_op jit(solution)/shard_map/ppermute | solution.py:438
  18.9 9.6 %collective-permute-start.4 = (bf16[512,256]{1,0:T(8,128)(2,1)S(1)}, bf16[512,256]{1,0:T(8,128)(2,1)S(1)}, u32[]{:S(2)}, u32[]{:S(2)}) collective-permute-start(bf16[512,256]{1,0:T(8,128)(2,1)S(1)} %get-tuple-element.62.p0), channel_id=1, source_target_pairs={{0,1},{1,2},{2,3},{3,0},{4,5},{5,6},{6,7},{7,4},{8,9},{9,10},{10,1... | collective-permute-start | bytes 786440 | tf_op jit(solution)/shard_map/ppermute | solution.py:403
  19.1 9.6 %collective-permute-start.5 = (bf16[512,256]{1,0:T(8,128)(2,1)S(1)}, bf16[512,256]{1,0:T(8,128)(2,1)S(1)}, u32[]{:S(2)}, u32[]{:S(2)}) collective-permute-start(bf16[512,256]{1,0:T(8,128)(2,1)S(1)} %get-tuple-element.62.p0), channel_id=1, source_target_pairs={{0,3},{1,0},{2,1},{3,2},{4,7},{5,4},{6,5},{7,6},{8,11},{9,8},{10,9... | collective-permute-start | bytes 786440 | tf_op jit(solution)/shard_map/ppermute | solution.py:403
  21.7 10.7 %collective-permute-start.8 = (bf16[544,256]{1,0:T(8,128)(2,1)S(1)}, bf16[544,256]{1,0:T(8,128)(2,1)S(1)}, u32[]{:S(2)}, u32[]{:S(2)}) collective-permute-start(bf16[544,256]{1,0:T(8,128)(2,1)S(1)} %slice.17), channel_id=1, source_target_pairs={{0,2},{1,3},{2,0},{3,1},{4,6},{5,7},{6,4},{7,5},{8,10},{9,11},{10,... | collective-permute-start | bytes 835592 | tf_op jit(solution)/shard_map/ppermute | solution.py:403
  28.6 7.7 %collective-permute-start.6 = (bf16[256,256]{1,0:T(8,128)(2,1)S(1)}, bf16[256,256]{1,0:T(8,128)(2,1)S(1)}, u32[]{:S(2)}, u32[]{:S(2)}) collective-permute-start(bf16[256,256]{1,0:T(8,128)(2,1)S(1)} %slice.20), channel_id=1, source_target_pairs={{0,1},{1,2},{2,3},{3,0},{4,5},{5,6},{6,7},{7,4},{8,9},{9,10},{10,1... | collective-permute-start | bytes 393224 | tf_op jit(solution)/shard_map/ppermute | solution.py:403
  28.7 7.6 %collective-permute-start.7 = (bf16[256,256]{1,0:T(8,128)(2,1)S(1)}, bf16[256,256]{1,0:T(8,128)(2,1)S(1)}, u32[]{:S(2)}, u32[]{:S(2)}) collective-permute-start(bf16[256,256]{1,0:T(8,128)(2,1)S(1)} %slice.21), channel_id=1, source_target_pairs={{0,3},{1,0},{2,1},{3,2},{4,7},{5,4},{6,5},{7,6},{8,11},{9,8},{10,9... | collective-permute-start | bytes 393224 | tf_op jit(solution)/shard_map/ppermute | solution.py:403
  56.1 6.2 %collective-permute-start.9 = (bf16[2176,128]{1,0:T(8,128)(2,1)S(1)}, bf16[2176,128]{1,0:T(8,128)(2,1)S(1)}, u32[]{:S(2)}, u32[]{:S(2)}) collective-permute-start(bf16[2176,128]{1,0:T(8,128)(2,1)S(1)} %get-tuple-element.76), channel_id=1, source_target_pairs={{0,4},{4,0},{1,5},{5,1},{2,6},{6,2},{3,7},{7,3},{8,12},{12,8},{9,1... | collective-permute-start | bytes 1671176 | tf_op jit(solution)/shard_map/ppermute | solution.py:403
  62.5 10.7 %collective-permute-start.10 = (bf16[640,128]{1,0:T(8,128)(2,1)S(1)}, bf16[640,128]{1,0:T(8,128)(2,1)S(1)}, u32[]{:S(2)}, u32[]{:S(2)}) collective-permute-start(bf16[640,128]{1,0:T(8,128)(2,1)S(1)} %get-tuple-element.80), channel_id=1, source_target_pairs={{0,1},{1,2},{2,3},{3,0},{4,5},{5,6},{6,7},{7,4},{8,9},{9,10},{10,1... | collective-permute-start | bytes 491528 | tf_op jit(solution)/shard_map/ppermute | solution.py:403
  62.6 10.6 %collective-permute-start.12 = (bf16[640,128]{1,0:T(8,128)(2,1)S(1)}, bf16[640,128]{1,0:T(8,128)(2,1)S(1)}, u32[]{:S(2)}, u32[]{:S(2)}) collective-permute-start(bf16[640,128]{1,0:T(8,128)(2,1)S(1)} %get-tuple-element.82), channel_id=1, source_target_pairs={{0,3},{1,0},{2,1},{3,2},{4,7},{5,4},{6,5},{7,6},{8,11},{9,8},{10,9... | collective-permute-start | bytes 491528 | tf_op jit(solution)/shard_map/ppermute | solution.py:403
  66.0 7.2 %collective-permute-start.11 = (bf16[384,128]{1,0:T(8,128)(2,1)S(1)}, bf16[384,128]{1,0:T(8,128)(2,1)S(1)}, u32[]{:S(2)}, u32[]{:S(2)}) collective-permute-start(bf16[384,128]{1,0:T(8,128)(2,1)S(1)} %get-tuple-element.81), channel_id=1, source_target_pairs={{0,2},{1,3},{2,0},{3,1},{4,6},{5,7},{6,4},{7,5},{8,10},{9,11},{10,... | collective-permute-start | bytes 294920 | tf_op jit(solution)/shard_map/ppermute | solution.py:403
  106.9 10.4 %collective-permute-start.14 = (bf16[64,48,128]{2,1,0:T(8,128)(2,1)S(1)}, bf16[64,48,128]{2,1,0:T(8,128)(2,1)S(1)}, u32[]{:S(2)}, u32[]{:S(2)}) collective-permute-start(bf16[64,48,128]{2,1,0:T(8,128)(2,1)S(1)} %all_to_all.11.mine_ref), channel_id=1, source_target_pairs={{0,4},{4,0},{1,5},{5,1},{2,6},{6,2},{3,7},{7,3},{8,12},{12,8},{9,1... | collective-permute-start | bytes 2359304 | tf_op jit(solution)/shard_map/ppermute | solution.py:403
  110.6 5.6 %collective-permute-start.13 = (bf16[128,256]{1,0:T(8,128)(2,1)S(1)}, bf16[128,256]{1,0:T(8,128)(2,1)S(1)}, u32[]{:S(2)}, u32[]{:S(2)}) collective-permute-start(bf16[128,256]{1,0:T(8,128)(2,1)S(1)} %get-tuple-element.86), channel_id=1, source_target_pairs={{4,8},{12,16},{20,24},{28,32},{36,40},{44,48},{52,56},{60,64},{68,... | collective-permute-start | bytes 196616 | tf_op jit(solution)/shard_map/ppermute | solution.py:516
where the time goes:
time: 120 us; the launch traced here: 119 us
  blocking collectives  33.5 us (28%)
  Pallas kernels  32.7 us (27%)
  starting transfers between devices  29.9 us (25%)
  waiting for transfers between devices  21.4 us (18%)
  between operations  1.44 us (1%)
    pallas_call x8, Pallas kernels, run(): pl.pallas_call(body if copies else kernel, out_shape=shapes, in_specs=[pl...  32.7 us
    ppermute x13, starting transfers between devices, send(): lax.ppermute(value, axis, [(i, (i + step) % size) for i in range(size)])  24.6 us
    all_to_all x1, blocking collectives, shards(): mine = lax.all_to_all(copies, CHIPS, 0, 0, tiled=True)  18.6 us
    ppermute x13, waiting for transfers between devices, send(): lax.ppermute(value, axis, [(i, (i + step) % size) for i in range(size)])  18 us
    all_to_all x1, blocking collectives, shards(): both = lax.all_to_all(both, PLANE, 0, 0, tiled=True)  15 us
    ppermute x1, waiting for transfers between devices, shards(): from_b = lax.ppermute(ghost_b, ROW, between)  3.47 us
    ppermute x1, starting transfers between devices, shards(): from_b = lax.ppermute(rim, ROW, between)  3.16 us
  transfers between devices with their start and end apart: 15, of which 5 were waited for; matrix products, arithmetic and copies ran while one was open for 0% of the time, Pallas kernels for 4%

commit v1 on v0

--- a/solution.py
+++ b/solution.py
@@ -58,12 +58,6 @@
     return jnp.where(hit, 1.0, 0.0).astype(BF)
 
 
-def receivers_of(dst_ref, live_ref, at):
-    row = dst_ref[:, at : at + CHUNK]
-    slot = lax.broadcasted_iota(jnp.int32, row.shape, 1) + at
-    return jnp.where(slot < 128 * live_ref[0, 0], row, -1)
-
-
 def norm_of(summed):
     inverse = lax.rsqrt(jnp.mean(summed * summed, axis=-1, keepdims=True) + EPS)
     return inverse, summed * inverse
@@ -81,7 +75,9 @@
     return (preact * sig).astype(BF), sig * (1.0 + preact * (1.0 - sig))
 
 
-def start_kernel(own_ref, export_ref, cot_ref, assign_ref, rim_ref, pack_ref):
+def start_kernel(
+    own_ref, export_ref, cot_ref, assign_ref, dst_ref, place_ref, rim_ref, pack_ref, target_ref
+):
     rim_count = export_ref.shape[1]
     rim = dot(pick_matrix(export_ref[...], own_ref.shape[0]), own_ref[...]).astype(BF)
     rim_ref[...] = rim
@@ -95,25 +91,26 @@
     at = rim_count + CNODE
     pack_ref[at : at + 16, :] = packed[:, :256]
     pack_ref[at + 16 : at + 32, :] = packed[:, 256:]
-
-
-def own_kernel(own_ref, src_ref, dst_ref, live_ref, w1_ref, part_ref):
+    slot = lax.broadcasted_iota(jnp.int32, dst_ref.shape, 1)
+    target_ref[...] = jnp.where(slot < place_ref[2], dst_ref[...], -1)
+
+
+def own_kernel(own_ref, src_ref, target_ref, w1_ref, part_ref):
     nodes, feature = own_ref.shape
     for at in range(0, src_ref.shape[1], CHUNK):
         here = slice(at, at + CHUNK)
         left = dot(pick_matrix(src_ref[:, here], nodes), own_ref[...]).astype(BF)
-        target = receivers_of(dst_ref, live_ref, at)
-        right = dot(pick_matrix(target, nodes), own_ref[...]).astype(BF)
+        right = dot(pick_matrix(target_ref[:, here], nodes), own_ref[...]).astype(BF)
         part_ref[here, :] = dot(left, w1_ref[0:feature, :]) + dot(right, w1_ref[feature:, :])
 
 
 def fine_forward_kernel(
-    part_ref, own_ref, ra, rb, rw, re, src_ref, dst_ref, live_ref, core_ref, col_ref,
+    part_ref, own_ref, ra, rb, rw, re, src_ref, target_ref, place_ref,
     w1_ref, w2_ref, gain_ref, assign_ref, slope_ref, acc_out, summed_ref, pooled_ref, table, acc,
 ):
     nodes, feature = own_ref.shape
     rim = ra.shape[0]
-    core, col = core_ref[0], col_ref[0]
+    col, core = place_ref[0], place_ref[1]
     table[0:nodes, :] = own_ref[...]
     table[pl.ds(pl.multiple_of(nodes + rim * (1 - core), rim), rim), :] = ra[...]
     table[pl.ds(pl.multiple_of(nodes + rim * core, rim), rim), :] = rb[...]
@@ -128,7 +125,7 @@
         preact = part_ref[here, :] + dot(left, w1_ref[0:feature, :])
         hidden, slope = activations(preact)
         slope_ref[here, :] = slope
-        part = dot(sum_matrix(receivers_of(dst_ref, live_ref, at), nodes), hidden)
+        part = dot(sum_matrix(target_ref[:, here], nodes), hidden)
         if at == 0:
             acc[...] = part
         else:
@@ -146,7 +143,7 @@
 
 def coarse_kernel(
     p0, p1, p2, p3, p4, g0, g1, g2, g3, src_ref, dst_ref, w1_ref, w2_ref, gain_ref, cot_ref,
-    assign_ref, col_ref, grad_fine_ref, pack_ref,
+    assign_ref, place_ref, grad_fine_ref, pack_ref,
     table, slope, pick_t, sum_t, acc, by_src, by_dst,
 ):
     feature = p0.shape[1]
@@ -204,7 +201,7 @@
     high, low = halves(grad_c0 * weight)
     spread = pick_matrix(assign_ref[...], CNODE)
     grad_fine_ref[...] = cot_ref[...].astype(F32) + dot(spread, high) + dot(spread, low)
-    own = pl.ds(pl.multiple_of(col_ref[0] * 128, 128), 128)
+    own = pl.ds(pl.multiple_of(place_ref[0] * 128, 128), 128)
     for half, rows in enumerate((by_src, by_dst)):
         pack_ref[half, 0:256, :] = dot_lt(table[...], rows[:, own].astype(BF))
     second = dot_lt(acc[:, own].astype(BF), grad_summed)
@@ -216,18 +213,18 @@
 
 
 def fine_backward_kernel(
-    grad_fine_ref, summed_ref, slope_ref, acc_ref, table_ref, src_ref, dst_ref,
-    live_ref, core_ref, w1_ref, w2_ref, gain_ref, coarse_ref,
+    grad_fine_ref, summed_ref, slope_ref, acc_ref, table_ref, src_ref, target_ref,
+    place_ref, w1_ref, w2_ref, gain_ref, coarse_ref,
     local_ref, give_ref, keep_ref, ghost_b, ghost_w, ghost_e, by_src, by_dst, ghost,
 ):
     nodes, feature = grad_fine_ref.shape
     rim = ghost_b.shape[0]
-    core = core_ref[0]
+    core = place_ref[1]
     grad_fine = grad_fine_ref[...]
     grad_summed = summed_grad(grad_fine, gain_ref[...], summed_ref[...])
     for at in range(0, src_ref.shape[1], CHUNK):
         here = slice(at, at + CHUNK)
-        target = receivers_of(dst_ref, live_ref, at)
+        target = target_ref[:, here]
         grad_message = dot(pick_matrix(target, nodes), grad_summed).astype(BF)
         grad_preact = (dot_rt(grad_message, w2_ref[...]) * slope_ref[here, :]).astype(BF)
         part_src = dot(sum_matrix(src_ref[:, here], table_ref.shape[0]), grad_preact)
@@ -265,8 +262,8 @@
         out[1536:1920, :] = coarse_ref[half].astype(out.dtype)
 
 
-def split_kernel(keep_ref, got_ref, ghost_w, ghost_e, col_ref, total_ref, coarse_ref, *sends):
-    col = col_ref[0]
+def split_kernel(keep_ref, got_ref, ghost_w, ghost_e, place_ref, total_ref, coarse_ref, *sends):
+    col = place_ref[0]
 
     def block(step):
         rows = pl.ds(pl.multiple_of(lax.rem(col + step, 4) * 384, 384), 384)
@@ -280,10 +277,10 @@
     sends[2][384:, :] = ghost_w[...]
 
 
-def return_kernel(local_ref, from_core, from_b, from_west, from_east, export_ref, col_ref, out_ref):
+def return_kernel(local_ref, from_core, from_b, from_west, from_east, export_ref, place_ref, out_ref):
     rim = export_ref.shape[1]
     adds = sum_matrix(export_ref[...], local_ref.shape[0])
-    col = col_ref[0]
+    col = place_ref[0]
 
     def wide(ref):
         at = ref.shape[0] - 2 * rim
@@ -298,10 +295,10 @@
 
 
 def unpack_kernel(
-    mine_ref, other_ref, core_ref, fine1_ref, fine2_ref, coarse1_ref, coarse2_ref,
+    mine_ref, other_ref, place_ref, fine1_ref, fine2_ref, coarse1_ref, coarse2_ref,
     *, fine_scale, coarse_scale,
 ):
-    for ref, half in ((mine_ref, core_ref[0]), (other_ref, 1 - core_ref[0])):
+    for ref, half in ((mine_ref, place_ref[1]), (other_ref, 1 - place_ref[1])):
         for plane in range(16):
             for x in range(4):
                 values = ref[plane * 4 + x].astype(F32)
@@ -421,18 +418,22 @@
     coarse_gain = coarse_gain[None, :]
     between = [(i, i + 1) for i in range(1, rows - 1, 2)]
     between = between + [(target, source) for source, target in between]
-    column = lax.axis_index("x").astype(jnp.int32)[None]
-    core = lax.axis_index("core").astype(jnp.int32)[None]
-    own, column, core = lax.optimization_barrier((own, column, core))
+    place = jnp.stack([lax.axis_index("x"), lax.axis_index("core"), 128 * live_blocks[0, 0]])
+    own, place = lax.optimization_barrier((own, place.astype(jnp.int32)))
     wide = 2 * feature
 
-    rim, pack, own_in, src_in, dst_in, w1_in, w2_in, gain_in, assign_in, export_in = run(
+    rim, pack, target, own_in, src_in, w1_in, w2_in, gain_in, assign_in, export_in = run(
         start_kernel,
-        [((rim_count, feature), BF), ((rim_count + CNODE + 32, feature), BF)],
-        [own, export, cot, assign],
-        late=(0, 1, 2, 3),
-        inner=(0, 1),
-        ahead=[own, src, dst, fine_w1, fine_w2, fine_gain, assign, export],
+        [
+            ((rim_count, feature), BF),
+            ((rim_count + CNODE + 32, feature), BF),
+            ((1, edges), jnp.int32),
+        ],
+        [own, export, cot, assign, dst, place],
+        scalars=(5,),
+        late=(0, 1, 2, 3, 4),
+        inner=(0, 1, 2),
+        ahead=[own, src, fine_w1, fine_w2, fine_gain, assign, export],
     )
     from_a = send(rim, "core", 1)
     from_b = lax.ppermute(rim, ROW, between)
@@ -440,8 +441,7 @@
     part, csrc_in, cdst_in, cw1_in, cw2_in, cgain_in, cot_in = run(
         own_kernel,
         [((edges, hidden), F32)],
-        [own_in, src_in, dst_in, live_blocks, w1_in],
-        scalars=(3,),
+        [own_in, src_in, target, w1_in],
         inner=(0,),
         ahead=[coarse_src, coarse_dst, coarse_w1, coarse_w2, coarse_gain, cot],
         limit=LIMITS[0],
@@ -456,15 +456,16 @@
             ((nodes + 4 * rim_count, feature), BF),
         ],
         [
-            part, own_in, from_a, from_b, packs[1], packs[2], src_in, dst_in, live_blocks, core,
-            column, w1_in, w2_in, gain_in, assign_in,
+            part, own_in, from_a, from_b, packs[1], packs[2], src_in, target, place,
+            w1_in, w2_in, gain_in, assign_in,
         ],
         [((nodes, hidden), F32)],
-        scalars=(8, 9, 10),
+        scalars=(8,),
         inner=(0, 1, 2, 3, 4),
         limit=LIMITS[1],
     )
     half_rows = CNODE // 2
+    pooled, packs[3] = lax.optimization_barrier((pooled, packs[3]))
     left, right = send(pooled, "x", 1), send(pooled, "x", 3)
     across = [send(left[:half_rows], "x", 1), send(right[half_rows:], "x", 3)]
 
@@ -473,7 +474,7 @@
         [((nodes, feature), F32), ((2, 384, 128), F32)],
         [
             pooled, left, right, *across, *packs, csrc_in, cdst_in, cw1_in, cw2_in, cgain_in,
-            cot_in, assign_in, column,
+            cot_in, assign_in, place,
         ],
         [
             ((CNODE, feature), BF),
@@ -500,7 +501,7 @@
             ((2 * rim_count, 128), BF),
         ],
         [
-            grad_fine, summed, slope, acc, table, src_in, dst_in, live_blocks, core,
+            grad_fine, summed, slope, acc, table, src_in, target, place,
             w1_in, w2_in, gain_in, coarse_pack,
         ],
         [
@@ -508,7 +509,7 @@
             ((nodes, hidden), F32),
             ((4 * rim_count, feature), BF),
         ],
-        scalars=(7, 8),
+        scalars=(7,),
         inner=(0, 1, 2, 3, 4, 5),
         limit=LIMITS[3],
     )
@@ -523,7 +524,7 @@
             ((384, 128), BF),
             ((384 + 2 * rim_count, 128), BF),
         ],
-        [keep, from_core, ghost_w, ghost_e, column],
+        [keep, from_core, ghost_w, ghost_e, place],
         scalars=(4,),
         inner=(0, 1, 2, 3, 4),
     )
@@ -539,6 +540,7 @@
     both = jnp.concatenate(
         [total.reshape(16, 24, 128), coarse_total.reshape(16, 24, 128)], axis=1
     ).astype(BF)
+    both, from_b = lax.optimization_barrier((both, from_b))
     both = lax.all_to_all(both, PLANE, 0, 0, tiled=True)
     both = jnp.sum(both.astype(F32), axis=0).astype(BF)
     copies = jnp.broadcast_to(both[None], (64,) + both.shape)
@@ -548,7 +550,7 @@
     (grad_latent,) = run(
         return_kernel,
         [((nodes, feature), F32)],
-        [local, from_core, from_b, from_west, from_east, export_in, column],
+        [local, from_core, from_b, from_west, from_east, export_in, place],
         scalars=(6,),
     )
     unpack = functools.partial(
@@ -564,7 +566,7 @@
             ((2 * feature, hidden), F32),
             ((hidden, feature), F32),
         ],
-        [mine, other, core],
+        [mine, other, place],
         scalars=(2,),
     )
     return (grad_latent[None, None], *weight_grads)

time: 120 us -> 119 us (level)
  waiting for transfers between devices: 21.4 us -> 11.8 us
  starting transfers between devices: 29.9 us -> 35 us
  Pallas kernels: 32.7 us -> 35.9 us
    ppermute x13, waiting for transfers between devices: 18 us -> 11.5 us  [send(): lax.ppermute(value, axis, [(i, (i + step) % size) for i in range(size)])]
    ppermute x1, waiting for transfers between devices: 3.47 us -> 0.21 us  [shards(): from_b = lax.ppermute(ghost_b, ROW, between)]
    ppermute x13, starting transfers between devices: 24.6 us -> 27.8 us  [send(): lax.ppermute(value, axis, [(i, (i + step) % size) for i in range(size)])]
    pallas_call x8, Pallas kernels: 32.7 us -> 35.9 us  [run(): pl.pallas_call(body if copies else kernel, out_shape=shapes, in_specs=[pl...]
    ppermute x1, starting transfers between devices: 2.1 us -> 4.13 us  [shards(): from_b = lax.ppermute(ghost_b, ROW, between)]
  transfers between devices with their start and end apart: 15 -> 15, of which waited for: 5 -> 8; matrix products, arithmetic and copies ran while one was open for 0% -> 0% of each run, Pallas kernels for 4% -> 8%
where the time goes in v1:
time: 119 us; the launch traced here: 118 us
  Pallas kernels  35.9 us (30%)
  starting transfers between devices  35 us (29%)
  blocking collectives  34 us (29%)
  waiting for transfers between devices  11.8 us (10%)
  between operations  1.4 us (1%)
    pallas_call x8, Pallas kernels, run(): pl.pallas_call(body if copies else kernel, out_shape=shapes, in_specs=[pl...  35.9 us
    ppermute x13, starting transfers between devices, send(): lax.ppermute(value, axis, [(i, (i + step) % size) for i in range(size)])  27.8 us
    all_to_all x1, blocking collectives, shards(): mine = lax.all_to_all(copies, CHIPS, 0, 0, tiled=True)  18.8 us
    all_to_all x1, blocking collectives, shards(): both = lax.all_to_all(both, PLANE, 0, 0, tiled=True)  15.2 us
    ppermute x13, waiting for transfers between devices, send(): lax.ppermute(value, axis, [(i, (i + step) % size) for i in range(size)])  11.5 us
    ppermute x1, starting transfers between devices, shards(): from_b = lax.ppermute(ghost_b, ROW, between)  4.13 us
    ppermute x1, starting transfers between devices, shards(): from_b = lax.ppermute(rim, ROW, between)  3.08 us
  transfers between devices with their start and end apart: 15, of which 8 were waited for; matrix products, arithmetic and copies ran while one was open for 0% of the time, Pallas kernels for 8%

profile of v1, /device:TPU:1, one launch (start us, length us, event | category | flops | bytes accessed | tf_op | source)
XLA Modules:
  0.0 118.5 jit_solution(5150889083411052715)
XLA Ops:
  1.3 0.1 pad_add_fusion.refs_5_.place_ref
  1.4 2.4 %shard_map.182 = (bf16[128,256]{1,0:T(8,128)(2,1)S(1)}, bf16[672,256]{1,0:T(8,128)(2,1)S(1)}, s32[1,2048]{1,0:T(1,128)S(1)}, bf16[512,256]{1,0:T(8,128)(2,1)S(1)...) custom-call(bf16[512,256]{1,0:T(8,128)(2,1)} %bitcast.16, ...), custom_call_target="tpu_custom_call" | custom-call | bytes 2013196 | tf_op jit(solution)/shard_map/pallas_call | solution.py:380
  3.8 2.1 %collective-permute-start.2 = (bf16[672,256]{1,0:T(8,128)(2,1)S(1)}, bf16[672,256]{1,0:T(8,128)(2,1)S(1)}, u32[]{:S(2)}, u32[]{:S(2)}) collective-permute-start(bf16[672,256]{1,0:T(8,128)(2,1)S(1)} %get-tuple-element.60.g0), channel_id=1, source_target_pairs={{0,1},{1,2},{2,3},{3,0},{4,5},{5,6},{6,7},{7,4},{8,9},{9,10},{10,1... | collective-permute-start | bytes 1032200 | tf_op jit(solution)/shard_map/ppermute | solution.py:400
  5.9 1.4 %collective-permute-start.3 = (bf16[672,256]{1,0:T(8,128)(2,1)S(1)}, bf16[672,256]{1,0:T(8,128)(2,1)S(1)}, u32[]{:S(2)}, u32[]{:S(2)}) collective-permute-start(bf16[672,256]{1,0:T(8,128)(2,1)S(1)} %get-tuple-element.60.g0), channel_id=1, source_target_pairs={{0,3},{1,0},{2,1},{3,2},{4,7},{5,4},{6,5},{7,6},{8,11},{9,8},{10,9... | collective-permute-start | bytes 1032200 | tf_op jit(solution)/shard_map/ppermute | solution.py:400
  7.3 1.7 %collective-permute-start.4 = (bf16[544,256]{1,0:T(8,128)(2,1)S(1)}, bf16[544,256]{1,0:T(8,128)(2,1)S(1)}, u32[]{:S(2)}, u32[]{:S(2)}) collective-permute-start(bf16[544,256]{1,0:T(8,128)(2,1)S(1)} %slice.15), channel_id=1, source_target_pairs={{0,2},{1,3},{2,0},{3,1},{4,6},{5,7},{6,4},{7,5},{8,10},{9,11},{10,... | collective-permute-start | bytes 835592 | tf_op jit(solution)/shard_map/ppermute | solution.py:400
  9.0 1.5 %collective-permute-start = (bf16[128,256]{1,0:T(8,128)(2,1)S(1)}, bf16[128,256]{1,0:T(8,128)(2,1)S(1)}, u32[]{:S(2)}, u32[]{:S(2)}) collective-permute-start(bf16[128,256]{1,0:T(8,128)(2,1)S(1)} %get-tuple-element.59), channel_id=1, source_target_pairs={{0,4},{4,0},{1,5},{5,1},{2,6},{6,2},{3,7},{7,3},{8,12},{12,8},{9,1... | collective-permute-start | bytes 196616 | tf_op jit(solution)/shard_map/ppermute | solution.py:400
  10.5 3.1 %collective-permute-start.1 = (bf16[128,256]{1,0:T(8,128)(2,1)S(1)}, bf16[128,256]{1,0:T(8,128)(2,1)S(1)}, u32[]{:S(2)}, u32[]{:S(2)}) collective-permute-start(bf16[128,256]{1,0:T(8,128)(2,1)S(1)} %get-tuple-element.59), channel_id=1, source_target_pairs={{4,8},{12,16},{20,24},{28,32},{36,40},{44,48},{52,56},{60,64},{68,... | collective-permute-start | bytes 196616 | tf_op jit(solution)/shard_map/ppermute | solution.py:439
  13.6 2.6 %shard_map.183 = (f32[2048,512]{1,0:T(8,128)S(1)}, s32[1,3072]{1,0:T(1,128)S(1)}, s32[1,3072]{1,0:T(1,128)S(1)}, bf16[512,512]{1,0:T(8,128)(2,1)S(1)}, bf16[512,...) custom-call(bf16[512,256]{1,0:T(8,128)(2,1)S(1)} %get-tuple-element.54.refs_0_.own_ref, ...), custom_call_target="tpu_custom_call" | custom-call | bytes 6071296 | tf_op jit(solution)/shard_map/pallas_call | solution.py:380
  16.3 0.0 collective-permute-done.ra
  16.3 0.1 collective-permute-done.1.rb
  16.4 0.0 collective-permute-done.2.rw.g1
  16.4 0.0 collective-permute-done.3.re.g2
  16.4 5.1 %shard_map.184 = (f32[2048,512]{1,0:T(8,128)S(1)}, bf16[512,512]{1,0:T(8,128)(2,1)S(1)}, f32[512,256]{1,0:T(8,128)S(1)}, bf16[512,256]{1,0:T(8,128)(2,1)S(1)}, bf16[1024,256]{1,0:T(8,128)(2,1)S(1)}) custom-call(f32[2048,512]{1,0:T(8,128)S(1)} %get-tuple-element.58.part_ref, bf16[512,256]{1,0:T(8,128)(2,1)S(1)} %get-tuple-element.54.refs_0_.own_ref, ...), custom_call_target="tpu_custom_call" | custom-call | bytes 12110860 | tf_op jit(solution)/shard_map/pallas_call | solution.py:380
  21.5 0.2 collective-permute-done.4.g3
  21.8 0.5 collective-permute-start.5
  22.3 2.1 %collective-permute-start.6 = (bf16[512,256]{1,0:T(8,128)(2,1)S(1)}, bf16[512,256]{1,0:T(8,128)(2,1)S(1)}, u32[]{:S(2)}, u32[]{:S(2)}) collective-permute-start(bf16[512,256]{1,0:T(8,128)(2,1)S(1)} %get-tuple-element.65.p0), channel_id=1, source_target_pairs={{0,3},{1,0},{2,1},{3,2},{4,7},{5,4},{6,5},{7,6},{8,11},{9,8},{10,9... | collective-permute-start | bytes 786440 | tf_op jit(solution)/shard_map/ppermute | solution.py:400
  24.5 3.8 %collective-permute-done.5.p1 = bf16[512,256]{1,0:T(8,128)(2,1)S(1)} collective-permute-done((bf16[512,256]{1,0:T(8,128)(2,1)S(1)}, bf16[512,256]{1,0:T(8,128)(2,1)S(1)}, u32[]{:S(2)}, u32[]{:S(2)}) %collective-permute-start.5) | collective-permute-done | bytes 262176 | tf_op jit(solution)/shard_map/ppermute | solution.py:400
  28.2 0.1 collective-permute-start.7
  28.3 0.0 collective-permute-done.6.p2
  28.4 2.9 %collective-permute-start.8 = (bf16[256,256]{1,0:T(8,128)(2,1)S(1)}, bf16[256,256]{1,0:T(8,128)(2,1)S(1)}, u32[]{:S(2)}, u32[]{:S(2)}) collective-permute-start(bf16[256,256]{1,0:T(8,128)(2,1)S(1)} %slice.21), channel_id=1, source_target_pairs={{0,3},{1,0},{2,1},{3,2},{4,7},{5,4},{6,5},{7,6},{8,11},{9,8},{10,9... | collective-permute-start | bytes 393224 | tf_op jit(solution)/shard_map/ppermute | solution.py:400
  31.2 3.7 %collective-permute-done.7.p3 = bf16[256,256]{1,0:T(8,128)(2,1)S(1)} collective-permute-done((bf16[256,256]{1,0:T(8,128)(2,1)S(1)}, bf16[256,256]{1,0:T(8,128)(2,1)S(1)}, u32[]{:S(2)}, u32[]{:S(2)}) %collective-permute-start.7) | collective-permute-done | bytes 131104 | tf_op jit(solution)/shard_map/ppermute | solution.py:400
  35.0 0.0 collective-permute-done.8.p4
  35.0 14.0 %shard_map.185 = (f32[512,256]{1,0:T(8,128)S(1)}, f32[2,384,128]{2,1,0:T(8,128)S(1)}) custom-call(bf16[512,256]{1,0:T(8,128)(2,1)S(1)} %get-tuple-element.65.p0, bf16[512,256]{1,0:T(8,128)(2,1)S(1)} %collective-permute-done.5.p1, bf16[512,256]{1,0:T(8,128)(2,1)S(1)} %collective-permute-done.6.p2, bf16[256,256]{1,0:T(8,128)(2,1)S(1)} %collective-permute-done.7.p3, ...), custom_call_target="tpu_custom_call" | custom-call | bytes 4353036 | tf_op jit(solution)/shard_map/pallas_call | solution.py:380
  49.0 6.9 %shard_map.186 = (f32[512,256]{1,0:T(8,128)S(1)}, bf16[2176,128]{1,0:T(8,128)(2,1)S(1)}, f32[1920,128]{1,0:T(8,128)S(1)}, bf16[128,256]{1,0:T(8,128)(2,1)S(1)}, ...) custom-call(f32[512,256]{1,0:T(8,128)S(1)} %get-tuple-element.73.grad_fine_ref, ...), custom_call_target="tpu_custom_call" | custom-call | bytes 9749516 | tf_op jit(solution)/shard_map/pallas_call | solution.py:380
  55.9 7.6 %collective-permute-start.9 = (bf16[2176,128]{1,0:T(8,128)(2,1)S(1)}, bf16[2176,128]{1,0:T(8,128)(2,1)S(1)}, u32[]{:S(2)}, u32[]{:S(2)}) collective-permute-start(bf16[2176,128]{1,0:T(8,128)(2,1)S(1)} %get-tuple-element.80), channel_id=1, source_target_pairs={{0,4},{4,0},{1,5},{5,1},{2,6},{6,2},{3,7},{7,3},{8,12},{12,8},{9,1... | collective-permute-start | bytes 1671176 | tf_op jit(solution)/shard_map/ppermute | solution.py:400
  63.4 1.6 %collective-permute-done.9.got_ref.from_core = bf16[2176,128]{1,0:T(8,128)(2,1)S(1)} collective-permute-done((bf16[2176,128]{1,0:T(8,128)(2,1)S(1)}, bf16[2176,128]{1,0:T(8,128)(2,1)S(1)}, u32[]{:S(2)}, u32[]{:S(2)}) %collective-permute-start.9) | collective-permute-done | bytes 557088 | tf_op jit(solution)/shard_map/ppermute | solution.py:400
  65.0 0.7 shard_map.187
  65.7 0.1 collective-permute-start.10
  65.8 3.3 %collective-permute-start.12 = (bf16[640,128]{1,0:T(8,128)(2,1)S(1)}, bf16[640,128]{1,0:T(8,128)(2,1)S(1)}, u32[]{:S(2)}, u32[]{:S(2)}) collective-permute-start(bf16[640,128]{1,0:T(8,128)(2,1)S(1)} %get-tuple-element.86), channel_id=1, source_target_pairs={{0,3},{1,0},{2,1},{3,2},{4,7},{5,4},{6,5},{7,6},{8,11},{9,8},{10,9... | collective-permute-start | bytes 491528 | tf_op jit(solution)/shard_map/ppermute | solution.py:400
  69.1 1.1 collective-permute-start.11
  70.2 4.1 %collective-permute-start.13 = (bf16[128,256]{1,0:T(8,128)(2,1)S(1)}, bf16[128,256]{1,0:T(8,128)(2,1)S(1)}, u32[]{:S(2)}, u32[]{:S(2)}) collective-permute-start(bf16[128,256]{1,0:T(8,128)(2,1)S(1)} %get-tuple-element.88), channel_id=1, source_target_pairs={{4,8},{12,16},{20,24},{28,32},{36,40},{44,48},{52,56},{60,64},{68,... | collective-permute-start | bytes 196616 | tf_op jit(solution)/shard_map/ppermute | solution.py:517
  74.3 1.9 %collective-permute-done.11 = bf16[384,128]{1,0:T(8,128)(2,1)S(1)} collective-permute-done((bf16[384,128]{1,0:T(8,128)(2,1)S(1)}, bf16[384,128]{1,0:T(8,128)(2,1)S(1)}, u32[]{:S(2)}, u32[]{:S(2)}) %collective-permute-start.11) | collective-permute-done | bytes 98336 | tf_op jit(solution)/shard_map/ppermute | solution.py:400
  76.2 0.0 collective-permute-done.10.from_west
  76.2 0.0 collective-permute-done.12.from_east
  76.2 0.1 add_convert_fusion
  76.3 0.2 collective-permute-done.13.from_b
  76.5 15.2 %all_to_all.10 = bf16[16,48,128]{2,1,0:T(8,128)(2,1)S(1)} all-to-all(bf16[16,48,128]{2,1,0:T(8,128)(2,1)S(1)} %pad_maximum_fusion), channel_id=1, replica_groups=mesh['z'=4,'y'=4,'core'=2,'x'=4] {'z','y'}, dimensions={0} | all-to-all | bytes 393216 | tf_op jit(solution)/shard_map/all_to_all | solution.py:544
  91.7 0.1 broadcast_in_dim.17
  91.8 18.8 %all_to_all.11.mine_ref = bf16[64,48,128]{2,1,0:T(8,128)(2,1)S(1)} all-to-all(bf16[64,48,128]{2,1,0:T(8,128)(2,1)S(1)} %broadcast_in_dim.17), channel_id=1, replica_groups=mesh['z'=4,'y'=4,'core'=2,'x'=4] {'z','y','x'}, dimensions={0} | all-to-all | bytes 1572864 | tf_op jit(solution)/shard_map/all_to_all | solution.py:547
  110.6 3.4 %collective-permute-start.14 = (bf16[64,48,128]{2,1,0:T(8,128)(2,1)S(1)}, bf16[64,48,128]{2,1,0:T(8,128)(2,1)S(1)}, u32[]{:S(2)}, u32[]{:S(2)}) collective-permute-start(bf16[64,48,128]{2,1,0:T(8,128)(2,1)S(1)} %all_to_all.11.mine_ref), channel_id=1, source_target_pairs={{0,4},{4,0},{1,5},{5,1},{2,6},{6,2},{3,7},{7,3},{8,12},{12,8},{9,1... | collective-permute-start | bytes 2359304 | tf_op jit(solution)/shard_map/ppermute | solution.py:400
  114.0 1.7 %shard_map.188 = f32[512,256]{1,0:T(8,128)} custom-call(f32[512,256]{1,0:T(8,128)S(1)} %get-tuple-element.91.local_ref, bf16[2176,128]{1,0:T(8,128)(2,1)S(1)} %collective-permute-done.9.got_ref.from_core, bf16[128,256]{1,0:T(8,128)(2,1)S(1)} %collective-permute-done.13.from_b, bf16[640,128]{1,0:T(8,128)(2,1)S(1)} %collective-permute-done.10.from_west, ...), custom_call_target="tpu_custom_call" | custom-call | bytes 1999372 | tf_op jit(solution)/shard_map/pallas_call | solution.py:380
  115.7 0.3 collective-permute-done.14.other_ref
  115.9 2.5 %shard_map.189 = (f32[512,512]{1,0:T(8,128)}, f32[512,256]{1,0:T(8,128)}, f32[512,512]{1,0:T(8,128)}, f32[512,256]{1,0:T(8,128)}) custom-call(bf16[64,48,128]{2,1,0:T(8,128)(2,1)S(1)} %all_to_all.11.mine_ref, bf16[64,48,128]{2,1,0:T(8,128)(2,1)S(1)} %collective-permute-done.14.other_ref, s32[3]{0:T(128)S(1)} %pad_add_fusion.refs_5_.place_ref), custom_call_target="tpu_custom_call" | custom-call | bytes 4718604 | tf_op jit(solution)/shard_map/pallas_call | solution.py:380
  (6 shorter events, 0.1 us)
Async XLA Ops:
  3.8 12.6 %collective-permute-start.2 = (bf16[672,256]{1,0:T(8,128)(2,1)S(1)}, bf16[672,256]{1,0:T(8,128)(2,1)S(1)}, u32[]{:S(2)}, u32[]{:S(2)}) collective-permute-start(bf16[672,256]{1,0:T(8,128)(2,1)S(1)} %get-tuple-element.60.g0), channel_id=1, source_target_pairs={{0,1},{1,2},{2,3},{3,0},{4,5},{5,6},{6,7},{7,4},{8,9},{9,10},{10,1... | collective-permute-start | bytes 1032200 | tf_op jit(solution)/shard_map/ppermute | solution.py:400
  5.9 10.5 %collective-permute-start.3 = (bf16[672,256]{1,0:T(8,128)(2,1)S(1)}, bf16[672,256]{1,0:T(8,128)(2,1)S(1)}, u32[]{:S(2)}, u32[]{:S(2)}) collective-permute-start(bf16[672,256]{1,0:T(8,128)(2,1)S(1)} %get-tuple-element.60.g0), channel_id=1, source_target_pairs={{0,3},{1,0},{2,1},{3,2},{4,7},{5,4},{6,5},{7,6},{8,11},{9,8},{10,9... | collective-permute-start | bytes 1032200 | tf_op jit(solution)/shard_map/ppermute | solution.py:400
  7.3 14.5 %collective-permute-start.4 = (bf16[544,256]{1,0:T(8,128)(2,1)S(1)}, bf16[544,256]{1,0:T(8,128)(2,1)S(1)}, u32[]{:S(2)}, u32[]{:S(2)}) collective-permute-start(bf16[544,256]{1,0:T(8,128)(2,1)S(1)} %slice.15), channel_id=1, source_target_pairs={{0,2},{1,3},{2,0},{3,1},{4,6},{5,7},{6,4},{7,5},{8,10},{9,11},{10,... | collective-permute-start | bytes 835592 | tf_op jit(solution)/shard_map/ppermute | solution.py:400
  9.0 7.3 %collective-permute-start = (bf16[128,256]{1,0:T(8,128)(2,1)S(1)}, bf16[128,256]{1,0:T(8,128)(2,1)S(1)}, u32[]{:S(2)}, u32[]{:S(2)}) collective-permute-start(bf16[128,256]{1,0:T(8,128)(2,1)S(1)} %get-tuple-element.59), channel_id=1, source_target_pairs={{0,4},{4,0},{1,5},{5,1},{2,6},{6,2},{3,7},{7,3},{8,12},{12,8},{9,1... | collective-permute-start | bytes 196616 | tf_op jit(solution)/shard_map/ppermute | solution.py:400
  10.5 5.9 %collective-permute-start.1 = (bf16[128,256]{1,0:T(8,128)(2,1)S(1)}, bf16[128,256]{1,0:T(8,128)(2,1)S(1)}, u32[]{:S(2)}, u32[]{:S(2)}) collective-permute-start(bf16[128,256]{1,0:T(8,128)(2,1)S(1)} %get-tuple-element.59), channel_id=1, source_target_pairs={{4,8},{12,16},{20,24},{28,32},{36,40},{44,48},{52,56},{60,64},{68,... | collective-permute-start | bytes 196616 | tf_op jit(solution)/shard_map/ppermute | solution.py:439
  21.8 6.4 %collective-permute-start.5 = (bf16[512,256]{1,0:T(8,128)(2,1)S(1)}, bf16[512,256]{1,0:T(8,128)(2,1)S(1)}, u32[]{:S(2)}, u32[]{:S(2)}) collective-permute-start(bf16[512,256]{1,0:T(8,128)(2,1)S(1)} %get-tuple-element.65.p0), channel_id=1, source_target_pairs={{0,1},{1,2},{2,3},{3,0},{4,5},{5,6},{6,7},{7,4},{8,9},{9,10},{10,1... | collective-permute-start | bytes 786440 | tf_op jit(solution)/shard_map/ppermute | solution.py:400
  22.3 6.0 %collective-permute-start.6 = (bf16[512,256]{1,0:T(8,128)(2,1)S(1)}, bf16[512,256]{1,0:T(8,128)(2,1)S(1)}, u32[]{:S(2)}, u32[]{:S(2)}) collective-permute-start(bf16[512,256]{1,0:T(8,128)(2,1)S(1)} %get-tuple-element.65.p0), channel_id=1, source_target_pairs={{0,3},{1,0},{2,1},{3,2},{4,7},{5,4},{6,5},{7,6},{8,11},{9,8},{10,9... | collective-permute-start | bytes 786440 | tf_op jit(solution)/shard_map/ppermute | solution.py:400
  28.2 6.7 %collective-permute-start.7 = (bf16[256,256]{1,0:T(8,128)(2,1)S(1)}, bf16[256,256]{1,0:T(8,128)(2,1)S(1)}, u32[]{:S(2)}, u32[]{:S(2)}) collective-permute-start(bf16[256,256]{1,0:T(8,128)(2,1)S(1)} %slice.20), channel_id=1, source_target_pairs={{0,1},{1,2},{2,3},{3,0},{4,5},{5,6},{6,7},{7,4},{8,9},{9,10},{10,1... | collective-permute-start | bytes 393224 | tf_op jit(solution)/shard_map/ppermute | solution.py:400
  28.4 6.6 %collective-permute-start.8 = (bf16[256,256]{1,0:T(8,128)(2,1)S(1)}, bf16[256,256]{1,0:T(8,128)(2,1)S(1)}, u32[]{:S(2)}, u32[]{:S(2)}) collective-permute-start(bf16[256,256]{1,0:T(8,128)(2,1)S(1)} %slice.21), channel_id=1, source_target_pairs={{0,3},{1,0},{2,1},{3,2},{4,7},{5,4},{6,5},{7,6},{8,11},{9,8},{10,9... | collective-permute-start | bytes 393224 | tf_op jit(solution)/shard_map/ppermute | solution.py:400
  55.9 9.1 %collective-permute-start.9 = (bf16[2176,128]{1,0:T(8,128)(2,1)S(1)}, bf16[2176,128]{1,0:T(8,128)(2,1)S(1)}, u32[]{:S(2)}, u32[]{:S(2)}) collective-permute-start(bf16[2176,128]{1,0:T(8,128)(2,1)S(1)} %get-tuple-element.80), channel_id=1, source_target_pairs={{0,4},{4,0},{1,5},{5,1},{2,6},{6,2},{3,7},{7,3},{8,12},{12,8},{9,1... | collective-permute-start | bytes 1671176 | tf_op jit(solution)/shard_map/ppermute | solution.py:400
  65.7 10.5 %collective-permute-start.10 = (bf16[640,128]{1,0:T(8,128)(2,1)S(1)}, bf16[640,128]{1,0:T(8,128)(2,1)S(1)}, u32[]{:S(2)}, u32[]{:S(2)}) collective-permute-start(bf16[640,128]{1,0:T(8,128)(2,1)S(1)} %get-tuple-element.84), channel_id=1, source_target_pairs={{0,1},{1,2},{2,3},{3,0},{4,5},{5,6},{6,7},{7,4},{8,9},{9,10},{10,1... | collective-permute-start | bytes 491528 | tf_op jit(solution)/shard_map/ppermute | solution.py:400
  65.8 10.5 %collective-permute-start.12 = (bf16[640,128]{1,0:T(8,128)(2,1)S(1)}, bf16[640,128]{1,0:T(8,128)(2,1)S(1)}, u32[]{:S(2)}, u32[]{:S(2)}) collective-permute-start(bf16[640,128]{1,0:T(8,128)(2,1)S(1)} %get-tuple-element.86), channel_id=1, source_target_pairs={{0,3},{1,0},{2,1},{3,2},{4,7},{5,4},{6,5},{7,6},{8,11},{9,8},{10,9... | collective-permute-start | bytes 491528 | tf_op jit(solution)/shard_map/ppermute | solution.py:400
  69.1 7.2 %collective-permute-start.11 = (bf16[384,128]{1,0:T(8,128)(2,1)S(1)}, bf16[384,128]{1,0:T(8,128)(2,1)S(1)}, u32[]{:S(2)}, u32[]{:S(2)}) collective-permute-start(bf16[384,128]{1,0:T(8,128)(2,1)S(1)} %get-tuple-element.85), channel_id=1, source_target_pairs={{0,2},{1,3},{2,0},{3,1},{4,6},{5,7},{6,4},{7,5},{8,10},{9,11},{10,... | collective-permute-start | bytes 294920 | tf_op jit(solution)/shard_map/ppermute | solution.py:400
  70.2 6.4 %collective-permute-start.13 = (bf16[128,256]{1,0:T(8,128)(2,1)S(1)}, bf16[128,256]{1,0:T(8,128)(2,1)S(1)}, u32[]{:S(2)}, u32[]{:S(2)}) collective-permute-start(bf16[128,256]{1,0:T(8,128)(2,1)S(1)} %get-tuple-element.88), channel_id=1, source_target_pairs={{4,8},{12,16},{20,24},{28,32},{36,40},{44,48},{52,56},{60,64},{68,... | collective-permute-start | bytes 196616 | tf_op jit(solution)/shard_map/ppermute | solution.py:517
  110.6 5.3 %collective-permute-start.14 = (bf16[64,48,128]{2,1,0:T(8,128)(2,1)S(1)}, bf16[64,48,128]{2,1,0:T(8,128)(2,1)S(1)}, u32[]{:S(2)}, u32[]{:S(2)}) collective-permute-start(bf16[64,48,128]{2,1,0:T(8,128)(2,1)S(1)} %all_to_all.11.mine_ref), channel_id=1, source_target_pairs={{0,4},{4,0},{1,5},{5,1},{2,6},{6,2},{3,7},{7,3},{8,12},{12,8},{9,1... | collective-permute-start | bytes 2359304 | tf_op jit(solution)/shard_map/ppermute | solution.py:400

commit v2 on v1

--- a/solution.py
+++ b/solution.py
@@ -12,7 +12,7 @@
 EPS = 1e-05
 CNODE = 512
 CHUNK = 1024
-LIMITS = (20, 20, 36, 22)
+LIMITS = (16, 16, 18, 18, 18)
 BF = jnp.bfloat16
 F32 = jnp.float32
 
@@ -75,28 +75,25 @@
     return (preact * sig).astype(BF), sig * (1.0 + preact * (1.0 - sig))
 
 
-def start_kernel(
-    own_ref, export_ref, cot_ref, assign_ref, dst_ref, place_ref, rim_ref, pack_ref, target_ref
-):
-    rim_count = export_ref.shape[1]
-    rim = dot(pick_matrix(export_ref[...], own_ref.shape[0]), own_ref[...]).astype(BF)
-    rim_ref[...] = rim
-    pack_ref[0:rim_count, :] = rim
+def rim_kernel(own_ref, export_ref, rim_ref):
+    rim_ref[...] = dot(pick_matrix(export_ref[...], own_ref.shape[0]), own_ref[...]).astype(BF)
+
+
+def pool_kernel(cot_ref, assign_ref, pack_ref, count_ref):
     pool = sum_matrix(assign_ref[...], CNODE)
-    pack_ref[rim_count : rim_count + CNODE, :] = dot(pool, cot_ref[...]).astype(BF)
+    pack_ref[...] = dot(pool, cot_ref[...]).astype(BF)
     count = dot_rt(jnp.ones((16, pool.shape[1]), BF), pool)
     coarse_part = jnp.floor(count * (1.0 / 256.0)) * 256.0
     upper = lax.broadcasted_iota(jnp.int32, count.shape, 0) < 8
     packed = jnp.where(upper, coarse_part, count - coarse_part).astype(BF)
-    at = rim_count + CNODE
-    pack_ref[at : at + 16, :] = packed[:, :256]
-    pack_ref[at + 16 : at + 32, :] = packed[:, 256:]
+    count_ref[0:16, :] = packed[:, :256]
+    count_ref[16:32, :] = packed[:, 256:]
+
+
+def own_kernel(own_ref, src_ref, dst_ref, w1_ref, place_ref, target_ref, part_ref):
+    nodes, feature = own_ref.shape
     slot = lax.broadcasted_iota(jnp.int32, dst_ref.shape, 1)
     target_ref[...] = jnp.where(slot < place_ref[2], dst_ref[...], -1)
-
-
-def own_kernel(own_ref, src_ref, target_ref, w1_ref, part_ref):
-    nodes, feature = own_ref.shape
     for at in range(0, src_ref.shape[1], CHUNK):
         here = slice(at, at + CHUNK)
         left = dot(pick_matrix(src_ref[:, here], nodes), own_ref[...]).astype(BF)
@@ -106,18 +103,17 @@
 
 def fine_forward_kernel(
     part_ref, own_ref, ra, rb, rw, re, src_ref, target_ref, place_ref,
-    w1_ref, w2_ref, gain_ref, assign_ref, slope_ref, acc_out, summed_ref, pooled_ref, table, acc,
+    w1_ref, w2_ref, gain_ref, assign_ref, count_ref, slope_ref, acc_out, summed_ref, pooled_ref, table,
+    acc,
 ):
     nodes, feature = own_ref.shape
     rim = ra.shape[0]
-    col, core = place_ref[0], place_ref[1]
+    core = place_ref[1]
     table[0:nodes, :] = own_ref[...]
     table[pl.ds(pl.multiple_of(nodes + rim * (1 - core), rim), rim), :] = ra[...]
     table[pl.ds(pl.multiple_of(nodes + rim * core, rim), rim), :] = rb[...]
-    west = rw[0:rim, :].astype(F32) * jnp.where(col > 0, 1.0, 0.0)
-    east = re[0:rim, :].astype(F32) * jnp.where(col < 3, 1.0, 0.0)
-    table[nodes + 2 * rim : nodes + 3 * rim, :] = west.astype(BF)
-    table[nodes + 3 * rim :, :] = east.astype(BF)
+    table[nodes + 2 * rim : nodes + 3 * rim, :] = rw[...]
+    table[nodes + 3 * rim :, :] = re[...]
     for at in range(0, src_ref.shape[1], CHUNK):
         here = slice(at, at + CHUNK)
         picks = pick_matrix(src_ref[:, here] - nodes, 4 * rim)
@@ -138,30 +134,28 @@
     fine_new = own_ref[...].astype(F32) + normed * gain_ref[...]
     high, low = halves(fine_new)
     pool = sum_matrix(assign_ref[...], CNODE)
-    pooled_ref[...] = (dot(pool, high) + dot(pool, low)).astype(BF)
-
-
-def coarse_kernel(
-    p0, p1, p2, p3, p4, g0, g1, g2, g3, src_ref, dst_ref, w1_ref, w2_ref, gain_ref, cot_ref,
-    assign_ref, place_ref, grad_fine_ref, pack_ref,
-    table, slope, pick_t, sum_t, acc, by_src, by_dst,
+    pooled_ref[0:CNODE, :] = (dot(pool, high) + dot(pool, low)).astype(BF)
+    pooled_ref[CNODE:, :] = count_ref[...]
+
+
+def coarse_forward_kernel(
+    p0, p1, p2, p3, p4, src_ref, dst_ref, w1_ref, w2_ref,
+    table, weight_ref, slope, pick_t, sum_t, acc, summed_ref,
 ):
     feature = p0.shape[1]
     edges = src_ref.shape[1]
-    grads = []
     count = None
-    for ref in (g0, g1, g2, g3):
-        skip = ref.shape[0] - CNODE - 32
-        grads.append(ref[skip : skip + CNODE, :].astype(F32))
-        tail = ref[skip + CNODE :, :].astype(F32)
+    for ref in (p0, p1, p2, p4):
+        tail = ref[ref.shape[0] - 32 :, :].astype(F32)
         tail = [tail[at : at + 1, :] + tail[at + 8 : at + 9, :] for at in (0, 16)]
         tail = jnp.concatenate(tail, axis=1)
         count = tail if count is None else count + tail
-    grad_c1 = (grads[0] + grads[1]) + (grads[2] + grads[3])
     weight = spread_row(1.0 / jnp.maximum(count, 1.0))
     weight = jnp.concatenate([weight] * (feature // 128), axis=1)
-    across = jnp.concatenate([p3[...].astype(F32), p4[...].astype(F32)], axis=0)
-    pooled = (p0[...].astype(F32) + p1[...].astype(F32)) + (p2[...].astype(F32) + across)
+    weight_ref[...] = weight
+    across = jnp.concatenate([p3[...].astype(F32), p4[0 : CNODE // 2, :].astype(F32)], axis=0)
+    near = [ref[0:CNODE, :].astype(F32) for ref in (p0, p1, p2)]
+    pooled = (near[0] + near[1]) + (near[2] + across)
     table[...] = (pooled * weight).astype(BF)
     for at in range(0, edges, CHUNK):
         here = slice(at, at + CHUNK)
@@ -179,8 +173,20 @@
         else:
             acc[...] += part
     high, low = halves(acc[...])
-    summed = dot(high, w2_ref[...]) + dot(low, w2_ref[...])
-    grad_summed = summed_grad(grad_c1, gain_ref[...], summed)
+    summed_ref[...] = dot(high, w2_ref[...]) + dot(low, w2_ref[...])
+
+
+def coarse_backward_kernel(
+    g0, g1, g2, g3, table, weight_ref, slope, pick_t, sum_t, acc, summed_ref,
+    src_ref, w1_ref, w2_ref, gain_ref, cot_ref, assign_ref, place_ref, grad_fine_ref, pack_ref,
+    by_src, by_dst,
+):
+    feature = g0.shape[1]
+    edges = src_ref.shape[1]
+    weight = weight_ref[...]
+    grads = [ref[...].astype(F32) for ref in (g0, g1, g2, g3)]
+    grad_c1 = (grads[0] + grads[1]) + (grads[2] + grads[3])
+    grad_summed = summed_grad(grad_c1, gain_ref[...], summed_ref[...])
     for at in range(0, edges, CHUNK):
         here = slice(at, at + CHUNK)
         grad_message = dot(pick_t[here, :], grad_summed).astype(BF)
@@ -294,33 +300,68 @@
     out_ref[...] = local_ref[...] + dot(adds, high) + dot(adds, low)
 
 
-def unpack_kernel(
-    mine_ref, other_ref, place_ref, fine1_ref, fine2_ref, coarse1_ref, coarse2_ref,
-    *, fine_scale, coarse_scale,
-):
-    for ref, half in ((mine_ref, place_ref[1]), (other_ref, 1 - place_ref[1])):
+def unpack_kernel(ref, place_ref, *rest, other, fine_scale, coarse_scale):
+    outs, (fine1, fine2, coarse1, coarse2, sems) = rest[-9:-5], rest[-5:]
+    half = 1 - place_ref[1] if other else place_ref[1]
+    start = pl.multiple_of(half * 256, 256)
+    for x in range(4):
         for plane in range(16):
-            for x in range(4):
-                values = ref[plane * 4 + x].astype(F32)
-                for at in range(0, 24, 8):
-                    row = x * 384 + plane * 24 + at
-                    piece = values[at : at + 8, :] * fine_scale
-                    if row < 1024:
-                        lanes = pl.ds(pl.multiple_of(half * 256 + row // 512 * 128, 128), 128)
-                        fine1_ref[row % 512 : row % 512 + 8, lanes] = piece
-                    else:
-                        start = pl.multiple_of(half * 256 + row % 256, 8)
-                        lane = (row - 1024) // 256 * 128
-                        fine2_ref[pl.ds(start, 8), lane : lane + 128] = piece
-                    row = plane * 24 + at
-                    piece = values[24 + at : 32 + at, :] * coarse_scale
-                    if row < 256:
-                        start = pl.multiple_of(half * 256 + row, 8)
-                        coarse1_ref[pl.ds(start, 8), x * 128 : x * 128 + 128] = piece
-                    else:
-                        start = pl.multiple_of(half * 64 + x * 128 + row % 64, 8)
-                        lane = (row - 256) // 64 * 128
-                        coarse2_ref[pl.ds(start, 8), lane : lane + 128] = piece
+            values = ref[plane * 4 + x].astype(F32)
+            for at in range(0, 24, 8):
+                row = x * 384 + plane * 24 + at
+                piece = values[at : at + 8, :] * fine_scale
+                if row < 1024:
+                    lane = row // 512 * 128
+                    fine1[row % 512 : row % 512 + 8, lane : lane + 128] = piece
+                else:
+                    lane = (row - 1024) // 256 * 128
+                    fine2[row % 256 : row % 256 + 8, lane : lane + 128] = piece
+                row = plane * 24 + at
+                piece = values[24 + at : 32 + at, :] * coarse_scale
+                if row < 256:
+                    coarse1[row : row + 8, x * 128 : x * 128 + 128] = piece
+                else:
+                    lane = (row - 256) // 64 * 128
+                    row = row % 64
+                    coarse2[x, row : row + 8, lane : lane + 128] = piece
+    copies = [
+        pltpu.make_async_copy(fine1, outs[0].at[:, pl.ds(start, 256)], sems.at[0]),
+        pltpu.make_async_copy(fine2, outs[1].at[pl.ds(start, 256), :], sems.at[1]),
+        pltpu.make_async_copy(coarse1, outs[2].at[pl.ds(start, 256), :], sems.at[2]),
+    ]
+    for x in range(4):
+        rows = pl.ds(pl.multiple_of(x * 128 + half * 64, 64), 64)
+        copies.append(pltpu.make_async_copy(coarse2.at[x], outs[3].at[rows, :], sems.at[3 + x]))
+    for copy in copies:
+        copy.start()
+    for copy in copies:
+        copy.wait()
+
+
+def unpack(part, place, earlier, shapes, fine_scale, coarse_scale):
+    body = functools.partial(
+        unpack_kernel, other=bool(earlier), fine_scale=fine_scale, coarse_scale=coarse_scale
+    )
+    return pl.pallas_call(
+        body,
+        out_shape=[pltpu.HBM(shape, F32) for shape in shapes],
+        in_specs=[
+            pl.BlockSpec(memory_space=pltpu.VMEM),
+            pl.BlockSpec(memory_space=pltpu.SMEM),
+        ]
+        + [pl.BlockSpec(memory_space=pltpu.HBM)] * len(earlier),
+        out_specs=[pl.BlockSpec(memory_space=pltpu.HBM)] * len(shapes),
+        scratch_shapes=[
+            pltpu.VMEM((512, 256), F32),
+            pltpu.VMEM((256, 256), F32),
+            pltpu.VMEM((256, 512), F32),
+            pltpu.VMEM((4, 64, 256), F32),
+            pltpu.SemaphoreType.DMA((7,)),
+        ],
+        input_output_aliases={2 + i: i for i in range(len(earlier))},
+        compiler_params=pltpu.CompilerParams(vmem_limit_bytes=16 * 1024 * 1024),
+        cost_estimate=pl.CostEstimate(flops=0, bytes_accessed=3 * 2**20, transcendentals=0),
+    )(part, place, *earlier)
 
 
 class Late:
@@ -342,7 +383,7 @@
             self.copy = None
 
 
-def run(kernel, outs, operands, scratch=(), scalars=(), late=(), inner=(), ahead=(), limit=16):
+def run(kernel, outs, operands, scratch=(), scalars=(), late=(), inner=(), ahead=(), limit=16, work=0.1):
     size = sum(math.prod(x.shape) * x.dtype.itemsize for x in [*operands, *ahead]) + sum(
         math.prod(shape) * jnp.dtype(kind).itemsize for shape, kind in outs
     )
@@ -386,7 +427,9 @@
         + [pltpu.VMEM(operands[i].shape, operands[i].dtype) for i in late]
         + ([pltpu.SemaphoreType.DMA((copies,))] if copies else []),
         compiler_params=pltpu.CompilerParams(vmem_limit_bytes=limit * 1024 * 1024),
-        cost_estimate=pl.CostEstimate(flops=0, bytes_accessed=size, transcendentals=0),
+        cost_estimate=pl.CostEstimate(
+            flops=int(2e9 * work), bytes_accessed=size, transcendentals=0
+        ),
     )(*operands)
 
 
@@ -422,72 +465,95 @@
     own, place = lax.optimization_barrier((own, place.astype(jnp.int32)))
     wide = 2 * feature
 
-    rim, pack, target, own_in, src_in, w1_in, w2_in, gain_in, assign_in, export_in = run(
-        start_kernel,
-        [
-            ((rim_count, feature), BF),
-            ((rim_count + CNODE + 32, feature), BF),
-            ((1, edges), jnp.int32),
-        ],
-        [own, export, cot, assign, dst, place],
-        scalars=(5,),
-        late=(0, 1, 2, 3, 4),
-        inner=(0, 1, 2),
-        ahead=[own, src, fine_w1, fine_w2, fine_gain, assign, export],
-    )
+    east = [(i, i + 1) for i in range(cols - 1)]
+    west = [(i + 1, i) for i in range(cols - 1)]
+    rim, own_in, src_in, w1_in, export_in = run(
+        rim_kernel,
+        [((rim_count, feature), BF)],
+        [own, export],
+        late=(0, 1),
+        inner=(0,),
+        ahead=[own, src, fine_w1, export],
+    )
+    from_west = lax.ppermute(rim, "x", east)
+    from_east = lax.ppermute(rim, "x", west)
+    from_b = lax.ppermute(rim, ROW, between)
     from_a = send(rim, "core", 1)
-    from_b = lax.ppermute(rim, ROW, between)
-    packs = [pack, send(pack, "x", 1), send(pack, "x", 3), send(pack[rim_count:], "x", 2)]
-    part, csrc_in, cdst_in, cw1_in, cw2_in, cgain_in, cot_in = run(
+    target, part, csrc_in, cdst_in, cw1_in, cw2_in, cgain_in, cot_in = run(
         own_kernel,
-        [((edges, hidden), F32)],
-        [own_in, src_in, target, w1_in],
-        inner=(0,),
+        [((1, edges), jnp.int32), ((edges, hidden), F32)],
+        [own_in, src_in, dst, w1_in, place],
+        scalars=(4,),
+        late=(2,),
+        inner=(0, 1),
         ahead=[coarse_src, coarse_dst, coarse_w1, coarse_w2, coarse_gain, cot],
         limit=LIMITS[0],
-    )
+        work=1.1,
+    )
+    cot_in, part = lax.optimization_barrier((cot_in, part))
+    pack, count, w2_in, gain_in, assign_in = run(
+        pool_kernel,
+        [((CNODE, feature), BF), ((32, feature), BF)],
+        [cot_in, assign],
+        late=(1,),
+        inner=(0, 1),
+        ahead=[fine_w2, fine_gain, assign],
+    )
+    packs = [pack, send(pack, "x", 1), send(pack, "x", 3)]
     slope, acc, summed, pooled, table = run(
         fine_forward_kernel,
         [
             ((edges, hidden), F32),
             ((nodes, hidden), BF),
             ((nodes, feature), F32),
-            ((CNODE, feature), BF),
+            ((CNODE + 32, feature), BF),
             ((nodes + 4 * rim_count, feature), BF),
         ],
         [
-            part, own_in, from_a, from_b, packs[1], packs[2], src_in, target, place,
-            w1_in, w2_in, gain_in, assign_in,
+            part, own_in, from_a, from_b, from_west, from_east, src_in, target, place,
+            w1_in, w2_in, gain_in, assign_in, count,
         ],
         [((nodes, hidden), F32)],
         scalars=(8,),
         inner=(0, 1, 2, 3, 4),
         limit=LIMITS[1],
+        work=1.6,
     )
     half_rows = CNODE // 2
-    pooled, packs[3] = lax.optimization_barrier((pooled, packs[3]))
+    pooled, packs = lax.optimization_barrier((pooled, packs))
     left, right = send(pooled, "x", 1), send(pooled, "x", 3)
     across = [send(left[:half_rows], "x", 1), send(right[half_rows:], "x", 3)]
-
-    grad_fine, coarse_pack = run(
-        coarse_kernel,
-        [((nodes, feature), F32), ((2, 384, 128), F32)],
-        [
-            pooled, left, right, *across, *packs, csrc_in, cdst_in, cw1_in, cw2_in, cgain_in,
-            cot_in, assign_in, place,
-        ],
+    pack, left, right, across = lax.optimization_barrier((packs[0], left, right, across))
+    packs.append(send(pack, "x", 2))
+
+    ctable, weight, cslope, pick, adds, cacc, csummed = run(
+        coarse_forward_kernel,
         [
             ((CNODE, feature), BF),
+            ((CNODE, feature), F32),
             ((coarse_edges, hidden), F32),
             ((coarse_edges, CNODE), BF),
             ((CNODE, coarse_edges), BF),
             ((CNODE, hidden), F32),
-            ((CNODE, hidden), F32),
-            ((CNODE, hidden), F32),
-        ],
-        scalars=(16,),
+            ((CNODE, feature), F32),
+        ],
+        [pooled, left, right, *across, csrc_in, cdst_in, cw1_in, cw2_in],
+        inner=(0, 1, 2, 3, 4, 5, 6),
+        limit=LIMITS[2],
+        work=2.6,
+    )
+    grad_fine, coarse_pack = run(
+        coarse_backward_kernel,
+        [((nodes, feature), F32), ((2, 384, 128), F32)],
+        [
+            *packs, ctable, weight, cslope, pick, adds, cacc, csummed,
+            csrc_in, cw1_in, cw2_in, cgain_in, cot_in, assign_in, place,
+        ],
+        [((CNODE, hidden), F32), ((CNODE, hidden), F32)],
+        scalars=(17,),
         inner=(0, 1),
-        limit=LIMITS[2],
+        limit=LIMITS[3],
+        work=2.8,
     )
 
     local, give, keep, ghost_b, ghost_w, ghost_e = run(
@@ -511,7 +577,8 @@
         ],
         scalars=(7,),
         inner=(0, 1, 2, 3, 4, 5),
-        limit=LIMITS[3],
+        limit=LIMITS[4],
+        work=2.8,
     )
     from_core = send(give, "core", 1)
     from_b = lax.ppermute(ghost_b, ROW, between)
@@ -553,23 +620,11 @@
         [local, from_core, from_b, from_west, from_east, export_in, place],
         scalars=(6,),
     )
-    unpack = functools.partial(
-        unpack_kernel,
-        fine_scale=1.0 / math.sqrt(edges * rows * cols),
-        coarse_scale=1.0 / math.sqrt(coarse_edges * rows),
-    )
-    weight_grads = run(
-        unpack,
-        [
-            ((2 * feature, hidden), F32),
-            ((hidden, feature), F32),
-            ((2 * feature, hidden), F32),
-            ((hidden, feature), F32),
-        ],
-        [mine, other, place],
-        scalars=(2,),
-    )
-    return (grad_latent[None, None], *weight_grads)
+    shapes = [(wide, hidden), (hidden, feature), (wide, hidden), (hidden, feature)]
+    scales = (1.0 / math.sqrt(edges * rows * cols), 1.0 / math.sqrt(coarse_edges * rows))
+    grads = unpack(mine, place, [], shapes, *scales)
+    grads = unpack(other, place, list(grads), shapes, *scales)
+    return (grad_latent[None, None], *grads)
 
 
 def solution(mesh):

time: 119 us -> 125 us (1.050)
  waiting for transfers between devices: 11.8 us -> 17.2 us
  Pallas kernels: 35.9 us -> 39 us
  starting transfers between devices: 35 us -> 32.1 us
    ppermute x13, starting transfers between devices: 27.8 us -> 18.9 us  [send(): lax.ppermute(value, axis, [(i, (i + step) % size) for i in range(size)])]
    ppermute x0 -> x2, starting transfers between devices: none -> 4.41 us  [the longest x1 3.12 us: shards(): from_west = lax.ppermute(rim, 'x', east)]
    ppermute x13, waiting for transfers between devices: 11.5 us -> 15.4 us  [send(): lax.ppermute(value, axis, [(i, (i + step) % size) for i in range(size)])]
    pallas_call x0 -> x2, Pallas kernels: none -> 3.52 us  [unpack(): pl.pallas_call(body, out_shape=[pltpu.HBM(shape, F32) for shape in shapes...]
    ppermute x1, waiting for transfers between devices: 0.21 us -> 1.79 us  [shards(): from_b = lax.ppermute(ghost_b, ROW, between)]
    ppermute x1, starting transfers between devices: 4.13 us -> 5.58 us  [shards(): from_b = lax.ppermute(ghost_b, ROW, between)]
    pallas_call x8 -> x9, Pallas kernels: 35.9 us -> 35.4 us  [run(): pl.pallas_call(body if copies else kernel, out_shape=shapes, in_specs=[pl...]
  transfers between devices with their start and end apart: 15 -> 17, of which waited for: 8 -> 7; matrix products, arithmetic and copies ran while one was open for 0% -> 0% of each run, Pallas kernels for 8% -> 17%
where the time goes in v2:
time: 125 us; the launch traced here: 124 us
  Pallas kernels  39 us (31%)
  blocking collectives  34.1 us (27%)
  starting transfers between devices  32.1 us (26%)
  waiting for transfers between devices  17.2 us (14%)
  between operations  1.64 us (1%)
    pallas_call x9, Pallas kernels, run(): pl.pallas_call(body if copies else kernel, out_shape=shapes, in_specs=[pl...  35.4 us
    all_to_all x1, blocking collectives, shards(): mine = lax.all_to_all(copies, CHIPS, 0, 0, tiled=True)  18.9 us
    ppermute x13, starting transfers between devices, send(): lax.ppermute(value, axis, [(i, (i + step) % size) for i in range(size)])  18.9 us
    ppermute x13, waiting for transfers between devices, send(): lax.ppermute(value, axis, [(i, (i + step) % size) for i in range(size)])  15.4 us
    all_to_all x1, blocking collectives, shards(): both = lax.all_to_all(both, PLANE, 0, 0, tiled=True)  15.2 us
    ppermute x1, starting transfers between devices, shards(): from_b = lax.ppermute(ghost_b, ROW, between)  5.58 us
    pallas_call x2, Pallas kernels, unpack(): pl.pallas_call(body, out_shape=[pltpu.HBM(shape, F32) for shape in shapes...  3.52 us
    ppermute x1, starting transfers between devices, shards(): from_b = lax.ppermute(rim, ROW, between)  3.19 us
  transfers between devices with their start and end apart: 17, of which 7 were waited for; matrix products, arithmetic and copies ran while one was open for 0% of the time, Pallas kernels for 17%

profile of v2, /device:TPU:1, one launch (start us, length us, event | category | flops | bytes accessed | tf_op | source)
XLA Modules:
  0.0 124.4 jit_solution(15449386497429991876)
XLA Ops:
  1.3 0.1 pad_add_fusion.refs_4_.place_ref
  1.4 1.3 %shard_map.182 = (bf16[128,256]{1,0:T(8,128)(2,1)S(1)}, bf16[512,256]{1,0:T(8,128)(2,1)S(1)}, s32[1,2048]{1,0:T(1,128)S(1)}, bf16[512,512]{1,0:T(8,128)(2,1)S(1)}, s32[1,128]{1,0:T(1,128)S(1)}) custom-call(bf16[512,256]{1,0:T(8,128)(2,1)} %bitcast.14, s32[1,128]{1,0:T(1,128)} %bitcast.20, bf16[512,256]{1,0:T(8,128)(2,1)} %bitcast.15, s32[1,2048]{1,0:T(1,128)} %bitcast.19, ...), custom_call_target="tpu_custom_call" | custom-call | flops 200000000 | bytes 1123328 | tf_op jit(solution)/shard_map/pallas_call | solution.py:421
  2.7 1.5 %collective-permute-start = (bf16[128,256]{1,0:T(8,128)(2,1)S(1)}, bf16[128,256]{1,0:T(8,128)(2,1)S(1)}, u32[]{:S(2)}, u32[]{:S(2)}) collective-permute-start(bf16[128,256]{1,0:T(8,128)(2,1)S(1)} %get-tuple-element.81), channel_id=1, source_target_pairs={{0,4},{4,0},{1,5},{5,1},{2,6},{6,2},{3,7},{7,3},{8,12},{12,8},{9,1... | collective-permute-start | bytes 196616 | tf_op jit(solution)/shard_map/ppermute | solution.py:443
  4.2 3.2 %collective-permute-start.1 = (bf16[128,256]{1,0:T(8,128)(2,1)S(1)}, bf16[128,256]{1,0:T(8,128)(2,1)S(1)}, u32[]{:S(2)}, u32[]{:S(2)}) collective-permute-start(bf16[128,256]{1,0:T(8,128)(2,1)S(1)} %get-tuple-element.81), channel_id=1, source_target_pairs={{4,8},{12,16},{20,24},{28,32},{36,40},{44,48},{52,56},{60,64},{68,... | collective-permute-start | bytes 196616 | tf_op jit(solution)/shard_map/ppermute | solution.py:480
  7.4 3.1 %collective-permute-start.2 = (bf16[128,256]{1,0:T(8,128)(2,1)S(1)}, bf16[128,256]{1,0:T(8,128)(2,1)S(1)}, u32[]{:S(2)}, u32[]{:S(2)}) collective-permute-start(bf16[128,256]{1,0:T(8,128)(2,1)S(1)} %get-tuple-element.81), channel_id=1, source_target_pairs={{0,1},{1,2},{2,3},{4,5},{5,6},{6,7},{8,9},{9,10},{10,11},{12,13},{... | collective-permute-start | bytes 196616 | tf_op jit(solution)/shard_map/ppermute | solution.py:478
  10.5 1.3 %collective-permute-start.3 = (bf16[128,256]{1,0:T(8,128)(2,1)S(1)}, bf16[128,256]{1,0:T(8,128)(2,1)S(1)}, u32[]{:S(2)}, u32[]{:S(2)}) collective-permute-start(bf16[128,256]{1,0:T(8,128)(2,1)S(1)} %get-tuple-element.81), channel_id=1, source_target_pairs={{1,0},{2,1},{3,2},{5,4},{6,5},{7,6},{9,8},{10,9},{11,10},{13,12},{... | collective-permute-start | bytes 196616 | tf_op jit(solution)/shard_map/ppermute | solution.py:479
  11.8 3.9 %shard_map.183 = (s32[1,2048]{1,0:T(1,128)S(1)}, f32[2048,512]{1,0:T(8,128)S(1)}, s32[1,3072]{1,0:T(1,128)S(1)}, s32[1,3072]{1,0:T(1,128)S(1)}, bf16[512,512]{1,...) custom-call(bf16[512,256]{1,0:T(8,128)(2,1)S(1)} %get-tuple-element.74.refs_0_, ...), custom_call_target="tpu_custom_call" | custom-call | flops 2200000000 | bytes 6079500 | tf_op jit(solution)/shard_map/pallas_call | solution.py:421
  15.7 1.2 shard_map.184
  16.9 2.2 %collective-permute-start.4 = (bf16[512,256]{1,0:T(8,128)(2,1)S(1)}, bf16[512,256]{1,0:T(8,128)(2,1)S(1)}, u32[]{:S(2)}, u32[]{:S(2)}) collective-permute-start(bf16[512,256]{1,0:T(8,128)(2,1)S(1)} %get-tuple-element.94.g0), channel_id=1, source_target_pairs={{0,1},{1,2},{2,3},{3,0},{4,5},{5,6},{6,7},{7,4},{8,9},{9,10},{10,1... | collective-permute-start | bytes 786440 | tf_op jit(solution)/shard_map/ppermute | solution.py:443
  19.0 0.0 collective-permute-done.ra
  19.0 1.4 %collective-permute-start.5 = (bf16[512,256]{1,0:T(8,128)(2,1)S(1)}, bf16[512,256]{1,0:T(8,128)(2,1)S(1)}, u32[]{:S(2)}, u32[]{:S(2)}) collective-permute-start(bf16[512,256]{1,0:T(8,128)(2,1)S(1)} %get-tuple-element.94.g0), channel_id=1, source_target_pairs={{0,3},{1,0},{2,1},{3,2},{4,7},{5,4},{6,5},{7,6},{8,11},{9,8},{10,9... | collective-permute-start | bytes 786440 | tf_op jit(solution)/shard_map/ppermute | solution.py:443
  20.4 0.0 collective-permute-done.1.rb
  20.4 0.0 collective-permute-done.2.rw
  20.4 0.0 collective-permute-done.3.re
  20.4 5.2 %shard_map.185 = (f32[2048,512]{1,0:T(8,128)S(1)}, bf16[512,512]{1,0:T(8,128)(2,1)S(1)}, f32[512,256]{1,0:T(8,128)S(1)}, bf16[544,256]{1,0:T(8,128)(2,1)S(1)}, bf16[1024,256]{1,0:T(8,128)(2,1)S(1)}) custom-call(f32[2048,512]{1,0:T(8,128)S(1)} %get-tuple-element.80.part_ref, bf16[512,256]{1,0:T(8,128)(2,1)S(1)} %get-tuple-element.74.refs_0_.own_ref, ...), custom_call_target="tpu_custom_call" | custom-call | flops 3200000000 | bytes 11586572 | tf_op jit(solution)/shard_map/pallas_call | solution.py:421
  25.6 0.0 collective-permute-done.4.g1
  25.6 0.4 collective-permute-done.5.g2
  25.9 2.3 %collective-permute-start.7 = (bf16[544,256]{1,0:T(8,128)(2,1)S(1)}, bf16[544,256]{1,0:T(8,128)(2,1)S(1)}, u32[]{:S(2)}, u32[]{:S(2)}) collective-permute-start(bf16[544,256]{1,0:T(8,128)(2,1)S(1)} %get-tuple-element.93.p0), channel_id=1, source_target_pairs={{0,3},{1,0},{2,1},{3,2},{4,7},{5,4},{6,5},{7,6},{8,11},{9,8},{10,9... | collective-permute-start | bytes 835592 | tf_op jit(solution)/shard_map/ppermute | solution.py:443
  28.2 0.0 collective-permute-start.6
  28.2 6.4 %collective-permute-done.7.p2 = bf16[544,256]{1,0:T(8,128)(2,1)S(1)} collective-permute-done((bf16[544,256]{1,0:T(8,128)(2,1)S(1)}, bf16[544,256]{1,0:T(8,128)(2,1)S(1)}, u32[]{:S(2)}, u32[]{:S(2)}) %collective-permute-start.7) | collective-permute-done | bytes 278560 | tf_op jit(solution)/shard_map/ppermute | solution.py:443
  34.6 3.0 %collective-permute-start.9 = (bf16[288,256]{1,0:T(8,128)(2,1)S(1)}, bf16[288,256]{1,0:T(8,128)(2,1)S(1)}, u32[]{:S(2)}, u32[]{:S(2)}) collective-permute-start(bf16[288,256]{1,0:T(8,128)(2,1)S(1)} %slice.17), channel_id=1, source_target_pairs={{0,3},{1,0},{2,1},{3,2},{4,7},{5,4},{6,5},{7,6},{8,11},{9,8},{10,9... | collective-permute-start | bytes 442376 | tf_op jit(solution)/shard_map/ppermute | solution.py:443
  37.6 0.5 collective-permute-done.6.p1
  38.0 0.1 collective-permute-start.8
  38.1 5.9 %collective-permute-done.8.p3 = bf16[256,256]{1,0:T(8,128)(2,1)S(1)} collective-permute-done((bf16[256,256]{1,0:T(8,128)(2,1)S(1)}, bf16[256,256]{1,0:T(8,128)(2,1)S(1)}, u32[]{:S(2)}, u32[]{:S(2)}) %collective-permute-start.8) | collective-permute-done | bytes 131104 | tf_op jit(solution)/shard_map/ppermute | solution.py:443
  44.0 0.0 collective-permute-done.9.p4
  44.0 0.0 collective-permute-start.10
  44.0 7.3 %shard_map.186 = (bf16[512,256]{1,0:T(8,128)(2,1)S(1)}, f32[512,256]{1,0:T(8,128)S(1)}, f32[3072,512]{1,0:T(8,128)S(1)}, bf16[3072,512]{1,0:T(8,128)(2,1)S(1)}, ...) custom-call(bf16[544,256]{1,0:T(8,128)(2,1)S(1)} %get-tuple-element.93.p0, ...), custom_call_target="tpu_custom_call" | custom-call | flops 5200000000 | bytes 16867328 | tf_op jit(solution)/shard_map/pallas_call | solution.py:421
  51.3 0.8 collective-permute-done.10.g3
  52.1 7.5 %shard_map.187 = (f32[512,256]{1,0:T(8,128)S(1)}, f32[2,384,128]{2,1,0:T(8,128)S(1)}) custom-call(bf16[512,256]{1,0:T(8,128)(2,1)S(1)} %get-tuple-element.94.g0, bf16[512,256]{1,0:T(8,128)(2,1)S(1)} %collective-permute-done.4.g1, bf16[512,256]{1,0:T(8,128)(2,1)S(1)} %collective-permute-done.5.g2, bf16[512,256]{1,0:T(8,128)(2,1)S(1)} %collective-permute-done.10.g3, ...), custom_call_target="tpu_custom_call" | custom-call | flops 5600000000 | bytes 17972236 | tf_op jit(solution)/shard_map/pallas_call | solution.py:421
  59.6 6.8 %shard_map.188 = (f32[512,256]{1,0:T(8,128)S(1)}, bf16[2176,128]{1,0:T(8,128)(2,1)S(1)}, f32[1920,128]{1,0:T(8,128)S(1)}, bf16[128,256]{1,0:T(8,128)(2,1)S(1)}, ...) custom-call(f32[512,256]{1,0:T(8,128)S(1)} %get-tuple-element.111.grad_fine_ref, ...), custom_call_target="tpu_custom_call" | custom-call | flops 5600000000 | bytes 9749516 | tf_op jit(solution)/shard_map/pallas_call | solution.py:421
  66.4 2.2 %collective-permute-start.11 = (bf16[2176,128]{1,0:T(8,128)(2,1)S(1)}, bf16[2176,128]{1,0:T(8,128)(2,1)S(1)}, u32[]{:S(2)}, u32[]{:S(2)}) collective-permute-start(bf16[2176,128]{1,0:T(8,128)(2,1)S(1)} %get-tuple-element.118), channel_id=1, source_target_pairs={{0,4},{4,0},{1,5},{5,1},{2,6},{6,2},{3,7},{7,3},{8,12},{12,8},{9,1... | collective-permute-start | bytes 1671176 | tf_op jit(solution)/shard_map/ppermute | solution.py:443
  68.7 1.6 %collective-permute-done.11.got_ref.from_core = bf16[2176,128]{1,0:T(8,128)(2,1)S(1)} collective-permute-done((bf16[2176,128]{1,0:T(8,128)(2,1)S(1)}, bf16[2176,128]{1,0:T(8,128)(2,1)S(1)}, u32[]{:S(2)}, u32[]{:S(2)}) %collective-permute-start.11) | collective-permute-done | bytes 557088 | tf_op jit(solution)/shard_map/ppermute | solution.py:443
  70.2 0.7 shard_map.189
  70.9 0.1 collective-permute-start.12
  71.0 2.7 %collective-permute-start.14 = (bf16[640,128]{1,0:T(8,128)(2,1)S(1)}, bf16[640,128]{1,0:T(8,128)(2,1)S(1)}, u32[]{:S(2)}, u32[]{:S(2)}) collective-permute-start(bf16[640,128]{1,0:T(8,128)(2,1)S(1)} %get-tuple-element.124), channel_id=1, source_target_pairs={{0,3},{1,0},{2,1},{3,2},{4,7},{5,4},{6,5},{7,6},{8,11},{9,8},{10,9... | collective-permute-start | bytes 491528 | tf_op jit(solution)/shard_map/ppermute | solution.py:443
  73.7 0.4 collective-permute-start.13
  74.0 5.6 %collective-permute-start.15 = (bf16[128,256]{1,0:T(8,128)(2,1)S(1)}, bf16[128,256]{1,0:T(8,128)(2,1)S(1)}, u32[]{:S(2)}, u32[]{:S(2)}) collective-permute-start(bf16[128,256]{1,0:T(8,128)(2,1)S(1)} %get-tuple-element.126), channel_id=1, source_target_pairs={{4,8},{12,16},{20,24},{28,32},{36,40},{44,48},{52,56},{60,64},{68,... | collective-permute-start | bytes 196616 | tf_op jit(solution)/shard_map/ppermute | solution.py:584
  79.6 0.0 collective-permute-done.13
  79.6 0.0 collective-permute-done.12.from_west
  79.7 0.0 collective-permute-done.14.from_east
  79.7 0.1 add_convert_fusion
  79.8 1.8 %collective-permute-done.15.from_b = bf16[128,256]{1,0:T(8,128)(2,1)S(1)} collective-permute-done((bf16[128,256]{1,0:T(8,128)(2,1)S(1)}, bf16[128,256]{1,0:T(8,128)(2,1)S(1)}, u32[]{:S(2)}, u32[]{:S(2)}) %collective-permute-start.15) | collective-permute-done | bytes 65568 | tf_op jit(solution)/shard_map/ppermute | solution.py:584
  81.6 15.2 %all_to_all.10 = bf16[16,48,128]{2,1,0:T(8,128)(2,1)S(1)} all-to-all(bf16[16,48,128]{2,1,0:T(8,128)(2,1)S(1)} %pad_maximum_fusion), channel_id=1, replica_groups=mesh['z'=4,'y'=4,'core'=2,'x'=4] {'z','y'}, dimensions={0} | all-to-all | bytes 393216 | tf_op jit(solution)/shard_map/all_to_all | solution.py:611
  96.8 0.1 broadcast_in_dim.17
  96.9 18.9 %all_to_all.11.ref = bf16[64,48,128]{2,1,0:T(8,128)(2,1)S(1)} all-to-all(bf16[64,48,128]{2,1,0:T(8,128)(2,1)S(1)} %broadcast_in_dim.17), channel_id=1, replica_groups=mesh['z'=4,'y'=4,'core'=2,'x'=4] {'z','y','x'}, dimensions={0} | all-to-all | bytes 1572864 | tf_op jit(solution)/shard_map/all_to_all | solution.py:614
  115.8 3.2 %collective-permute-start.16 = (bf16[64,48,128]{2,1,0:T(8,128)(2,1)S(1)}, bf16[64,48,128]{2,1,0:T(8,128)(2,1)S(1)}, u32[]{:S(2)}, u32[]{:S(2)}) collective-permute-start(bf16[64,48,128]{2,1,0:T(8,128)(2,1)S(1)} %all_to_all.11.ref), channel_id=1, source_target_pairs={{0,4},{4,0},{1,5},{5,1},{2,6},{6,2},{3,7},{7,3},{8,12},{12,8},{9,1... | collective-permute-start | bytes 2359304 | tf_op jit(solution)/shard_map/ppermute | solution.py:443
  119.1 1.8 %shard_map.191 = (f32[512,512]{1,0:T(8,128)}, f32[512,256]{1,0:T(8,128)}, f32[512,512]{1,0:T(8,128)}, f32[512,256]{1,0:T(8,128)}) custom-call(bf16[64,48,128]{2,1,0:T(8,128)(2,1)S(1)} %all_to_all.11.ref, s32[3]{0:T(128)S(1)} %pad_add_fusion.refs_4_.place_ref), custom_call_target="tpu_custom_call" | custom-call | bytes 3145728 | tf_op jit(solution)/shard_map/pallas_call | solution.py:345
  120.8 1.7 %shard_map.190 = f32[512,256]{1,0:T(8,128)} custom-call(f32[512,256]{1,0:T(8,128)S(1)} %get-tuple-element.129.local_ref, bf16[2176,128]{1,0:T(8,128)(2,1)S(1)} %collective-permute-done.11.got_ref.from_core, bf16[128,256]{1,0:T(8,128)(2,1)S(1)} %collective-permute-done.15.from_b, bf16[640,128]{1,0:T(8,128)(2,1)S(1)} %collective-permute-done.12.from_west, ...), custom_call_target="tpu_custom_call" | custom-call | flops 200000000 | bytes 1999372 | tf_op jit(solution)/shard_map/pallas_call | solution.py:421
  122.5 0.0 collective-permute-done.16.ref
  122.5 1.8 %shard_map.192 = (f32[512,512]{1,0:T(8,128)}, f32[512,256]{1,0:T(8,128)}, f32[512,512]{1,0:T(8,128)}, f32[512,256]{1,0:T(8,128)}) custom-call(bf16[64,48,128]{2,1,0:T(8,128)(2,1)S(1)} %collective-permute-done.16.ref, s32[3]{0:T(128)S(1)} %pad_add_fusion.refs_4_.place_ref, ...), custom_call_target="tpu_custom_call", output_to_operand_aliasing={{0}: (2, {}), {1}: (3, {}), {2}: (4, {}), {3}: (5, {})} | custom-call | bytes 3145728 | tf_op jit(solution)/shard_map/pallas_call | solution.py:345
  (5 shorter events, 0.1 us)
Async XLA Ops:
  2.7 16.4 %collective-permute-start = (bf16[128,256]{1,0:T(8,128)(2,1)S(1)}, bf16[128,256]{1,0:T(8,128)(2,1)S(1)}, u32[]{:S(2)}, u32[]{:S(2)}) collective-permute-start(bf16[128,256]{1,0:T(8,128)(2,1)S(1)} %get-tuple-element.81), channel_id=1, source_target_pairs={{0,4},{4,0},{1,5},{5,1},{2,6},{6,2},{3,7},{7,3},{8,12},{12,8},{9,1... | collective-permute-start | bytes 196616 | tf_op jit(solution)/shard_map/ppermute | solution.py:443
  4.2 16.2 %collective-permute-start.1 = (bf16[128,256]{1,0:T(8,128)(2,1)S(1)}, bf16[128,256]{1,0:T(8,128)(2,1)S(1)}, u32[]{:S(2)}, u32[]{:S(2)}) collective-permute-start(bf16[128,256]{1,0:T(8,128)(2,1)S(1)} %get-tuple-element.81), channel_id=1, source_target_pairs={{4,8},{12,16},{20,24},{28,32},{36,40},{44,48},{52,56},{60,64},{68,... | collective-permute-start | bytes 196616 | tf_op jit(solution)/shard_map/ppermute | solution.py:480
  7.4 13.0 %collective-permute-start.2 = (bf16[128,256]{1,0:T(8,128)(2,1)S(1)}, bf16[128,256]{1,0:T(8,128)(2,1)S(1)}, u32[]{:S(2)}, u32[]{:S(2)}) collective-permute-start(bf16[128,256]{1,0:T(8,128)(2,1)S(1)} %get-tuple-element.81), channel_id=1, source_target_pairs={{0,1},{1,2},{2,3},{4,5},{5,6},{6,7},{8,9},{9,10},{10,11},{12,13},{... | collective-permute-start | bytes 196616 | tf_op jit(solution)/shard_map/ppermute | solution.py:478
  10.5 9.9 %collective-permute-start.3 = (bf16[128,256]{1,0:T(8,128)(2,1)S(1)}, bf16[128,256]{1,0:T(8,128)(2,1)S(1)}, u32[]{:S(2)}, u32[]{:S(2)}) collective-permute-start(bf16[128,256]{1,0:T(8,128)(2,1)S(1)} %get-tuple-element.81), channel_id=1, source_target_pairs={{1,0},{2,1},{3,2},{5,4},{6,5},{7,6},{9,8},{10,9},{11,10},{13,12},{... | collective-permute-start | bytes 196616 | tf_op jit(solution)/shard_map/ppermute | solution.py:479
  16.9 8.7 %collective-permute-start.4 = (bf16[512,256]{1,0:T(8,128)(2,1)S(1)}, bf16[512,256]{1,0:T(8,128)(2,1)S(1)}, u32[]{:S(2)}, u32[]{:S(2)}) collective-permute-start(bf16[512,256]{1,0:T(8,128)(2,1)S(1)} %get-tuple-element.94.g0), channel_id=1, source_target_pairs={{0,1},{1,2},{2,3},{3,0},{4,5},{5,6},{6,7},{7,4},{8,9},{9,10},{10,1... | collective-permute-start | bytes 786440 | tf_op jit(solution)/shard_map/ppermute | solution.py:443
  19.0 6.9 %collective-permute-start.5 = (bf16[512,256]{1,0:T(8,128)(2,1)S(1)}, bf16[512,256]{1,0:T(8,128)(2,1)S(1)}, u32[]{:S(2)}, u32[]{:S(2)}) collective-permute-start(bf16[512,256]{1,0:T(8,128)(2,1)S(1)} %get-tuple-element.94.g0), channel_id=1, source_target_pairs={{0,3},{1,0},{2,1},{3,2},{4,7},{5,4},{6,5},{7,6},{8,11},{9,8},{10,9... | collective-permute-start | bytes 786440 | tf_op jit(solution)/shard_map/ppermute | solution.py:443
  25.9 8.7 %collective-permute-start.7 = (bf16[544,256]{1,0:T(8,128)(2,1)S(1)}, bf16[544,256]{1,0:T(8,128)(2,1)S(1)}, u32[]{:S(2)}, u32[]{:S(2)}) collective-permute-start(bf16[544,256]{1,0:T(8,128)(2,1)S(1)} %get-tuple-element.93.p0), channel_id=1, source_target_pairs={{0,3},{1,0},{2,1},{3,2},{4,7},{5,4},{6,5},{7,6},{8,11},{9,8},{10,9... | collective-permute-start | bytes 835592 | tf_op jit(solution)/shard_map/ppermute | solution.py:443
  28.2 9.8 %collective-permute-start.6 = (bf16[544,256]{1,0:T(8,128)(2,1)S(1)}, bf16[544,256]{1,0:T(8,128)(2,1)S(1)}, u32[]{:S(2)}, u32[]{:S(2)}) collective-permute-start(bf16[544,256]{1,0:T(8,128)(2,1)S(1)} %get-tuple-element.93.p0), channel_id=1, source_target_pairs={{0,1},{1,2},{2,3},{3,0},{4,5},{5,6},{6,7},{7,4},{8,9},{9,10},{10,1... | collective-permute-start | bytes 835592 | tf_op jit(solution)/shard_map/ppermute | solution.py:443
  34.6 9.4 %collective-permute-start.9 = (bf16[288,256]{1,0:T(8,128)(2,1)S(1)}, bf16[288,256]{1,0:T(8,128)(2,1)S(1)}, u32[]{:S(2)}, u32[]{:S(2)}) collective-permute-start(bf16[288,256]{1,0:T(8,128)(2,1)S(1)} %slice.17), channel_id=1, source_target_pairs={{0,3},{1,0},{2,1},{3,2},{4,7},{5,4},{6,5},{7,6},{8,11},{9,8},{10,9... | collective-permute-start | bytes 442376 | tf_op jit(solution)/shard_map/ppermute | solution.py:443
  38.0 6.0 %collective-permute-start.8 = (bf16[256,256]{1,0:T(8,128)(2,1)S(1)}, bf16[256,256]{1,0:T(8,128)(2,1)S(1)}, u32[]{:S(2)}, u32[]{:S(2)}) collective-permute-start(bf16[256,256]{1,0:T(8,128)(2,1)S(1)} %slice.16), channel_id=1, source_target_pairs={{0,1},{1,2},{2,3},{3,0},{4,5},{5,6},{6,7},{7,4},{8,9},{9,10},{10,1... | collective-permute-start | bytes 393224 | tf_op jit(solution)/shard_map/ppermute | solution.py:443
  44.0 8.1 %collective-permute-start.10 = (bf16[512,256]{1,0:T(8,128)(2,1)S(1)}, bf16[512,256]{1,0:T(8,128)(2,1)S(1)}, u32[]{:S(2)}, u32[]{:S(2)}) collective-permute-start(bf16[512,256]{1,0:T(8,128)(2,1)S(1)} %get-tuple-element.94.g0), channel_id=1, source_target_pairs={{0,2},{1,3},{2,0},{3,1},{4,6},{5,7},{6,4},{7,5},{8,10},{9,11},{10,... | collective-permute-start | bytes 786440 | tf_op jit(solution)/shard_map/ppermute | solution.py:443
  66.4 3.8 %collective-permute-start.11 = (bf16[2176,128]{1,0:T(8,128)(2,1)S(1)}, bf16[2176,128]{1,0:T(8,128)(2,1)S(1)}, u32[]{:S(2)}, u32[]{:S(2)}) collective-permute-start(bf16[2176,128]{1,0:T(8,128)(2,1)S(1)} %get-tuple-element.118), channel_id=1, source_target_pairs={{0,4},{4,0},{1,5},{5,1},{2,6},{6,2},{3,7},{7,3},{8,12},{12,8},{9,1... | collective-permute-start | bytes 1671176 | tf_op jit(solution)/shard_map/ppermute | solution.py:443
  70.9 8.7 %collective-permute-start.12 = (bf16[640,128]{1,0:T(8,128)(2,1)S(1)}, bf16[640,128]{1,0:T(8,128)(2,1)S(1)}, u32[]{:S(2)}, u32[]{:S(2)}) collective-permute-start(bf16[640,128]{1,0:T(8,128)(2,1)S(1)} %get-tuple-element.122), channel_id=1, source_target_pairs={{0,1},{1,2},{2,3},{3,0},{4,5},{5,6},{6,7},{7,4},{8,9},{9,10},{10,1... | collective-permute-start | bytes 491528 | tf_op jit(solution)/shard_map/ppermute | solution.py:443
  71.0 8.7 %collective-permute-start.14 = (bf16[640,128]{1,0:T(8,128)(2,1)S(1)}, bf16[640,128]{1,0:T(8,128)(2,1)S(1)}, u32[]{:S(2)}, u32[]{:S(2)}) collective-permute-start(bf16[640,128]{1,0:T(8,128)(2,1)S(1)} %get-tuple-element.124), channel_id=1, source_target_pairs={{0,3},{1,0},{2,1},{3,2},{4,7},{5,4},{6,5},{7,6},{8,11},{9,8},{10,9... | collective-permute-start | bytes 491528 | tf_op jit(solution)/shard_map/ppermute | solution.py:443
  73.7 6.0 %collective-permute-start.13 = (bf16[384,128]{1,0:T(8,128)(2,1)S(1)}, bf16[384,128]{1,0:T(8,128)(2,1)S(1)}, u32[]{:S(2)}, u32[]{:S(2)}) collective-permute-start(bf16[384,128]{1,0:T(8,128)(2,1)S(1)} %get-tuple-element.123), channel_id=1, source_target_pairs={{0,2},{1,3},{2,0},{3,1},{4,6},{5,7},{6,4},{7,5},{8,10},{9,11},{10,... | collective-permute-start | bytes 294920 | tf_op jit(solution)/shard_map/ppermute | solution.py:443
  74.0 7.5 %collective-permute-start.15 = (bf16[128,256]{1,0:T(8,128)(2,1)S(1)}, bf16[128,256]{1,0:T(8,128)(2,1)S(1)}, u32[]{:S(2)}, u32[]{:S(2)}) collective-permute-start(bf16[128,256]{1,0:T(8,128)(2,1)S(1)} %get-tuple-element.126), channel_id=1, source_target_pairs={{4,8},{12,16},{20,24},{28,32},{36,40},{44,48},{52,56},{60,64},{68,... | collective-permute-start | bytes 196616 | tf_op jit(solution)/shard_map/ppermute | solution.py:584
  115.8 6.7 %collective-permute-start.16 = (bf16[64,48,128]{2,1,0:T(8,128)(2,1)S(1)}, bf16[64,48,128]{2,1,0:T(8,128)(2,1)S(1)}, u32[]{:S(2)}, u32[]{:S(2)}) collective-permute-start(bf16[64,48,128]{2,1,0:T(8,128)(2,1)S(1)} %all_to_all.11.ref), channel_id=1, source_target_pairs={{0,4},{4,0},{1,5},{5,1},{2,6},{6,2},{3,7},{7,3},{8,12},{12,8},{9,1... | collective-permute-start | bytes 2359304 | tf_op jit(solution)/shard_map/ppermute | solution.py:443

commit v3 on v1

--- a/solution.py
+++ b/solution.py
@@ -113,7 +113,8 @@
     col, core = place_ref[0], place_ref[1]
     table[0:nodes, :] = own_ref[...]
     table[pl.ds(pl.multiple_of(nodes + rim * (1 - core), rim), rim), :] = ra[...]
-    table[pl.ds(pl.multiple_of(nodes + rim * core, rim), rim), :] = rb[...]
+    beyond = rb[...].astype(F32) * jnp.where(place_ref[3] > 0, 1.0, 0.0)
+    table[pl.ds(pl.multiple_of(nodes + rim * core, rim), rim), :] = beyond.astype(BF)
     west = rw[0:rim, :].astype(F32) * jnp.where(col > 0, 1.0, 0.0)
     east = re[0:rim, :].astype(F32) * jnp.where(col < 3, 1.0, 0.0)
     table[nodes + 2 * rim : nodes + 3 * rim, :] = west.astype(BF)
@@ -289,7 +290,8 @@
 
     west = wide(from_west) * jnp.where(col > 0, 1.0, 0.0)
     east = wide(from_east) * jnp.where(col < 3, 1.0, 0.0)
-    arrived = (wide(from_core) + from_b[...].astype(F32)) + (west + east)
+    beyond = from_b[...].astype(F32) * jnp.where(place_ref[3] > 0, 1.0, 0.0)
+    arrived = (wide(from_core) + beyond) + (west + east)
     high, low = halves(arrived)
     out_ref[...] = local_ref[...] + dot(adds, high) + dot(adds, low)
 
@@ -418,7 +420,12 @@
     coarse_gain = coarse_gain[None, :]
     between = [(i, i + 1) for i in range(1, rows - 1, 2)]
     between = between + [(target, source) for source, target in between]
-    place = jnp.stack([lax.axis_index("x"), lax.axis_index("core"), 128 * live_blocks[0, 0]])
+    between = between + [(rows - 1, 0), (0, rows - 1)]
+    row = lax.axis_index(ROW)
+    inside = jnp.logical_and(row > 0, row < rows - 1)
+    place = jnp.stack(
+        [lax.axis_index("x"), lax.axis_index("core"), 128 * live_blocks[0, 0], inside]
+    )
     own, place = lax.optimization_barrier((own, place.astype(jnp.int32)))
     wide = 2 * feature
 

time: 119 us -> 120 us (level)
  starting transfers between devices: 35 us -> 30.3 us
  waiting for transfers between devices: 11.8 us -> 15.4 us
  blocking collectives: 34 us -> 36.1 us
    ppermute x13, waiting for transfers between devices: 11.5 us -> 15.3 us  [send(): lax.ppermute(value, axis, [(i, (i + step) % size) for i in range(size)])]
    ppermute x1, starting transfers between devices: 4.13 us -> 2.23 us  [shards(): from_b = lax.ppermute(ghost_b, ROW, between)]
    ppermute x1, starting transfers between devices: 3.08 us -> 1.18 us  [shards(): from_b = lax.ppermute(rim, ROW, between)]
    all_to_all x1, blocking collectives: 18.8 us -> 20.7 us  [shards(): mine = lax.all_to_all(copies, CHIPS, 0, 0, tiled=True)]
  transfers between devices with their start and end apart: 15 -> 15, of which waited for: 8 -> 7; matrix products, arithmetic and copies ran while one was open for 0% -> 0% of each run, Pallas kernels for 8% -> 8%
where the time goes in v3:
time: 120 us
  blocking collectives  36.1 us (30%)
  Pallas kernels  35.9 us (30%)
  starting transfers between devices  30.3 us (25%)
  waiting for transfers between devices  15.4 us (13%)
  between operations  1.42 us (1%)
    pallas_call x8, Pallas kernels, run(): pl.pallas_call(body if copies else kernel, out_shape=shapes, in_specs=[pl...  35.9 us
    ppermute x13, starting transfers between devices, send(): lax.ppermute(value, axis, [(i, (i + step) % size) for i in range(size)])  26.9 us
    all_to_all x1, blocking collectives, shards(): mine = lax.all_to_all(copies, CHIPS, 0, 0, tiled=True)  20.7 us
    all_to_all x1, blocking collectives, shards(): both = lax.all_to_all(both, PLANE, 0, 0, tiled=True)  15.4 us
    ppermute x13, waiting for transfers between devices, send(): lax.ppermute(value, axis, [(i, (i + step) % size) for i in range(size)])  15.3 us
  transfers between devices with their start and end apart: 15, of which 7 were waited for; matrix products, arithmetic and copies ran while one was open for 0% of the time, Pallas kernels for 8%

profile of v3, /device:TPU:1, one launch (start us, length us, event | category | flops | bytes accessed | tf_op | source)
XLA Modules:
  0.0 119.6 jit_solution(18345335396631662454)
XLA Ops:
  1.3 0.1 pad_add_fusion.refs_5_.place_ref
  1.4 2.4 %shard_map.182 = (bf16[128,256]{1,0:T(8,128)(2,1)S(1)}, bf16[672,256]{1,0:T(8,128)(2,1)S(1)}, s32[1,2048]{1,0:T(1,128)S(1)}, bf16[512,256]{1,0:T(8,128)(2,1)S(1)...) custom-call(bf16[512,256]{1,0:T(8,128)(2,1)} %bitcast.17, ...), custom_call_target="tpu_custom_call" | custom-call | bytes 2013200 | tf_op jit(solution)/shard_map/pallas_call | solution.py:382
  3.8 2.1 %collective-permute-start.2 = (bf16[672,256]{1,0:T(8,128)(2,1)S(1)}, bf16[672,256]{1,0:T(8,128)(2,1)S(1)}, u32[]{:S(2)}, u32[]{:S(2)}) collective-permute-start(bf16[672,256]{1,0:T(8,128)(2,1)S(1)} %get-tuple-element.60.g0), channel_id=1, source_target_pairs={{0,1},{1,2},{2,3},{3,0},{4,5},{5,6},{6,7},{7,4},{8,9},{9,10},{10,1... | collective-permute-start | bytes 1032200 | tf_op jit(solution)/shard_map/ppermute | solution.py:402
  5.9 1.4 %collective-permute-start.3 = (bf16[672,256]{1,0:T(8,128)(2,1)S(1)}, bf16[672,256]{1,0:T(8,128)(2,1)S(1)}, u32[]{:S(2)}, u32[]{:S(2)}) collective-permute-start(bf16[672,256]{1,0:T(8,128)(2,1)S(1)} %get-tuple-element.60.g0), channel_id=1, source_target_pairs={{0,3},{1,0},{2,1},{3,2},{4,7},{5,4},{6,5},{7,6},{8,11},{9,8},{10,9... | collective-permute-start | bytes 1032200 | tf_op jit(solution)/shard_map/ppermute | solution.py:402
  7.3 1.7 %collective-permute-start.4 = (bf16[544,256]{1,0:T(8,128)(2,1)S(1)}, bf16[544,256]{1,0:T(8,128)(2,1)S(1)}, u32[]{:S(2)}, u32[]{:S(2)}) collective-permute-start(bf16[544,256]{1,0:T(8,128)(2,1)S(1)} %slice.15), channel_id=1, source_target_pairs={{0,2},{1,3},{2,0},{3,1},{4,6},{5,7},{6,4},{7,5},{8,10},{9,11},{10,... | collective-permute-start | bytes 835592 | tf_op jit(solution)/shard_map/ppermute | solution.py:402
  9.0 1.5 %collective-permute-start = (bf16[128,256]{1,0:T(8,128)(2,1)S(1)}, bf16[128,256]{1,0:T(8,128)(2,1)S(1)}, u32[]{:S(2)}, u32[]{:S(2)}) collective-permute-start(bf16[128,256]{1,0:T(8,128)(2,1)S(1)} %get-tuple-element.59), channel_id=1, source_target_pairs={{0,4},{4,0},{1,5},{5,1},{2,6},{6,2},{3,7},{7,3},{8,12},{12,8},{9,1... | collective-permute-start | bytes 196616 | tf_op jit(solution)/shard_map/ppermute | solution.py:402
  10.5 1.2 collective-permute-start.1
  11.7 2.6 %shard_map.183 = (f32[2048,512]{1,0:T(8,128)S(1)}, s32[1,3072]{1,0:T(1,128)S(1)}, s32[1,3072]{1,0:T(1,128)S(1)}, bf16[512,512]{1,0:T(8,128)(2,1)S(1)}, bf16[512,...) custom-call(bf16[512,256]{1,0:T(8,128)(2,1)S(1)} %get-tuple-element.54.refs_0_.own_ref, ...), custom_call_target="tpu_custom_call" | custom-call | bytes 6071296 | tf_op jit(solution)/shard_map/pallas_call | solution.py:382
  14.4 0.0 collective-permute-done.ra
  14.4 0.2 collective-permute-done.1.rb
  14.5 0.0 collective-permute-done.2.rw.g1
  14.5 0.0 collective-permute-done.3.re.g2
  14.5 5.1 %shard_map.184 = (f32[2048,512]{1,0:T(8,128)S(1)}, bf16[512,512]{1,0:T(8,128)(2,1)S(1)}, f32[512,256]{1,0:T(8,128)S(1)}, bf16[512,256]{1,0:T(8,128)(2,1)S(1)}, bf16[1024,256]{1,0:T(8,128)(2,1)S(1)}) custom-call(f32[2048,512]{1,0:T(8,128)S(1)} %get-tuple-element.58.part_ref, bf16[512,256]{1,0:T(8,128)(2,1)S(1)} %get-tuple-element.54.refs_0_.own_ref, ...), custom_call_target="tpu_custom_call" | custom-call | bytes 12110864 | tf_op jit(solution)/shard_map/pallas_call | solution.py:382
  19.7 2.1 %collective-permute-done.4.g3 = bf16[544,256]{1,0:T(8,128)(2,1)S(1)} collective-permute-done((bf16[544,256]{1,0:T(8,128)(2,1)S(1)}, bf16[544,256]{1,0:T(8,128)(2,1)S(1)}, u32[]{:S(2)}, u32[]{:S(2)}) %collective-permute-start.4) | collective-permute-done | bytes 278560 | tf_op jit(solution)/shard_map/ppermute | solution.py:402
  21.8 0.5 collective-permute-start.5
  22.3 2.1 %collective-permute-start.6 = (bf16[512,256]{1,0:T(8,128)(2,1)S(1)}, bf16[512,256]{1,0:T(8,128)(2,1)S(1)}, u32[]{:S(2)}, u32[]{:S(2)}) collective-permute-start(bf16[512,256]{1,0:T(8,128)(2,1)S(1)} %get-tuple-element.65.p0), channel_id=1, source_target_pairs={{0,3},{1,0},{2,1},{3,2},{4,7},{5,4},{6,5},{7,6},{8,11},{9,8},{10,9... | collective-permute-start | bytes 786440 | tf_op jit(solution)/shard_map/ppermute | solution.py:402
  24.5 3.8 %collective-permute-done.5.p1 = bf16[512,256]{1,0:T(8,128)(2,1)S(1)} collective-permute-done((bf16[512,256]{1,0:T(8,128)(2,1)S(1)}, bf16[512,256]{1,0:T(8,128)(2,1)S(1)}, u32[]{:S(2)}, u32[]{:S(2)}) %collective-permute-start.5) | collective-permute-done | bytes 262176 | tf_op jit(solution)/shard_map/ppermute | solution.py:402
  28.2 0.1 collective-permute-start.7
  28.3 0.0 collective-permute-done.6.p2
  28.4 2.9 %collective-permute-start.8 = (bf16[256,256]{1,0:T(8,128)(2,1)S(1)}, bf16[256,256]{1,0:T(8,128)(2,1)S(1)}, u32[]{:S(2)}, u32[]{:S(2)}) collective-permute-start(bf16[256,256]{1,0:T(8,128)(2,1)S(1)} %slice.21), channel_id=1, source_target_pairs={{0,3},{1,0},{2,1},{3,2},{4,7},{5,4},{6,5},{7,6},{8,11},{9,8},{10,9... | collective-permute-start | bytes 393224 | tf_op jit(solution)/shard_map/ppermute | solution.py:402
  31.3 3.7 %collective-permute-done.7.p3 = bf16[256,256]{1,0:T(8,128)(2,1)S(1)} collective-permute-done((bf16[256,256]{1,0:T(8,128)(2,1)S(1)}, bf16[256,256]{1,0:T(8,128)(2,1)S(1)}, u32[]{:S(2)}, u32[]{:S(2)}) %collective-permute-start.7) | collective-permute-done | bytes 131104 | tf_op jit(solution)/shard_map/ppermute | solution.py:402
  35.0 0.0 collective-permute-done.8.p4
  35.0 14.0 %shard_map.185 = (f32[512,256]{1,0:T(8,128)S(1)}, f32[2,384,128]{2,1,0:T(8,128)S(1)}) custom-call(bf16[512,256]{1,0:T(8,128)(2,1)S(1)} %get-tuple-element.65.p0, bf16[512,256]{1,0:T(8,128)(2,1)S(1)} %collective-permute-done.5.p1, bf16[512,256]{1,0:T(8,128)(2,1)S(1)} %collective-permute-done.6.p2, bf16[256,256]{1,0:T(8,128)(2,1)S(1)} %collective-permute-done.7.p3, ...), custom_call_target="tpu_custom_call" | custom-call | bytes 4353040 | tf_op jit(solution)/shard_map/pallas_call | solution.py:382
  49.0 6.9 %shard_map.186 = (f32[512,256]{1,0:T(8,128)S(1)}, bf16[2176,128]{1,0:T(8,128)(2,1)S(1)}, f32[1920,128]{1,0:T(8,128)S(1)}, bf16[128,256]{1,0:T(8,128)(2,1)S(1)}, ...) custom-call(f32[512,256]{1,0:T(8,128)S(1)} %get-tuple-element.73.grad_fine_ref, ...), custom_call_target="tpu_custom_call" | custom-call | bytes 9749520 | tf_op jit(solution)/shard_map/pallas_call | solution.py:382
  55.9 7.6 %collective-permute-start.9 = (bf16[2176,128]{1,0:T(8,128)(2,1)S(1)}, bf16[2176,128]{1,0:T(8,128)(2,1)S(1)}, u32[]{:S(2)}, u32[]{:S(2)}) collective-permute-start(bf16[2176,128]{1,0:T(8,128)(2,1)S(1)} %get-tuple-element.80), channel_id=1, source_target_pairs={{0,4},{4,0},{1,5},{5,1},{2,6},{6,2},{3,7},{7,3},{8,12},{12,8},{9,1... | collective-permute-start | bytes 1671176 | tf_op jit(solution)/shard_map/ppermute | solution.py:402
  63.4 1.6 %collective-permute-done.9.got_ref.from_core = bf16[2176,128]{1,0:T(8,128)(2,1)S(1)} collective-permute-done((bf16[2176,128]{1,0:T(8,128)(2,1)S(1)}, bf16[2176,128]{1,0:T(8,128)(2,1)S(1)}, u32[]{:S(2)}, u32[]{:S(2)}) %collective-permute-start.9) | collective-permute-done | bytes 557088 | tf_op jit(solution)/shard_map/ppermute | solution.py:402
  65.0 0.7 shard_map.187
  65.7 0.1 collective-permute-start.10
  65.8 3.3 %collective-permute-start.12 = (bf16[640,128]{1,0:T(8,128)(2,1)S(1)}, bf16[640,128]{1,0:T(8,128)(2,1)S(1)}, u32[]{:S(2)}, u32[]{:S(2)}) collective-permute-start(bf16[640,128]{1,0:T(8,128)(2,1)S(1)} %get-tuple-element.86), channel_id=1, source_target_pairs={{0,3},{1,0},{2,1},{3,2},{4,7},{5,4},{6,5},{7,6},{8,11},{9,8},{10,9... | collective-permute-start | bytes 491528 | tf_op jit(solution)/shard_map/ppermute | solution.py:402
  69.1 1.1 collective-permute-start.11
  70.2 2.2 %collective-permute-start.13 = (bf16[128,256]{1,0:T(8,128)(2,1)S(1)}, bf16[128,256]{1,0:T(8,128)(2,1)S(1)}, u32[]{:S(2)}, u32[]{:S(2)}) collective-permute-start(bf16[128,256]{1,0:T(8,128)(2,1)S(1)} %get-tuple-element.88), channel_id=1, source_target_pairs={{4,8},{12,16},{20,24},{28,32},{36,40},{44,48},{52,56},{60,64},{68,... | collective-permute-start | bytes 196616 | tf_op jit(solution)/shard_map/ppermute | solution.py:524
  72.4 3.8 %collective-permute-done.11 = bf16[384,128]{1,0:T(8,128)(2,1)S(1)} collective-permute-done((bf16[384,128]{1,0:T(8,128)(2,1)S(1)}, bf16[384,128]{1,0:T(8,128)(2,1)S(1)}, u32[]{:S(2)}, u32[]{:S(2)}) %collective-permute-start.11) | collective-permute-done | bytes 98336 | tf_op jit(solution)/shard_map/ppermute | solution.py:402
  76.2 0.0 collective-permute-done.10.from_west
  76.2 0.0 collective-permute-done.12.from_east
  76.2 0.1 add_convert_fusion
  76.3 0.0 collective-permute-done.13.from_b
  76.3 15.4 %all_to_all.10 = bf16[16,48,128]{2,1,0:T(8,128)(2,1)S(1)} all-to-all(bf16[16,48,128]{2,1,0:T(8,128)(2,1)S(1)} %pad_maximum_fusion), channel_id=1, replica_groups=mesh['z'=4,'y'=4,'core'=2,'x'=4] {'z','y'}, dimensions={0} | all-to-all | bytes 393216 | tf_op jit(solution)/shard_map/all_to_all | solution.py:551
  91.8 0.1 broadcast_in_dim.17
  91.9 20.7 %all_to_all.11.mine_ref = bf16[64,48,128]{2,1,0:T(8,128)(2,1)S(1)} all-to-all(bf16[64,48,128]{2,1,0:T(8,128)(2,1)S(1)} %broadcast_in_dim.17), channel_id=1, replica_groups=mesh['z'=4,'y'=4,'core'=2,'x'=4] {'z','y','x'}, dimensions={0} | all-to-all | bytes 1572864 | tf_op jit(solution)/shard_map/all_to_all | solution.py:554
  112.6 2.5 %collective-permute-start.14 = (bf16[64,48,128]{2,1,0:T(8,128)(2,1)S(1)}, bf16[64,48,128]{2,1,0:T(8,128)(2,1)S(1)}, u32[]{:S(2)}, u32[]{:S(2)}) collective-permute-start(bf16[64,48,128]{2,1,0:T(8,128)(2,1)S(1)} %all_to_all.11.mine_ref), channel_id=1, source_target_pairs={{0,4},{4,0},{1,5},{5,1},{2,6},{6,2},{3,7},{7,3},{8,12},{12,8},{9,1... | collective-permute-start | bytes 2359304 | tf_op jit(solution)/shard_map/ppermute | solution.py:402
  115.1 1.7 %shard_map.188 = f32[512,256]{1,0:T(8,128)} custom-call(f32[512,256]{1,0:T(8,128)S(1)} %get-tuple-element.91.local_ref, bf16[2176,128]{1,0:T(8,128)(2,1)S(1)} %collective-permute-done.9.got_ref.from_core, bf16[128,256]{1,0:T(8,128)(2,1)S(1)} %collective-permute-done.13.from_b, bf16[640,128]{1,0:T(8,128)(2,1)S(1)} %collective-permute-done.10.from_west, ...), custom_call_target="tpu_custom_call" | custom-call | bytes 1999376 | tf_op jit(solution)/shard_map/pallas_call | solution.py:382
  116.8 0.3 collective-permute-done.14.other_ref
  117.0 2.5 %shard_map.189 = (f32[512,512]{1,0:T(8,128)}, f32[512,256]{1,0:T(8,128)}, f32[512,512]{1,0:T(8,128)}, f32[512,256]{1,0:T(8,128)}) custom-call(bf16[64,48,128]{2,1,0:T(8,128)(2,1)S(1)} %all_to_all.11.mine_ref, bf16[64,48,128]{2,1,0:T(8,128)(2,1)S(1)} %collective-permute-done.14.other_ref, s32[4]{0:T(128)S(1)} %pad_add_fusion.refs_5_.place_ref), custom_call_target="tpu_custom_call" | custom-call | bytes 4718608 | tf_op jit(solution)/shard_map/pallas_call | solution.py:382
  (6 shorter events, 0.1 us)
Async XLA Ops:
  3.8 10.7 %collective-permute-start.2 = (bf16[672,256]{1,0:T(8,128)(2,1)S(1)}, bf16[672,256]{1,0:T(8,128)(2,1)S(1)}, u32[]{:S(2)}, u32[]{:S(2)}) collective-permute-start(bf16[672,256]{1,0:T(8,128)(2,1)S(1)} %get-tuple-element.60.g0), channel_id=1, source_target_pairs={{0,1},{1,2},{2,3},{3,0},{4,5},{5,6},{6,7},{7,4},{8,9},{9,10},{10,1... | collective-permute-start | bytes 1032200 | tf_op jit(solution)/shard_map/ppermute | solution.py:402
  5.9 8.6 %collective-permute-start.3 = (bf16[672,256]{1,0:T(8,128)(2,1)S(1)}, bf16[672,256]{1,0:T(8,128)(2,1)S(1)}, u32[]{:S(2)}, u32[]{:S(2)}) collective-permute-start(bf16[672,256]{1,0:T(8,128)(2,1)S(1)} %get-tuple-element.60.g0), channel_id=1, source_target_pairs={{0,3},{1,0},{2,1},{3,2},{4,7},{5,4},{6,5},{7,6},{8,11},{9,8},{10,9... | collective-permute-start | bytes 1032200 | tf_op jit(solution)/shard_map/ppermute | solution.py:402
  7.3 14.5 %collective-permute-start.4 = (bf16[544,256]{1,0:T(8,128)(2,1)S(1)}, bf16[544,256]{1,0:T(8,128)(2,1)S(1)}, u32[]{:S(2)}, u32[]{:S(2)}) collective-permute-start(bf16[544,256]{1,0:T(8,128)(2,1)S(1)} %slice.15), channel_id=1, source_target_pairs={{0,2},{1,3},{2,0},{3,1},{4,6},{5,7},{6,4},{7,5},{8,10},{9,11},{10,... | collective-permute-start | bytes 835592 | tf_op jit(solution)/shard_map/ppermute | solution.py:402
  9.0 5.3 %collective-permute-start = (bf16[128,256]{1,0:T(8,128)(2,1)S(1)}, bf16[128,256]{1,0:T(8,128)(2,1)S(1)}, u32[]{:S(2)}, u32[]{:S(2)}) collective-permute-start(bf16[128,256]{1,0:T(8,128)(2,1)S(1)} %get-tuple-element.59), channel_id=1, source_target_pairs={{0,4},{4,0},{1,5},{5,1},{2,6},{6,2},{3,7},{7,3},{8,12},{12,8},{9,1... | collective-permute-start | bytes 196616 | tf_op jit(solution)/shard_map/ppermute | solution.py:402
  10.5 4.0 %collective-permute-start.1 = (bf16[128,256]{1,0:T(8,128)(2,1)S(1)}, bf16[128,256]{1,0:T(8,128)(2,1)S(1)}, u32[]{:S(2)}, u32[]{:S(2)}) collective-permute-start(bf16[128,256]{1,0:T(8,128)(2,1)S(1)} %get-tuple-element.59), channel_id=1, source_target_pairs={{4,8},{12,16},{20,24},{28,32},{36,40},{44,48},{52,56},{60,64},{68,... | collective-permute-start | bytes 196616 | tf_op jit(solution)/shard_map/ppermute | solution.py:446
  21.8 6.4 %collective-permute-start.5 = (bf16[512,256]{1,0:T(8,128)(2,1)S(1)}, bf16[512,256]{1,0:T(8,128)(2,1)S(1)}, u32[]{:S(2)}, u32[]{:S(2)}) collective-permute-start(bf16[512,256]{1,0:T(8,128)(2,1)S(1)} %get-tuple-element.65.p0), channel_id=1, source_target_pairs={{0,1},{1,2},{2,3},{3,0},{4,5},{5,6},{6,7},{7,4},{8,9},{9,10},{10,1... | collective-permute-start | bytes 786440 | tf_op jit(solution)/shard_map/ppermute | solution.py:402
  22.3 6.0 %collective-permute-start.6 = (bf16[512,256]{1,0:T(8,128)(2,1)S(1)}, bf16[512,256]{1,0:T(8,128)(2,1)S(1)}, u32[]{:S(2)}, u32[]{:S(2)}) collective-permute-start(bf16[512,256]{1,0:T(8,128)(2,1)S(1)} %get-tuple-element.65.p0), channel_id=1, source_target_pairs={{0,3},{1,0},{2,1},{3,2},{4,7},{5,4},{6,5},{7,6},{8,11},{9,8},{10,9... | collective-permute-start | bytes 786440 | tf_op jit(solution)/shard_map/ppermute | solution.py:402
  28.2 6.7 %collective-permute-start.7 = (bf16[256,256]{1,0:T(8,128)(2,1)S(1)}, bf16[256,256]{1,0:T(8,128)(2,1)S(1)}, u32[]{:S(2)}, u32[]{:S(2)}) collective-permute-start(bf16[256,256]{1,0:T(8,128)(2,1)S(1)} %slice.20), channel_id=1, source_target_pairs={{0,1},{1,2},{2,3},{3,0},{4,5},{5,6},{6,7},{7,4},{8,9},{9,10},{10,1... | collective-permute-start | bytes 393224 | tf_op jit(solution)/shard_map/ppermute | solution.py:402
  28.4 6.6 %collective-permute-start.8 = (bf16[256,256]{1,0:T(8,128)(2,1)S(1)}, bf16[256,256]{1,0:T(8,128)(2,1)S(1)}, u32[]{:S(2)}, u32[]{:S(2)}) collective-permute-start(bf16[256,256]{1,0:T(8,128)(2,1)S(1)} %slice.21), channel_id=1, source_target_pairs={{0,3},{1,0},{2,1},{3,2},{4,7},{5,4},{6,5},{7,6},{8,11},{9,8},{10,9... | collective-permute-start | bytes 393224 | tf_op jit(solution)/shard_map/ppermute | solution.py:402
  55.9 9.1 %collective-permute-start.9 = (bf16[2176,128]{1,0:T(8,128)(2,1)S(1)}, bf16[2176,128]{1,0:T(8,128)(2,1)S(1)}, u32[]{:S(2)}, u32[]{:S(2)}) collective-permute-start(bf16[2176,128]{1,0:T(8,128)(2,1)S(1)} %get-tuple-element.80), channel_id=1, source_target_pairs={{0,4},{4,0},{1,5},{5,1},{2,6},{6,2},{3,7},{7,3},{8,12},{12,8},{9,1... | collective-permute-start | bytes 1671176 | tf_op jit(solution)/shard_map/ppermute | solution.py:402
  65.7 10.5 %collective-permute-start.10 = (bf16[640,128]{1,0:T(8,128)(2,1)S(1)}, bf16[640,128]{1,0:T(8,128)(2,1)S(1)}, u32[]{:S(2)}, u32[]{:S(2)}) collective-permute-start(bf16[640,128]{1,0:T(8,128)(2,1)S(1)} %get-tuple-element.84), channel_id=1, source_target_pairs={{0,1},{1,2},{2,3},{3,0},{4,5},{5,6},{6,7},{7,4},{8,9},{9,10},{10,1... | collective-permute-start | bytes 491528 | tf_op jit(solution)/shard_map/ppermute | solution.py:402
  65.8 10.5 %collective-permute-start.12 = (bf16[640,128]{1,0:T(8,128)(2,1)S(1)}, bf16[640,128]{1,0:T(8,128)(2,1)S(1)}, u32[]{:S(2)}, u32[]{:S(2)}) collective-permute-start(bf16[640,128]{1,0:T(8,128)(2,1)S(1)} %get-tuple-element.86), channel_id=1, source_target_pairs={{0,3},{1,0},{2,1},{3,2},{4,7},{5,4},{6,5},{7,6},{8,11},{9,8},{10,9... | collective-permute-start | bytes 491528 | tf_op jit(solution)/shard_map/ppermute | solution.py:402
  69.1 7.2 %collective-permute-start.11 = (bf16[384,128]{1,0:T(8,128)(2,1)S(1)}, bf16[384,128]{1,0:T(8,128)(2,1)S(1)}, u32[]{:S(2)}, u32[]{:S(2)}) collective-permute-start(bf16[384,128]{1,0:T(8,128)(2,1)S(1)} %get-tuple-element.85), channel_id=1, source_target_pairs={{0,2},{1,3},{2,0},{3,1},{4,6},{5,7},{6,4},{7,5},{8,10},{9,11},{10,... | collective-permute-start | bytes 294920 | tf_op jit(solution)/shard_map/ppermute | solution.py:402
  70.2 6.2 %collective-permute-start.13 = (bf16[128,256]{1,0:T(8,128)(2,1)S(1)}, bf16[128,256]{1,0:T(8,128)(2,1)S(1)}, u32[]{:S(2)}, u32[]{:S(2)}) collective-permute-start(bf16[128,256]{1,0:T(8,128)(2,1)S(1)} %get-tuple-element.88), channel_id=1, source_target_pairs={{4,8},{12,16},{20,24},{28,32},{36,40},{44,48},{52,56},{60,64},{68,... | collective-permute-start | bytes 196616 | tf_op jit(solution)/shard_map/ppermute | solution.py:524
  112.6 4.4 %collective-permute-start.14 = (bf16[64,48,128]{2,1,0:T(8,128)(2,1)S(1)}, bf16[64,48,128]{2,1,0:T(8,128)(2,1)S(1)}, u32[]{:S(2)}, u32[]{:S(2)}) collective-permute-start(bf16[64,48,128]{2,1,0:T(8,128)(2,1)S(1)} %all_to_all.11.mine_ref), channel_id=1, source_target_pairs={{0,4},{4,0},{1,5},{5,1},{2,6},{6,2},{3,7},{7,3},{8,12},{12,8},{9,1... | collective-permute-start | bytes 2359304 | tf_op jit(solution)/shard_map/ppermute | solution.py:402

commit v4 on v3

--- a/solution.py
+++ b/solution.py
@@ -75,24 +75,39 @@
     return (preact * sig).astype(BF), sig * (1.0 + preact * (1.0 - sig))
 
 
+def split_count(count):
+    many = jnp.floor(count * (1.0 / 256.0)) * 256.0
+    upper = lax.broadcasted_iota(jnp.int32, count.shape, 0) < 8
+    return jnp.where(upper, many, count - many).astype(BF)
+
+
+def whole_count(rows):
+    rows = rows.astype(F32)
+    parts = [rows[at : at + 1, :] + rows[at + 8 : at + 9, :] for at in (0, 16)]
+    return jnp.concatenate(parts, axis=1)
+
+
 def start_kernel(
     own_ref, export_ref, cot_ref, assign_ref, dst_ref, place_ref, rim_ref, pack_ref, target_ref
 ):
-    rim_count = export_ref.shape[1]
-    rim = dot(pick_matrix(export_ref[...], own_ref.shape[0]), own_ref[...]).astype(BF)
-    rim_ref[...] = rim
-    pack_ref[0:rim_count, :] = rim
+    rim_ref[...] = dot(pick_matrix(export_ref[...], own_ref.shape[0]), own_ref[...]).astype(BF)
     pool = sum_matrix(assign_ref[...], CNODE)
-    pack_ref[rim_count : rim_count + CNODE, :] = dot(pool, cot_ref[...]).astype(BF)
-    count = dot_rt(jnp.ones((16, pool.shape[1]), BF), pool)
-    coarse_part = jnp.floor(count * (1.0 / 256.0)) * 256.0
-    upper = lax.broadcasted_iota(jnp.int32, count.shape, 0) < 8
-    packed = jnp.where(upper, coarse_part, count - coarse_part).astype(BF)
-    at = rim_count + CNODE
-    pack_ref[at : at + 16, :] = packed[:, :256]
-    pack_ref[at + 16 : at + 32, :] = packed[:, 256:]
+    pack_ref[0:CNODE, :] = dot(pool, cot_ref[...]).astype(BF)
+    packed = split_count(dot_rt(jnp.ones((16, pool.shape[1]), BF), pool))
+    pack_ref[CNODE : CNODE + 16, :] = packed[:, :256]
+    pack_ref[CNODE + 16 : CNODE + 32, :] = packed[:, 256:]
     slot = lax.broadcasted_iota(jnp.int32, dst_ref.shape, 1)
     target_ref[...] = jnp.where(slot < place_ref[2], dst_ref[...], -1)
+
+
+def add_kernel(mine_ref, got_ref, out_ref):
+    out_ref[0:CNODE, :] = (
+        mine_ref[0:CNODE, :].astype(F32) + got_ref[0:CNODE, :].astype(F32)
+    ).astype(BF)
+    count = whole_count(mine_ref[CNODE:, :]) + whole_count(got_ref[CNODE:, :])
+    packed = split_count(jnp.broadcast_to(count, (16, CNODE)))
+    out_ref[CNODE : CNODE + 16, :] = packed[:, :256]
+    out_ref[CNODE + 16 : CNODE + 32, :] = packed[:, 256:]
 
 
 def own_kernel(own_ref, src_ref, target_ref, w1_ref, part_ref):
@@ -115,8 +130,8 @@
     table[pl.ds(pl.multiple_of(nodes + rim * (1 - core), rim), rim), :] = ra[...]
     beyond = rb[...].astype(F32) * jnp.where(place_ref[3] > 0, 1.0, 0.0)
     table[pl.ds(pl.multiple_of(nodes + rim * core, rim), rim), :] = beyond.astype(BF)
-    west = rw[0:rim, :].astype(F32) * jnp.where(col > 0, 1.0, 0.0)
-    east = re[0:rim, :].astype(F32) * jnp.where(col < 3, 1.0, 0.0)
+    west = rw[...].astype(F32) * jnp.where(col > 0, 1.0, 0.0)
+    east = re[...].astype(F32) * jnp.where(col < 3, 1.0, 0.0)
     table[nodes + 2 * rim : nodes + 3 * rim, :] = west.astype(BF)
     table[nodes + 3 * rim :, :] = east.astype(BF)
     for at in range(0, src_ref.shape[1], CHUNK):
@@ -143,22 +158,14 @@
 
 
 def coarse_kernel(
-    p0, p1, p2, p3, p4, g0, g1, g2, g3, src_ref, dst_ref, w1_ref, w2_ref, gain_ref, cot_ref,
+    p0, p1, p2, p3, p4, g0, g1, src_ref, dst_ref, w1_ref, w2_ref, gain_ref, cot_ref,
     assign_ref, place_ref, grad_fine_ref, pack_ref,
     table, slope, pick_t, sum_t, acc, by_src, by_dst,
 ):
     feature = p0.shape[1]
     edges = src_ref.shape[1]
-    grads = []
-    count = None
-    for ref in (g0, g1, g2, g3):
-        skip = ref.shape[0] - CNODE - 32
-        grads.append(ref[skip : skip + CNODE, :].astype(F32))
-        tail = ref[skip + CNODE :, :].astype(F32)
-        tail = [tail[at : at + 1, :] + tail[at + 8 : at + 9, :] for at in (0, 16)]
-        tail = jnp.concatenate(tail, axis=1)
-        count = tail if count is None else count + tail
-    grad_c1 = (grads[0] + grads[1]) + (grads[2] + grads[3])
+    grad_c1 = g0[0:CNODE, :].astype(F32) + g1[0:CNODE, :].astype(F32)
+    count = whole_count(g0[CNODE:, :]) + whole_count(g1[CNODE:, :])
     weight = spread_row(1.0 / jnp.maximum(count, 1.0))
     weight = jnp.concatenate([weight] * (feature // 128), axis=1)
     across = jnp.concatenate([p3[...].astype(F32), p4[...].astype(F32)], axis=0)
@@ -344,7 +351,7 @@
             self.copy = None
 
 
-def run(kernel, outs, operands, scratch=(), scalars=(), late=(), inner=(), ahead=(), limit=16):
+def run(kernel, outs, operands, scratch=(), scalars=(), late=(), inner=(), ahead=(), limit=16, work=0.1):
     size = sum(math.prod(x.shape) * x.dtype.itemsize for x in [*operands, *ahead]) + sum(
         math.prod(shape) * jnp.dtype(kind).itemsize for shape, kind in outs
     )
@@ -388,7 +395,9 @@
         + [pltpu.VMEM(operands[i].shape, operands[i].dtype) for i in late]
         + ([pltpu.SemaphoreType.DMA((copies,))] if copies else []),
         compiler_params=pltpu.CompilerParams(vmem_limit_bytes=limit * 1024 * 1024),
-        cost_estimate=pl.CostEstimate(flops=0, bytes_accessed=size, transcendentals=0),
+        cost_estimate=pl.CostEstimate(
+            flops=int(2e9 * work), bytes_accessed=size, transcendentals=0
+        ),
     )(*operands)
 
 
@@ -433,7 +442,7 @@
         start_kernel,
         [
             ((rim_count, feature), BF),
-            ((rim_count + CNODE + 32, feature), BF),
+            ((CNODE + 32, feature), BF),
             ((1, edges), jnp.int32),
         ],
         [own, export, cot, assign, dst, place],
@@ -442,9 +451,11 @@
         inner=(0, 1, 2),
         ahead=[own, src, fine_w1, fine_w2, fine_gain, assign, export],
     )
+    near, far = [(0, 1), (1, 0), (2, 3), (3, 2)], [(1, 2), (2, 1), (3, 0), (0, 3)]
+    pack_got = lax.ppermute(pack, "x", near)
+    from_west, from_east = send(rim, "x", 1), send(rim, "x", 3)
     from_a = send(rim, "core", 1)
     from_b = lax.ppermute(rim, ROW, between)
-    packs = [pack, send(pack, "x", 1), send(pack, "x", 3), send(pack[rim_count:], "x", 2)]
     part, csrc_in, cdst_in, cw1_in, cw2_in, cgain_in, cot_in = run(
         own_kernel,
         [((edges, hidden), F32)],
@@ -452,7 +463,12 @@
         inner=(0,),
         ahead=[coarse_src, coarse_dst, coarse_w1, coarse_w2, coarse_gain, cot],
         limit=LIMITS[0],
-    )
+        work=1.1,
+    )
+    pack, pack_got, part = lax.optimization_barrier((pack, pack_got, part))
+    (pair,) = run(add_kernel, [((CNODE + 32, feature), BF)], [pack, pack_got], inner=(0,))
+    pair, part = lax.optimization_barrier((pair, part))
+    pair_got = lax.ppermute(pair, "x", far)
     slope, acc, summed, pooled, table = run(
         fine_forward_kernel,
         [
@@ -463,16 +479,17 @@
             ((nodes + 4 * rim_count, feature), BF),
         ],
         [
-            part, own_in, from_a, from_b, packs[1], packs[2], src_in, target, place,
+            part, own_in, from_a, from_b, from_west, from_east, src_in, target, place,
             w1_in, w2_in, gain_in, assign_in,
         ],
         [((nodes, hidden), F32)],
         scalars=(8,),
         inner=(0, 1, 2, 3, 4),
         limit=LIMITS[1],
+        work=1.6,
     )
     half_rows = CNODE // 2
-    pooled, packs[3] = lax.optimization_barrier((pooled, packs[3]))
+    pooled, pair_got = lax.optimization_barrier((pooled, pair_got))
     left, right = send(pooled, "x", 1), send(pooled, "x", 3)
     across = [send(left[:half_rows], "x", 1), send(right[half_rows:], "x", 3)]
 
@@ -480,7 +497,7 @@
         coarse_kernel,
         [((nodes, feature), F32), ((2, 384, 128), F32)],
         [
-            pooled, left, right, *across, *packs, csrc_in, cdst_in, cw1_in, cw2_in, cgain_in,
+            pooled, left, right, *across, pair, pair_got, csrc_in, cdst_in, cw1_in, cw2_in, cgain_in,
             cot_in, assign_in, place,
         ],
         [
@@ -492,9 +509,10 @@
             ((CNODE, hidden), F32),
             ((CNODE, hidden), F32),
         ],
-        scalars=(16,),
+        scalars=(14,),
         inner=(0, 1),
         limit=LIMITS[2],
+        work=5.0,
     )
 
     local, give, keep, ghost_b, ghost_w, ghost_e = run(
@@ -519,6 +537,7 @@
         scalars=(7,),
         inner=(0, 1, 2, 3, 4, 5),
         limit=LIMITS[3],
+        work=2.8,
     )
     from_core = send(give, "core", 1)
     from_b = lax.ppermute(ghost_b, ROW, between)

time: 120 us -> 115 us (0.958)
  blocking collectives: 36.1 us -> 28.6 us
  waiting for transfers between devices: 15.4 us -> 18.1 us
    all_to_all x1, blocking collectives: 15.4 us -> 9.78 us  [shards(): both = lax.all_to_all(both, PLANE, 0, 0, tiled=True)]
    ppermute x0 -> x2, starting transfers between devices: none -> 3.52 us  [the longest x1 2.12 us: shards(): pack_got = lax.ppermute(pack, 'x', near)]
    ppermute x1, starting transfers between devices: 2.23 us -> 0.01 us  [shards(): from_b = lax.ppermute(ghost_b, ROW, between)]
    ppermute x13 -> x12, waiting for transfers between devices: 15.3 us -> 17.2 us  [send(): lax.ppermute(value, axis, [(i, (i + step) % size) for i in range(size)])]
    all_to_all x1, blocking collectives: 20.7 us -> 18.8 us  [shards(): mine = lax.all_to_all(copies, CHIPS, 0, 0, tiled=True)]
    ppermute x13 -> x12, starting transfers between devices: 26.9 us -> 25.9 us  [send(): lax.ppermute(value, axis, [(i, (i + step) % size) for i in range(size)])]
    pallas_call x8 -> x9, Pallas kernels: 35.9 us -> 36 us  [run(): pl.pallas_call(body if copies else kernel, out_shape=shapes, in_specs=[pl...]
  transfers between devices with their start and end apart: 15 -> 16, of which waited for: 7 -> 6; matrix products, arithmetic and copies ran while one was open for 0% -> 0% of each run, Pallas kernels for 8% -> 8%
where the time goes in v4:
time: 115 us
  Pallas kernels  36 us (31%)
  starting transfers between devices  30.6 us (27%)
  blocking collectives  28.6 us (25%)
  waiting for transfers between devices  18.1 us (16%)
  between operations  1.43 us (1%)
    pallas_call x9, Pallas kernels, run(): pl.pallas_call(body if copies else kernel, out_shape=shapes, in_specs=[pl...  36 us
    ppermute x12, starting transfers between devices, send(): lax.ppermute(value, axis, [(i, (i + step) % size) for i in range(size)])  25.9 us
    all_to_all x1, blocking collectives, shards(): mine = lax.all_to_all(copies, CHIPS, 0, 0, tiled=True)  18.8 us
    ppermute x12, waiting for transfers between devices, send(): lax.ppermute(value, axis, [(i, (i + step) % size) for i in range(size)])  17.2 us
    all_to_all x1, blocking collectives, shards(): both = lax.all_to_all(both, PLANE, 0, 0, tiled=True)  9.78 us
  transfers between devices with their start and end apart: 16, of which 6 were waited for; matrix products, arithmetic and copies ran while one was open for 0% of the time, Pallas kernels for 8%

profile of v4, /device:TPU:1, one launch (start us, length us, event | category | flops | bytes accessed | tf_op | source)
XLA Modules:
  0.0 115.1 jit_solution(3761026398984954448)
XLA Ops:
  1.3 0.1 pad_add_fusion.refs_5_.place_ref
  1.4 2.4 %shard_map.182 = (bf16[128,256]{1,0:T(8,128)(2,1)S(1)}, bf16[544,256]{1,0:T(8,128)(2,1)S(1)}, s32[1,2048]{1,0:T(1,128)S(1)}, bf16[512,256]{1,0:T(8,128)(2,1)S(1)...) custom-call(bf16[512,256]{1,0:T(8,128)(2,1)} %bitcast.15, ...), custom_call_target="tpu_custom_call" | custom-call | flops 200000000 | bytes 1947664 | tf_op jit(solution)/shard_map/pallas_call | solution.py:389
  3.8 2.1 %collective-permute-start = (bf16[544,256]{1,0:T(8,128)(2,1)S(1)}, bf16[544,256]{1,0:T(8,128)(2,1)S(1)}, u32[]{:S(2)}, u32[]{:S(2)}) collective-permute-start(bf16[544,256]{1,0:T(8,128)(2,1)S(1)} %get-tuple-element.65.mine_ref), channel_id=1, source_target_pairs={{0,1},{1,0},{2,3},{3,2},{4,5},{5,4},{6,7},{7,6},{8,9},{9,8},{10,11... | collective-permute-start | bytes 835592 | tf_op jit(solution)/shard_map/ppermute | solution.py:455
  5.9 1.0 collective-permute-start.1
  6.9 1.2 %collective-permute-start.2 = (bf16[128,256]{1,0:T(8,128)(2,1)S(1)}, bf16[128,256]{1,0:T(8,128)(2,1)S(1)}, u32[]{:S(2)}, u32[]{:S(2)}) collective-permute-start(bf16[128,256]{1,0:T(8,128)(2,1)S(1)} %get-tuple-element.69), channel_id=1, source_target_pairs={{4,8},{12,16},{20,24},{28,32},{36,40},{44,48},{52,56},{60,64},{68,... | collective-permute-start | bytes 196616 | tf_op jit(solution)/shard_map/ppermute | solution.py:458
  8.1 0.3 collective-permute-start.3
  8.3 2.4 %collective-permute-start.4 = (bf16[128,256]{1,0:T(8,128)(2,1)S(1)}, bf16[128,256]{1,0:T(8,128)(2,1)S(1)}, u32[]{:S(2)}, u32[]{:S(2)}) collective-permute-start(bf16[128,256]{1,0:T(8,128)(2,1)S(1)} %get-tuple-element.69), channel_id=1, source_target_pairs={{0,3},{1,0},{2,1},{3,2},{4,7},{5,4},{6,5},{7,6},{8,11},{9,8},{10,9... | collective-permute-start | bytes 196616 | tf_op jit(solution)/shard_map/ppermute | solution.py:411
  10.7 2.6 %shard_map.183 = (f32[2048,512]{1,0:T(8,128)S(1)}, s32[1,3072]{1,0:T(1,128)S(1)}, s32[1,3072]{1,0:T(1,128)S(1)}, bf16[512,512]{1,0:T(8,128)(2,1)S(1)}, bf16[512,...) custom-call(bf16[512,256]{1,0:T(8,128)(2,1)S(1)} %get-tuple-element.60.refs_0_.own_ref, ...), custom_call_target="tpu_custom_call" | custom-call | flops 2200000000 | bytes 6071296 | tf_op jit(solution)/shard_map/pallas_call | solution.py:389
  13.4 0.0 collective-permute-done.got_ref
  13.4 0.1 shard_map.184.g0
  13.5 1.4 %collective-permute-start.5 = (bf16[544,256]{1,0:T(8,128)(2,1)S(1)}, bf16[544,256]{1,0:T(8,128)(2,1)S(1)}, u32[]{:S(2)}, u32[]{:S(2)}) collective-permute-start(bf16[544,256]{1,0:T(8,128)(2,1)S(1)} %shard_map.184.g0), channel_id=1, source_target_pairs={{1,2},{2,1},{3,0},{0,3},{5,6},{6,5},{7,4},{4,7},{9,10},{10,9},{11,... | collective-permute-start | bytes 835592 | tf_op jit(solution)/shard_map/ppermute | solution.py:471
  14.9 0.0 collective-permute-done.1.ra
  14.9 0.0 collective-permute-done.2.rb
  14.9 0.0 collective-permute-done.3.rw
  14.9 0.0 collective-permute-done.4.re
  14.9 5.1 %shard_map.185 = (f32[2048,512]{1,0:T(8,128)S(1)}, bf16[512,512]{1,0:T(8,128)(2,1)S(1)}, f32[512,256]{1,0:T(8,128)S(1)}, bf16[512,256]{1,0:T(8,128)(2,1)S(1)}, bf16[1024,256]{1,0:T(8,128)(2,1)S(1)}) custom-call(f32[2048,512]{1,0:T(8,128)S(1)} %get-tuple-element.68.part_ref, bf16[512,256]{1,0:T(8,128)(2,1)S(1)} %get-tuple-element.60.refs_0_.own_ref, ...), custom_call_target="tpu_custom_call" | custom-call | flops 3200000000 | bytes 11553808 | tf_op jit(solution)/shard_map/pallas_call | solution.py:389
  20.1 0.8 collective-permute-done.5.g1
  20.9 0.0 collective-permute-start.6
  20.9 2.7 %collective-permute-start.7 = (bf16[512,256]{1,0:T(8,128)(2,1)S(1)}, bf16[512,256]{1,0:T(8,128)(2,1)S(1)}, u32[]{:S(2)}, u32[]{:S(2)}) collective-permute-start(bf16[512,256]{1,0:T(8,128)(2,1)S(1)} %get-tuple-element.75.p0), channel_id=1, source_target_pairs={{0,3},{1,0},{2,1},{3,2},{4,7},{5,4},{6,5},{7,6},{8,11},{9,8},{10,9... | collective-permute-start | bytes 786440 | tf_op jit(solution)/shard_map/ppermute | solution.py:411
  23.5 5.9 %collective-permute-done.6.p1 = bf16[512,256]{1,0:T(8,128)(2,1)S(1)} collective-permute-done((bf16[512,256]{1,0:T(8,128)(2,1)S(1)}, bf16[512,256]{1,0:T(8,128)(2,1)S(1)}, u32[]{:S(2)}, u32[]{:S(2)}) %collective-permute-start.6) | collective-permute-done | bytes 262176 | tf_op jit(solution)/shard_map/ppermute | solution.py:411
  29.4 0.1 collective-permute-start.8
  29.5 0.0 collective-permute-done.7.p2
  29.5 2.9 %collective-permute-start.9 = (bf16[256,256]{1,0:T(8,128)(2,1)S(1)}, bf16[256,256]{1,0:T(8,128)(2,1)S(1)}, u32[]{:S(2)}, u32[]{:S(2)}) collective-permute-start(bf16[256,256]{1,0:T(8,128)(2,1)S(1)} %slice.17), channel_id=1, source_target_pairs={{0,3},{1,0},{2,1},{3,2},{4,7},{5,4},{6,5},{7,6},{8,11},{9,8},{10,9... | collective-permute-start | bytes 393224 | tf_op jit(solution)/shard_map/ppermute | solution.py:411
  32.4 3.5 %collective-permute-done.8.p3 = bf16[256,256]{1,0:T(8,128)(2,1)S(1)} collective-permute-done((bf16[256,256]{1,0:T(8,128)(2,1)S(1)}, bf16[256,256]{1,0:T(8,128)(2,1)S(1)}, u32[]{:S(2)}, u32[]{:S(2)}) %collective-permute-start.8) | collective-permute-done | bytes 131104 | tf_op jit(solution)/shard_map/ppermute | solution.py:411
  35.9 0.0 collective-permute-done.9.p4
  35.9 14.0 %shard_map.186 = (f32[512,256]{1,0:T(8,128)S(1)}, f32[2,384,128]{2,1,0:T(8,128)S(1)}) custom-call(bf16[512,256]{1,0:T(8,128)(2,1)S(1)} %get-tuple-element.75.p0, bf16[512,256]{1,0:T(8,128)(2,1)S(1)} %collective-permute-done.6.p1, bf16[512,256]{1,0:T(8,128)(2,1)S(1)} %collective-permute-done.7.p2, bf16[256,256]{1,0:T(8,128)(2,1)S(1)} %collective-permute-done.8.p3, ...), custom_call_target="tpu_custom_call" | custom-call | flops 10000000000 | bytes 3599376 | tf_op jit(solution)/shard_map/pallas_call | solution.py:389
  49.9 6.9 %shard_map.187 = (f32[512,256]{1,0:T(8,128)S(1)}, bf16[2176,128]{1,0:T(8,128)(2,1)S(1)}, f32[1920,128]{1,0:T(8,128)S(1)}, bf16[128,256]{1,0:T(8,128)(2,1)S(1)}, ...) custom-call(f32[512,256]{1,0:T(8,128)S(1)} %get-tuple-element.83.grad_fine_ref, ...), custom_call_target="tpu_custom_call" | custom-call | flops 5600000000 | bytes 9749520 | tf_op jit(solution)/shard_map/pallas_call | solution.py:389
  56.8 8.5 %collective-permute-start.10 = (bf16[2176,128]{1,0:T(8,128)(2,1)S(1)}, bf16[2176,128]{1,0:T(8,128)(2,1)S(1)}, u32[]{:S(2)}, u32[]{:S(2)}) collective-permute-start(bf16[2176,128]{1,0:T(8,128)(2,1)S(1)} %get-tuple-element.90), channel_id=1, source_target_pairs={{0,4},{4,0},{1,5},{5,1},{2,6},{6,2},{3,7},{7,3},{8,12},{12,8},{9,1... | collective-permute-start | bytes 1671176 | tf_op jit(solution)/shard_map/ppermute | solution.py:411
  65.3 1.6 %collective-permute-done.10.got_ref.from_core = bf16[2176,128]{1,0:T(8,128)(2,1)S(1)} collective-permute-done((bf16[2176,128]{1,0:T(8,128)(2,1)S(1)}, bf16[2176,128]{1,0:T(8,128)(2,1)S(1)}, u32[]{:S(2)}, u32[]{:S(2)}) %collective-permute-start.10) | collective-permute-done | bytes 557088 | tf_op jit(solution)/shard_map/ppermute | solution.py:411
  66.9 0.7 shard_map.188
  67.5 0.1 collective-permute-start.11
  67.6 3.3 %collective-permute-start.13 = (bf16[640,128]{1,0:T(8,128)(2,1)S(1)}, bf16[640,128]{1,0:T(8,128)(2,1)S(1)}, u32[]{:S(2)}, u32[]{:S(2)}) collective-permute-start(bf16[640,128]{1,0:T(8,128)(2,1)S(1)} %get-tuple-element.96), channel_id=1, source_target_pairs={{0,3},{1,0},{2,1},{3,2},{4,7},{5,4},{6,5},{7,6},{8,11},{9,8},{10,9... | collective-permute-start | bytes 491528 | tf_op jit(solution)/shard_map/ppermute | solution.py:411
  70.9 1.1 collective-permute-start.12
  72.0 0.0 collective-permute-start.14
  72.0 6.0 %collective-permute-done.12 = bf16[384,128]{1,0:T(8,128)(2,1)S(1)} collective-permute-done((bf16[384,128]{1,0:T(8,128)(2,1)S(1)}, bf16[384,128]{1,0:T(8,128)(2,1)S(1)}, u32[]{:S(2)}, u32[]{:S(2)}) %collective-permute-start.12) | collective-permute-done | bytes 98336 | tf_op jit(solution)/shard_map/ppermute | solution.py:411
  78.1 0.0 collective-permute-done.11.from_west
  78.1 0.0 collective-permute-done.13.from_east
  78.1 0.1 add_convert_fusion
  78.2 0.0 collective-permute-done.14.from_b
  78.2 9.8 %all_to_all.10 = bf16[16,48,128]{2,1,0:T(8,128)(2,1)S(1)} all-to-all(bf16[16,48,128]{2,1,0:T(8,128)(2,1)S(1)} %pad_maximum_fusion), channel_id=1, replica_groups=mesh['z'=4,'y'=4,'core'=2,'x'=4] {'z','y'}, dimensions={0} | all-to-all | bytes 393216 | tf_op jit(solution)/shard_map/all_to_all | solution.py:570
  88.0 0.1 broadcast_in_dim.17
  88.1 18.8 %all_to_all.11.mine_ref = bf16[64,48,128]{2,1,0:T(8,128)(2,1)S(1)} all-to-all(bf16[64,48,128]{2,1,0:T(8,128)(2,1)S(1)} %broadcast_in_dim.17), channel_id=1, replica_groups=mesh['z'=4,'y'=4,'core'=2,'x'=4] {'z','y','x'}, dimensions={0} | all-to-all | bytes 1572864 | tf_op jit(solution)/shard_map/all_to_all | solution.py:573
  107.0 3.7 %collective-permute-start.15 = (bf16[64,48,128]{2,1,0:T(8,128)(2,1)S(1)}, bf16[64,48,128]{2,1,0:T(8,128)(2,1)S(1)}, u32[]{:S(2)}, u32[]{:S(2)}) collective-permute-start(bf16[64,48,128]{2,1,0:T(8,128)(2,1)S(1)} %all_to_all.11.mine_ref), channel_id=1, source_target_pairs={{0,4},{4,0},{1,5},{5,1},{2,6},{6,2},{3,7},{7,3},{8,12},{12,8},{9,1... | collective-permute-start | bytes 2359304 | tf_op jit(solution)/shard_map/ppermute | solution.py:411
  110.7 1.7 %shard_map.189 = f32[512,256]{1,0:T(8,128)} custom-call(f32[512,256]{1,0:T(8,128)S(1)} %get-tuple-element.101.local_ref, bf16[2176,128]{1,0:T(8,128)(2,1)S(1)} %collective-permute-done.10.got_ref.from_core, bf16[128,256]{1,0:T(8,128)(2,1)S(1)} %collective-permute-done.14.from_b, bf16[640,128]{1,0:T(8,128)(2,1)S(1)} %collective-permute-done.11.from_west, ...), custom_call_target="tpu_custom_call" | custom-call | flops 200000000 | bytes 1999376 | tf_op jit(solution)/shard_map/pallas_call | solution.py:389
  112.3 0.3 collective-permute-done.15.other_ref
  112.6 2.5 %shard_map.190 = (f32[512,512]{1,0:T(8,128)}, f32[512,256]{1,0:T(8,128)}, f32[512,512]{1,0:T(8,128)}, f32[512,256]{1,0:T(8,128)}) custom-call(bf16[64,48,128]{2,1,0:T(8,128)(2,1)S(1)} %all_to_all.11.mine_ref, bf16[64,48,128]{2,1,0:T(8,128)(2,1)S(1)} %collective-permute-done.15.other_ref, s32[4]{0:T(128)S(1)} %pad_add_fusion.refs_5_.place_ref), custom_call_target="tpu_custom_call" | custom-call | flops 200000000 | bytes 4718608 | tf_op jit(solution)/shard_map/pallas_call | solution.py:389
  (5 shorter events, 0.1 us)
Async XLA Ops:
  3.8 9.6 %collective-permute-start = (bf16[544,256]{1,0:T(8,128)(2,1)S(1)}, bf16[544,256]{1,0:T(8,128)(2,1)S(1)}, u32[]{:S(2)}, u32[]{:S(2)}) collective-permute-start(bf16[544,256]{1,0:T(8,128)(2,1)S(1)} %get-tuple-element.65.mine_ref), channel_id=1, source_target_pairs={{0,1},{1,0},{2,3},{3,2},{4,5},{5,4},{6,7},{7,6},{8,9},{9,8},{10,11... | collective-permute-start | bytes 835592 | tf_op jit(solution)/shard_map/ppermute | solution.py:455
  5.9 9.0 %collective-permute-start.1 = (bf16[128,256]{1,0:T(8,128)(2,1)S(1)}, bf16[128,256]{1,0:T(8,128)(2,1)S(1)}, u32[]{:S(2)}, u32[]{:S(2)}) collective-permute-start(bf16[128,256]{1,0:T(8,128)(2,1)S(1)} %get-tuple-element.69), channel_id=1, source_target_pairs={{0,4},{4,0},{1,5},{5,1},{2,6},{6,2},{3,7},{7,3},{8,12},{12,8},{9,1... | collective-permute-start | bytes 196616 | tf_op jit(solution)/shard_map/ppermute | solution.py:411
  6.9 8.0 %collective-permute-start.2 = (bf16[128,256]{1,0:T(8,128)(2,1)S(1)}, bf16[128,256]{1,0:T(8,128)(2,1)S(1)}, u32[]{:S(2)}, u32[]{:S(2)}) collective-permute-start(bf16[128,256]{1,0:T(8,128)(2,1)S(1)} %get-tuple-element.69), channel_id=1, source_target_pairs={{4,8},{12,16},{20,24},{28,32},{36,40},{44,48},{52,56},{60,64},{68,... | collective-permute-start | bytes 196616 | tf_op jit(solution)/shard_map/ppermute | solution.py:458
  8.1 6.8 %collective-permute-start.3 = (bf16[128,256]{1,0:T(8,128)(2,1)S(1)}, bf16[128,256]{1,0:T(8,128)(2,1)S(1)}, u32[]{:S(2)}, u32[]{:S(2)}) collective-permute-start(bf16[128,256]{1,0:T(8,128)(2,1)S(1)} %get-tuple-element.69), channel_id=1, source_target_pairs={{0,1},{1,2},{2,3},{3,0},{4,5},{5,6},{6,7},{7,4},{8,9},{9,10},{10,1... | collective-permute-start | bytes 196616 | tf_op jit(solution)/shard_map/ppermute | solution.py:411
  8.3 6.6 %collective-permute-start.4 = (bf16[128,256]{1,0:T(8,128)(2,1)S(1)}, bf16[128,256]{1,0:T(8,128)(2,1)S(1)}, u32[]{:S(2)}, u32[]{:S(2)}) collective-permute-start(bf16[128,256]{1,0:T(8,128)(2,1)S(1)} %get-tuple-element.69), channel_id=1, source_target_pairs={{0,3},{1,0},{2,1},{3,2},{4,7},{5,4},{6,5},{7,6},{8,11},{9,8},{10,9... | collective-permute-start | bytes 196616 | tf_op jit(solution)/shard_map/ppermute | solution.py:411
  13.5 7.4 %collective-permute-start.5 = (bf16[544,256]{1,0:T(8,128)(2,1)S(1)}, bf16[544,256]{1,0:T(8,128)(2,1)S(1)}, u32[]{:S(2)}, u32[]{:S(2)}) collective-permute-start(bf16[544,256]{1,0:T(8,128)(2,1)S(1)} %shard_map.184.g0), channel_id=1, source_target_pairs={{1,2},{2,1},{3,0},{0,3},{5,6},{6,5},{7,4},{4,7},{9,10},{10,9},{11,... | collective-permute-start | bytes 835592 | tf_op jit(solution)/shard_map/ppermute | solution.py:471
  20.9 8.5 %collective-permute-start.6 = (bf16[512,256]{1,0:T(8,128)(2,1)S(1)}, bf16[512,256]{1,0:T(8,128)(2,1)S(1)}, u32[]{:S(2)}, u32[]{:S(2)}) collective-permute-start(bf16[512,256]{1,0:T(8,128)(2,1)S(1)} %get-tuple-element.75.p0), channel_id=1, source_target_pairs={{0,1},{1,2},{2,3},{3,0},{4,5},{5,6},{6,7},{7,4},{8,9},{9,10},{10,1... | collective-permute-start | bytes 786440 | tf_op jit(solution)/shard_map/ppermute | solution.py:411
  20.9 8.6 %collective-permute-start.7 = (bf16[512,256]{1,0:T(8,128)(2,1)S(1)}, bf16[512,256]{1,0:T(8,128)(2,1)S(1)}, u32[]{:S(2)}, u32[]{:S(2)}) collective-permute-start(bf16[512,256]{1,0:T(8,128)(2,1)S(1)} %get-tuple-element.75.p0), channel_id=1, source_target_pairs={{0,3},{1,0},{2,1},{3,2},{4,7},{5,4},{6,5},{7,6},{8,11},{9,8},{10,9... | collective-permute-start | bytes 786440 | tf_op jit(solution)/shard_map/ppermute | solution.py:411
  29.4 6.5 %collective-permute-start.8 = (bf16[256,256]{1,0:T(8,128)(2,1)S(1)}, bf16[256,256]{1,0:T(8,128)(2,1)S(1)}, u32[]{:S(2)}, u32[]{:S(2)}) collective-permute-start(bf16[256,256]{1,0:T(8,128)(2,1)S(1)} %slice.16), channel_id=1, source_target_pairs={{0,1},{1,2},{2,3},{3,0},{4,5},{5,6},{6,7},{7,4},{8,9},{9,10},{10,1... | collective-permute-start | bytes 393224 | tf_op jit(solution)/shard_map/ppermute | solution.py:411
  29.5 6.4 %collective-permute-start.9 = (bf16[256,256]{1,0:T(8,128)(2,1)S(1)}, bf16[256,256]{1,0:T(8,128)(2,1)S(1)}, u32[]{:S(2)}, u32[]{:S(2)}) collective-permute-start(bf16[256,256]{1,0:T(8,128)(2,1)S(1)} %slice.17), channel_id=1, source_target_pairs={{0,3},{1,0},{2,1},{3,2},{4,7},{5,4},{6,5},{7,6},{8,11},{9,8},{10,9... | collective-permute-start | bytes 393224 | tf_op jit(solution)/shard_map/ppermute | solution.py:411
  56.8 10.1 %collective-permute-start.10 = (bf16[2176,128]{1,0:T(8,128)(2,1)S(1)}, bf16[2176,128]{1,0:T(8,128)(2,1)S(1)}, u32[]{:S(2)}, u32[]{:S(2)}) collective-permute-start(bf16[2176,128]{1,0:T(8,128)(2,1)S(1)} %get-tuple-element.90), channel_id=1, source_target_pairs={{0,4},{4,0},{1,5},{5,1},{2,6},{6,2},{3,7},{7,3},{8,12},{12,8},{9,1... | collective-permute-start | bytes 1671176 | tf_op jit(solution)/shard_map/ppermute | solution.py:411
  67.5 10.5 %collective-permute-start.11 = (bf16[640,128]{1,0:T(8,128)(2,1)S(1)}, bf16[640,128]{1,0:T(8,128)(2,1)S(1)}, u32[]{:S(2)}, u32[]{:S(2)}) collective-permute-start(bf16[640,128]{1,0:T(8,128)(2,1)S(1)} %get-tuple-element.94), channel_id=1, source_target_pairs={{0,1},{1,2},{2,3},{3,0},{4,5},{5,6},{6,7},{7,4},{8,9},{9,10},{10,1... | collective-permute-start | bytes 491528 | tf_op jit(solution)/shard_map/ppermute | solution.py:411
  67.6 10.5 %collective-permute-start.13 = (bf16[640,128]{1,0:T(8,128)(2,1)S(1)}, bf16[640,128]{1,0:T(8,128)(2,1)S(1)}, u32[]{:S(2)}, u32[]{:S(2)}) collective-permute-start(bf16[640,128]{1,0:T(8,128)(2,1)S(1)} %get-tuple-element.96), channel_id=1, source_target_pairs={{0,3},{1,0},{2,1},{3,2},{4,7},{5,4},{6,5},{7,6},{8,11},{9,8},{10,9... | collective-permute-start | bytes 491528 | tf_op jit(solution)/shard_map/ppermute | solution.py:411
  70.9 7.2 %collective-permute-start.12 = (bf16[384,128]{1,0:T(8,128)(2,1)S(1)}, bf16[384,128]{1,0:T(8,128)(2,1)S(1)}, u32[]{:S(2)}, u32[]{:S(2)}) collective-permute-start(bf16[384,128]{1,0:T(8,128)(2,1)S(1)} %get-tuple-element.95), channel_id=1, source_target_pairs={{0,2},{1,3},{2,0},{3,1},{4,6},{5,7},{6,4},{7,5},{8,10},{9,11},{10,... | collective-permute-start | bytes 294920 | tf_op jit(solution)/shard_map/ppermute | solution.py:411
  72.0 6.2 %collective-permute-start.14 = (bf16[128,256]{1,0:T(8,128)(2,1)S(1)}, bf16[128,256]{1,0:T(8,128)(2,1)S(1)}, u32[]{:S(2)}, u32[]{:S(2)}) collective-permute-start(bf16[128,256]{1,0:T(8,128)(2,1)S(1)} %get-tuple-element.98), channel_id=1, source_target_pairs={{4,8},{12,16},{20,24},{28,32},{36,40},{44,48},{52,56},{60,64},{68,... | collective-permute-start | bytes 196616 | tf_op jit(solution)/shard_map/ppermute | solution.py:543
  107.0 5.6 %collective-permute-start.15 = (bf16[64,48,128]{2,1,0:T(8,128)(2,1)S(1)}, bf16[64,48,128]{2,1,0:T(8,128)(2,1)S(1)}, u32[]{:S(2)}, u32[]{:S(2)}) collective-permute-start(bf16[64,48,128]{2,1,0:T(8,128)(2,1)S(1)} %all_to_all.11.mine_ref), channel_id=1, source_target_pairs={{0,4},{4,0},{1,5},{5,1},{2,6},{6,2},{3,7},{7,3},{8,12},{12,8},{9,1... | collective-permute-start | bytes 2359304 | tf_op jit(solution)/shard_map/ppermute | solution.py:411

commit v5 on v4

--- a/solution.py
+++ b/solution.py
@@ -108,6 +108,13 @@
     packed = split_count(jnp.broadcast_to(count, (16, CNODE)))
     out_ref[CNODE : CNODE + 16, :] = packed[:, :256]
     out_ref[CNODE + 16 : CNODE + 32, :] = packed[:, 256:]
+
+
+def pair_kernel(mine_ref, near_ref, far_ref, first_ref, second_ref):
+    half = near_ref.shape[0]
+    mine = mine_ref[...].astype(F32)
+    first_ref[...] = (mine[0:half] + near_ref[...].astype(F32)).astype(BF)
+    second_ref[...] = (mine[half:] + far_ref[...].astype(F32)).astype(BF)
 
 
 def own_kernel(own_ref, src_ref, target_ref, w1_ref, part_ref):
@@ -158,7 +165,7 @@
 
 
 def coarse_kernel(
-    p0, p1, p2, p3, p4, g0, g1, src_ref, dst_ref, w1_ref, w2_ref, gain_ref, cot_ref,
+    p0, p1, q0, q1, g0, g1, src_ref, dst_ref, w1_ref, w2_ref, gain_ref, cot_ref,
     assign_ref, place_ref, grad_fine_ref, pack_ref,
     table, slope, pick_t, sum_t, acc, by_src, by_dst,
 ):
@@ -168,8 +175,13 @@
     count = whole_count(g0[CNODE:, :]) + whole_count(g1[CNODE:, :])
     weight = spread_row(1.0 / jnp.maximum(count, 1.0))
     weight = jnp.concatenate([weight] * (feature // 128), axis=1)
-    across = jnp.concatenate([p3[...].astype(F32), p4[...].astype(F32)], axis=0)
-    pooled = (p0[...].astype(F32) + p1[...].astype(F32)) + (p2[...].astype(F32) + across)
+    pooled = jnp.concatenate(
+        [
+            p0[...].astype(F32) + p1[...].astype(F32),
+            q0[...].astype(F32) + q1[...].astype(F32),
+        ],
+        axis=0,
+    )
     table[...] = (pooled * weight).astype(BF)
     for at in range(0, edges, CHUNK):
         here = slice(at, at + CHUNK)
@@ -488,16 +500,22 @@
         limit=LIMITS[1],
         work=1.6,
     )
+    pooled, pair_got = lax.optimization_barrier((pooled, pair_got))
     half_rows = CNODE // 2
-    pooled, pair_got = lax.optimization_barrier((pooled, pair_got))
-    left, right = send(pooled, "x", 1), send(pooled, "x", 3)
-    across = [send(left[:half_rows], "x", 1), send(right[half_rows:], "x", 3)]
+    got = [
+        lax.ppermute(pooled[:half_rows], "x", near),
+        lax.ppermute(pooled[half_rows:], "x", far),
+    ]
+    first, second = run(
+        pair_kernel, [((half_rows, feature), BF)] * 2, [pooled, *got], inner=(0, 1)
+    )
+    got = [lax.ppermute(first, "x", far), lax.ppermute(second, "x", near)]
 
     grad_fine, coarse_pack = run(
         coarse_kernel,
         [((nodes, feature), F32), ((2, 384, 128), F32)],
         [
-            pooled, left, right, *across, pair, pair_got, csrc_in, cdst_in, cw1_in, cw2_in, cgain_in,
+            first, got[0], second, got[1], pair, pair_got, csrc_in, cdst_in, cw1_in, cw2_in, cgain_in,
             cot_in, assign_in, place,
         ],
         [
@@ -509,7 +527,7 @@
             ((CNODE, hidden), F32),
             ((CNODE, hidden), F32),
         ],
-        scalars=(14,),
+        scalars=(13,),
         inner=(0, 1),
         limit=LIMITS[2],
         work=5.0,

time: 115 us -> 113 us (0.983)
  starting transfers between devices: 30.6 us -> 24.7 us
  blocking collectives: 28.6 us -> 31.1 us
    ppermute x0 -> x4, waiting for transfers between devices: none -> 10.4 us  [the longest x2 5.09 us: shards(): got = [lax.ppermute(first, 'x', far), lax.ppermute(second, 'x', near)]]
    ppermute x12 -> x8, waiting for transfers between devices: 17.2 us -> 7.95 us  [send(): lax.ppermute(value, axis, [(i, (i + step) % size) for i in range(size)])]
    ppermute x12 -> x8, starting transfers between devices: 25.9 us -> 17.5 us  [send(): lax.ppermute(value, axis, [(i, (i + step) % size) for i in range(size)])]
    ppermute x0 -> x4, starting transfers between devices: none -> 2.49 us  [the longest x1 1.5 us: shards(): lax.ppermute(pooled[half_rows:], 'x', far)]
    all_to_all x1, blocking collectives: 9.78 us -> 11.3 us  [shards(): both = lax.all_to_all(both, PLANE, 0, 0, tiled=True)]
    pallas_call x9 -> x10, Pallas kernels: 36 us -> 36.1 us  [run(): pl.pallas_call(body if copies else kernel, out_shape=shapes, in_specs=[pl...]
  transfers between devices with their start and end apart: 16 -> 16, of which waited for: 6 -> 8; matrix products, arithmetic and copies ran while one was open for 0% -> 0% of each run, Pallas kernels for 8% -> 8%
where the time goes in v5:
time: 113 us
  Pallas kernels  36.1 us (32%)
  blocking collectives  31.1 us (28%)
  starting transfers between devices  24.7 us (22%)
  waiting for transfers between devices  19.2 us (17%)
  between operations  1.42 us (1%)
    pallas_call x10, Pallas kernels, run(): pl.pallas_call(body if copies else kernel, out_shape=shapes, in_specs=[pl...  36.1 us
    all_to_all x1, blocking collectives, shards(): mine = lax.all_to_all(copies, CHIPS, 0, 0, tiled=True)  19.8 us
    ppermute x8, starting transfers between devices, send(): lax.ppermute(value, axis, [(i, (i + step) % size) for i in range(size)])  17.5 us
    all_to_all x1, blocking collectives, shards(): both = lax.all_to_all(both, PLANE, 0, 0, tiled=True)  11.3 us
    ppermute x8, waiting for transfers between devices, send(): lax.ppermute(value, axis, [(i, (i + step) % size) for i in range(size)])  7.95 us
    ppermute x2, waiting for transfers between devices, shards(): got = [lax.ppermute(first, 'x', far), lax.ppermute(second, 'x', near)]  5.09 us
    ppermute x1, waiting for transfers between devices, shards(): lax.ppermute(pooled[half_rows:], 'x', far)  2.71 us
    ppermute x1, waiting for transfers between devices, shards(): lax.ppermute(pooled[:half_rows], 'x', near)  2.6 us
  transfers between devices with their start and end apart: 16, of which 8 were waited for; matrix products, arithmetic and copies ran while one was open for 0% of the time, Pallas kernels for 8%

profile of v5, /device:TPU:1, one launch (start us, length us, event | category | flops | bytes accessed | tf_op | source)
XLA Modules:
  0.0 112.8 jit_solution(18368087807545873093)
XLA Ops:
  1.3 0.1 pad_add_fusion.refs_5_.place_ref
  1.4 2.4 %shard_map.182 = (bf16[128,256]{1,0:T(8,128)(2,1)S(1)}, bf16[544,256]{1,0:T(8,128)(2,1)S(1)}, s32[1,2048]{1,0:T(1,128)S(1)}, bf16[512,256]{1,0:T(8,128)(2,1)S(1)...) custom-call(bf16[512,256]{1,0:T(8,128)(2,1)} %bitcast.15, ...), custom_call_target="tpu_custom_call" | custom-call | flops 200000000 | bytes 1947664 | tf_op jit(solution)/shard_map/pallas_call | solution.py:401
  3.8 2.1 %collective-permute-start = (bf16[544,256]{1,0:T(8,128)(2,1)S(1)}, bf16[544,256]{1,0:T(8,128)(2,1)S(1)}, u32[]{:S(2)}, u32[]{:S(2)}) collective-permute-start(bf16[544,256]{1,0:T(8,128)(2,1)S(1)} %get-tuple-element.67.mine_ref), channel_id=1, source_target_pairs={{0,1},{1,0},{2,3},{3,2},{4,5},{5,4},{6,7},{7,6},{8,9},{9,8},{10,11... | collective-permute-start | bytes 835592 | tf_op jit(solution)/shard_map/ppermute | solution.py:467
  5.9 1.0 collective-permute-start.1
  6.9 1.2 %collective-permute-start.2 = (bf16[128,256]{1,0:T(8,128)(2,1)S(1)}, bf16[128,256]{1,0:T(8,128)(2,1)S(1)}, u32[]{:S(2)}, u32[]{:S(2)}) collective-permute-start(bf16[128,256]{1,0:T(8,128)(2,1)S(1)} %get-tuple-element.71), channel_id=1, source_target_pairs={{4,8},{12,16},{20,24},{28,32},{36,40},{44,48},{52,56},{60,64},{68,... | collective-permute-start | bytes 196616 | tf_op jit(solution)/shard_map/ppermute | solution.py:470
  8.1 0.3 collective-permute-start.3
  8.3 2.4 %collective-permute-start.4 = (bf16[128,256]{1,0:T(8,128)(2,1)S(1)}, bf16[128,256]{1,0:T(8,128)(2,1)S(1)}, u32[]{:S(2)}, u32[]{:S(2)}) collective-permute-start(bf16[128,256]{1,0:T(8,128)(2,1)S(1)} %get-tuple-element.71), channel_id=1, source_target_pairs={{0,3},{1,0},{2,1},{3,2},{4,7},{5,4},{6,5},{7,6},{8,11},{9,8},{10,9... | collective-permute-start | bytes 196616 | tf_op jit(solution)/shard_map/ppermute | solution.py:423
  10.7 2.6 %shard_map.183 = (f32[2048,512]{1,0:T(8,128)S(1)}, s32[1,3072]{1,0:T(1,128)S(1)}, s32[1,3072]{1,0:T(1,128)S(1)}, bf16[512,512]{1,0:T(8,128)(2,1)S(1)}, bf16[512,...) custom-call(bf16[512,256]{1,0:T(8,128)(2,1)S(1)} %get-tuple-element.62.refs_0_.own_ref, ...), custom_call_target="tpu_custom_call" | custom-call | flops 2200000000 | bytes 6071296 | tf_op jit(solution)/shard_map/pallas_call | solution.py:401
  13.4 0.0 collective-permute-done.got_ref
  13.4 0.1 shard_map.184.g0
  13.5 1.4 %collective-permute-start.5 = (bf16[544,256]{1,0:T(8,128)(2,1)S(1)}, bf16[544,256]{1,0:T(8,128)(2,1)S(1)}, u32[]{:S(2)}, u32[]{:S(2)}) collective-permute-start(bf16[544,256]{1,0:T(8,128)(2,1)S(1)} %shard_map.184.g0), channel_id=1, source_target_pairs={{1,2},{2,1},{3,0},{0,3},{5,6},{6,5},{7,4},{4,7},{9,10},{10,9},{11,... | collective-permute-start | bytes 835592 | tf_op jit(solution)/shard_map/ppermute | solution.py:483
  14.9 0.0 collective-permute-done.1.ra
  14.9 0.0 collective-permute-done.2.rb
  14.9 0.0 collective-permute-done.3.rw
  14.9 0.0 collective-permute-done.4.re
  14.9 5.1 %shard_map.185 = (f32[2048,512]{1,0:T(8,128)S(1)}, bf16[512,512]{1,0:T(8,128)(2,1)S(1)}, f32[512,256]{1,0:T(8,128)S(1)}, bf16[512,256]{1,0:T(8,128)(2,1)S(1)}, bf16[1024,256]{1,0:T(8,128)(2,1)S(1)}) custom-call(f32[2048,512]{1,0:T(8,128)S(1)} %get-tuple-element.70.part_ref, bf16[512,256]{1,0:T(8,128)(2,1)S(1)} %get-tuple-element.62.refs_0_.own_ref, ...), custom_call_target="tpu_custom_call" | custom-call | flops 3200000000 | bytes 11553808 | tf_op jit(solution)/shard_map/pallas_call | solution.py:401
  20.0 0.8 collective-permute-done.5.g1
  20.9 0.1 collective-permute-start.6
  21.0 1.5 %collective-permute-start.7 = (bf16[256,256]{1,0:T(8,128)(2,1)S(1)}, bf16[256,256]{1,0:T(8,128)(2,1)S(1)}, u32[]{:S(2)}, u32[]{:S(2)}) collective-permute-start(bf16[256,256]{1,0:T(8,128)(2,1)S(1)} %get-tuple-element.113), channel_id=1, source_target_pairs={{1,2},{2,1},{3,0},{0,3},{5,6},{6,5},{7,4},{4,7},{9,10},{10,9},{11,... | collective-permute-start | bytes 393224 | tf_op jit(solution)/shard_map/ppermute | solution.py:507
  22.5 2.6 %collective-permute-done.6.near_ref = bf16[256,256]{1,0:T(8,128)(2,1)S(1)} collective-permute-done((bf16[256,256]{1,0:T(8,128)(2,1)S(1)}, bf16[256,256]{1,0:T(8,128)(2,1)S(1)}, u32[]{:S(2)}, u32[]{:S(2)}) %collective-permute-start.6) | collective-permute-done | bytes 131104 | tf_op jit(solution)/shard_map/ppermute | solution.py:506
  25.1 2.7 %collective-permute-done.7.far_ref = bf16[256,256]{1,0:T(8,128)(2,1)S(1)} collective-permute-done((bf16[256,256]{1,0:T(8,128)(2,1)S(1)}, bf16[256,256]{1,0:T(8,128)(2,1)S(1)}, u32[]{:S(2)}, u32[]{:S(2)}) %collective-permute-start.7) | collective-permute-done | bytes 131104 | tf_op jit(solution)/shard_map/ppermute | solution.py:507
  27.8 0.1 shard_map.186
  27.9 0.9 collective-permute-start.8
  28.8 0.0 collective-permute-start.9
  28.8 4.2 %collective-permute-done.8.p1 = bf16[256,256]{1,0:T(8,128)(2,1)S(1)} collective-permute-done((bf16[256,256]{1,0:T(8,128)(2,1)S(1)}, bf16[256,256]{1,0:T(8,128)(2,1)S(1)}, u32[]{:S(2)}, u32[]{:S(2)}) %collective-permute-start.8) | collective-permute-done | bytes 131104 | tf_op jit(solution)/shard_map/ppermute | solution.py:512
  33.0 0.9 collective-permute-done.9.q1
  33.8 14.1 %shard_map.187 = (f32[512,256]{1,0:T(8,128)S(1)}, f32[2,384,128]{2,1,0:T(8,128)S(1)}) custom-call(bf16[256,256]{1,0:T(8,128)(2,1)S(1)} %get-tuple-element.78.p0, bf16[256,256]{1,0:T(8,128)(2,1)S(1)} %collective-permute-done.8.p1, bf16[256,256]{1,0:T(8,128)(2,1)S(1)} %get-tuple-element.79.q0, bf16[256,256]{1,0:T(8,128)(2,1)S(1)} %collective-permute-done.9.q1, ...), custom_call_target="tpu_custom_call" | custom-call | flops 10000000000 | bytes 3075088 | tf_op jit(solution)/shard_map/pallas_call | solution.py:401
  47.9 6.9 %shard_map.188 = (f32[512,256]{1,0:T(8,128)S(1)}, bf16[2176,128]{1,0:T(8,128)(2,1)S(1)}, f32[1920,128]{1,0:T(8,128)S(1)}, bf16[128,256]{1,0:T(8,128)(2,1)S(1)}, ...) custom-call(f32[512,256]{1,0:T(8,128)S(1)} %get-tuple-element.87.grad_fine_ref, ...), custom_call_target="tpu_custom_call" | custom-call | flops 5600000000 | bytes 9749520 | tf_op jit(solution)/shard_map/pallas_call | solution.py:401
  54.8 7.7 %collective-permute-start.10 = (bf16[2176,128]{1,0:T(8,128)(2,1)S(1)}, bf16[2176,128]{1,0:T(8,128)(2,1)S(1)}, u32[]{:S(2)}, u32[]{:S(2)}) collective-permute-start(bf16[2176,128]{1,0:T(8,128)(2,1)S(1)} %get-tuple-element.94), channel_id=1, source_target_pairs={{0,4},{4,0},{1,5},{5,1},{2,6},{6,2},{3,7},{7,3},{8,12},{12,8},{9,1... | collective-permute-start | bytes 1671176 | tf_op jit(solution)/shard_map/ppermute | solution.py:423
  62.4 1.6 %collective-permute-done.10.got_ref.from_core = bf16[2176,128]{1,0:T(8,128)(2,1)S(1)} collective-permute-done((bf16[2176,128]{1,0:T(8,128)(2,1)S(1)}, bf16[2176,128]{1,0:T(8,128)(2,1)S(1)}, u32[]{:S(2)}, u32[]{:S(2)}) %collective-permute-start.10) | collective-permute-done | bytes 557088 | tf_op jit(solution)/shard_map/ppermute | solution.py:423
  64.0 0.7 shard_map.189
  64.7 0.1 collective-permute-start.11
  64.8 2.7 %collective-permute-start.13 = (bf16[640,128]{1,0:T(8,128)(2,1)S(1)}, bf16[640,128]{1,0:T(8,128)(2,1)S(1)}, u32[]{:S(2)}, u32[]{:S(2)}) collective-permute-start(bf16[640,128]{1,0:T(8,128)(2,1)S(1)} %get-tuple-element.100), channel_id=1, source_target_pairs={{0,3},{1,0},{2,1},{3,2},{4,7},{5,4},{6,5},{7,6},{8,11},{9,8},{10,9... | collective-permute-start | bytes 491528 | tf_op jit(solution)/shard_map/ppermute | solution.py:423
  67.4 0.3 collective-permute-start.12
  67.7 0.0 collective-permute-start.14
  67.7 6.1 %collective-permute-done.12 = bf16[384,128]{1,0:T(8,128)(2,1)S(1)} collective-permute-done((bf16[384,128]{1,0:T(8,128)(2,1)S(1)}, bf16[384,128]{1,0:T(8,128)(2,1)S(1)}, u32[]{:S(2)}, u32[]{:S(2)}) %collective-permute-start.12) | collective-permute-done | bytes 98336 | tf_op jit(solution)/shard_map/ppermute | solution.py:423
  73.8 0.0 collective-permute-done.11.from_west
  73.8 0.0 collective-permute-done.13.from_east
  73.8 0.1 add_convert_fusion
  73.9 0.0 collective-permute-done.14.from_b
  73.9 11.3 %all_to_all.10 = bf16[16,48,128]{2,1,0:T(8,128)(2,1)S(1)} all-to-all(bf16[16,48,128]{2,1,0:T(8,128)(2,1)S(1)} %pad_maximum_fusion), channel_id=1, replica_groups=mesh['z'=4,'y'=4,'core'=2,'x'=4] {'z','y'}, dimensions={0} | all-to-all | bytes 393216 | tf_op jit(solution)/shard_map/all_to_all | solution.py:588
  85.2 0.1 broadcast_in_dim.17
  85.4 19.8 %all_to_all.11.mine_ref = bf16[64,48,128]{2,1,0:T(8,128)(2,1)S(1)} all-to-all(bf16[64,48,128]{2,1,0:T(8,128)(2,1)S(1)} %broadcast_in_dim.17), channel_id=1, replica_groups=mesh['z'=4,'y'=4,'core'=2,'x'=4] {'z','y','x'}, dimensions={0} | all-to-all | bytes 1572864 | tf_op jit(solution)/shard_map/all_to_all | solution.py:591
  105.1 3.2 %collective-permute-start.15 = (bf16[64,48,128]{2,1,0:T(8,128)(2,1)S(1)}, bf16[64,48,128]{2,1,0:T(8,128)(2,1)S(1)}, u32[]{:S(2)}, u32[]{:S(2)}) collective-permute-start(bf16[64,48,128]{2,1,0:T(8,128)(2,1)S(1)} %all_to_all.11.mine_ref), channel_id=1, source_target_pairs={{0,4},{4,0},{1,5},{5,1},{2,6},{6,2},{3,7},{7,3},{8,12},{12,8},{9,1... | collective-permute-start | bytes 2359304 | tf_op jit(solution)/shard_map/ppermute | solution.py:423
  108.4 1.7 %shard_map.190 = f32[512,256]{1,0:T(8,128)} custom-call(f32[512,256]{1,0:T(8,128)S(1)} %get-tuple-element.105.local_ref, bf16[2176,128]{1,0:T(8,128)(2,1)S(1)} %collective-permute-done.10.got_ref.from_core, bf16[128,256]{1,0:T(8,128)(2,1)S(1)} %collective-permute-done.14.from_b, bf16[640,128]{1,0:T(8,128)(2,1)S(1)} %collective-permute-done.11.from_west, ...), custom_call_target="tpu_custom_call" | custom-call | flops 200000000 | bytes 1999376 | tf_op jit(solution)/shard_map/pallas_call | solution.py:401
  110.0 0.3 collective-permute-done.15.other_ref
  110.3 2.5 %shard_map.191 = (f32[512,512]{1,0:T(8,128)}, f32[512,256]{1,0:T(8,128)}, f32[512,512]{1,0:T(8,128)}, f32[512,256]{1,0:T(8,128)}) custom-call(bf16[64,48,128]{2,1,0:T(8,128)(2,1)S(1)} %all_to_all.11.mine_ref, bf16[64,48,128]{2,1,0:T(8,128)(2,1)S(1)} %collective-permute-done.15.other_ref, s32[4]{0:T(128)S(1)} %pad_add_fusion.refs_5_.place_ref), custom_call_target="tpu_custom_call" | custom-call | flops 200000000 | bytes 4718608 | tf_op jit(solution)/shard_map/pallas_call | solution.py:401
  (4 shorter events, 0.1 us)
Async XLA Ops:
  3.8 9.6 %collective-permute-start = (bf16[544,256]{1,0:T(8,128)(2,1)S(1)}, bf16[544,256]{1,0:T(8,128)(2,1)S(1)}, u32[]{:S(2)}, u32[]{:S(2)}) collective-permute-start(bf16[544,256]{1,0:T(8,128)(2,1)S(1)} %get-tuple-element.67.mine_ref), channel_id=1, source_target_pairs={{0,1},{1,0},{2,3},{3,2},{4,5},{5,4},{6,7},{7,6},{8,9},{9,8},{10,11... | collective-permute-start | bytes 835592 | tf_op jit(solution)/shard_map/ppermute | solution.py:467
  5.9 9.0 %collective-permute-start.1 = (bf16[128,256]{1,0:T(8,128)(2,1)S(1)}, bf16[128,256]{1,0:T(8,128)(2,1)S(1)}, u32[]{:S(2)}, u32[]{:S(2)}) collective-permute-start(bf16[128,256]{1,0:T(8,128)(2,1)S(1)} %get-tuple-element.71), channel_id=1, source_target_pairs={{0,4},{4,0},{1,5},{5,1},{2,6},{6,2},{3,7},{7,3},{8,12},{12,8},{9,1... | collective-permute-start | bytes 196616 | tf_op jit(solution)/shard_map/ppermute | solution.py:423
  6.9 8.0 %collective-permute-start.2 = (bf16[128,256]{1,0:T(8,128)(2,1)S(1)}, bf16[128,256]{1,0:T(8,128)(2,1)S(1)}, u32[]{:S(2)}, u32[]{:S(2)}) collective-permute-start(bf16[128,256]{1,0:T(8,128)(2,1)S(1)} %get-tuple-element.71), channel_id=1, source_target_pairs={{4,8},{12,16},{20,24},{28,32},{36,40},{44,48},{52,56},{60,64},{68,... | collective-permute-start | bytes 196616 | tf_op jit(solution)/shard_map/ppermute | solution.py:470
  8.1 6.8 %collective-permute-start.3 = (bf16[128,256]{1,0:T(8,128)(2,1)S(1)}, bf16[128,256]{1,0:T(8,128)(2,1)S(1)}, u32[]{:S(2)}, u32[]{:S(2)}) collective-permute-start(bf16[128,256]{1,0:T(8,128)(2,1)S(1)} %get-tuple-element.71), channel_id=1, source_target_pairs={{0,1},{1,2},{2,3},{3,0},{4,5},{5,6},{6,7},{7,4},{8,9},{9,10},{10,1... | collective-permute-start | bytes 196616 | tf_op jit(solution)/shard_map/ppermute | solution.py:423
  8.3 6.6 %collective-permute-start.4 = (bf16[128,256]{1,0:T(8,128)(2,1)S(1)}, bf16[128,256]{1,0:T(8,128)(2,1)S(1)}, u32[]{:S(2)}, u32[]{:S(2)}) collective-permute-start(bf16[128,256]{1,0:T(8,128)(2,1)S(1)} %get-tuple-element.71), channel_id=1, source_target_pairs={{0,3},{1,0},{2,1},{3,2},{4,7},{5,4},{6,5},{7,6},{8,11},{9,8},{10,9... | collective-permute-start | bytes 196616 | tf_op jit(solution)/shard_map/ppermute | solution.py:423
  13.5 7.4 %collective-permute-start.5 = (bf16[544,256]{1,0:T(8,128)(2,1)S(1)}, bf16[544,256]{1,0:T(8,128)(2,1)S(1)}, u32[]{:S(2)}, u32[]{:S(2)}) collective-permute-start(bf16[544,256]{1,0:T(8,128)(2,1)S(1)} %shard_map.184.g0), channel_id=1, source_target_pairs={{1,2},{2,1},{3,0},{0,3},{5,6},{6,5},{7,4},{4,7},{9,10},{10,9},{11,... | collective-permute-start | bytes 835592 | tf_op jit(solution)/shard_map/ppermute | solution.py:483
  20.9 4.2 %collective-permute-start.6 = (bf16[256,256]{1,0:T(8,128)(2,1)S(1)}, bf16[256,256]{1,0:T(8,128)(2,1)S(1)}, u32[]{:S(2)}, u32[]{:S(2)}) collective-permute-start(bf16[256,256]{1,0:T(8,128)(2,1)S(1)} %get-tuple-element.114), channel_id=1, source_target_pairs={{0,1},{1,0},{2,3},{3,2},{4,5},{5,4},{6,7},{7,6},{8,9},{9,8},{10,11... | collective-permute-start | bytes 393224 | tf_op jit(solution)/shard_map/ppermute | solution.py:506
  21.0 6.8 %collective-permute-start.7 = (bf16[256,256]{1,0:T(8,128)(2,1)S(1)}, bf16[256,256]{1,0:T(8,128)(2,1)S(1)}, u32[]{:S(2)}, u32[]{:S(2)}) collective-permute-start(bf16[256,256]{1,0:T(8,128)(2,1)S(1)} %get-tuple-element.113), channel_id=1, source_target_pairs={{1,2},{2,1},{3,0},{0,3},{5,6},{6,5},{7,4},{4,7},{9,10},{10,9},{11,... | collective-permute-start | bytes 393224 | tf_op jit(solution)/shard_map/ppermute | solution.py:507
  27.9 5.1 %collective-permute-start.8 = (bf16[256,256]{1,0:T(8,128)(2,1)S(1)}, bf16[256,256]{1,0:T(8,128)(2,1)S(1)}, u32[]{:S(2)}, u32[]{:S(2)}) collective-permute-start(bf16[256,256]{1,0:T(8,128)(2,1)S(1)} %get-tuple-element.78.p0), channel_id=1, source_target_pairs={{1,2},{2,1},{3,0},{0,3},{5,6},{6,5},{7,4},{4,7},{9,10},{10,9},{11,... | collective-permute-start | bytes 393224 | tf_op jit(solution)/shard_map/ppermute | solution.py:512
  28.8 5.1 %collective-permute-start.9 = (bf16[256,256]{1,0:T(8,128)(2,1)S(1)}, bf16[256,256]{1,0:T(8,128)(2,1)S(1)}, u32[]{:S(2)}, u32[]{:S(2)}) collective-permute-start(bf16[256,256]{1,0:T(8,128)(2,1)S(1)} %get-tuple-element.79.q0), channel_id=1, source_target_pairs={{0,1},{1,0},{2,3},{3,2},{4,5},{5,4},{6,7},{7,6},{8,9},{9,8},{10,11... | collective-permute-start | bytes 393224 | tf_op jit(solution)/shard_map/ppermute | solution.py:512
  54.8 9.2 %collective-permute-start.10 = (bf16[2176,128]{1,0:T(8,128)(2,1)S(1)}, bf16[2176,128]{1,0:T(8,128)(2,1)S(1)}, u32[]{:S(2)}, u32[]{:S(2)}) collective-permute-start(bf16[2176,128]{1,0:T(8,128)(2,1)S(1)} %get-tuple-element.94), channel_id=1, source_target_pairs={{0,4},{4,0},{1,5},{5,1},{2,6},{6,2},{3,7},{7,3},{8,12},{12,8},{9,1... | collective-permute-start | bytes 1671176 | tf_op jit(solution)/shard_map/ppermute | solution.py:423
  64.7 9.1 %collective-permute-start.11 = (bf16[640,128]{1,0:T(8,128)(2,1)S(1)}, bf16[640,128]{1,0:T(8,128)(2,1)S(1)}, u32[]{:S(2)}, u32[]{:S(2)}) collective-permute-start(bf16[640,128]{1,0:T(8,128)(2,1)S(1)} %get-tuple-element.98), channel_id=1, source_target_pairs={{0,1},{1,2},{2,3},{3,0},{4,5},{5,6},{6,7},{7,4},{8,9},{9,10},{10,1... | collective-permute-start | bytes 491528 | tf_op jit(solution)/shard_map/ppermute | solution.py:423
  64.8 9.1 %collective-permute-start.13 = (bf16[640,128]{1,0:T(8,128)(2,1)S(1)}, bf16[640,128]{1,0:T(8,128)(2,1)S(1)}, u32[]{:S(2)}, u32[]{:S(2)}) collective-permute-start(bf16[640,128]{1,0:T(8,128)(2,1)S(1)} %get-tuple-element.100), channel_id=1, source_target_pairs={{0,3},{1,0},{2,1},{3,2},{4,7},{5,4},{6,5},{7,6},{8,11},{9,8},{10,9... | collective-permute-start | bytes 491528 | tf_op jit(solution)/shard_map/ppermute | solution.py:423
  67.4 6.4 %collective-permute-start.12 = (bf16[384,128]{1,0:T(8,128)(2,1)S(1)}, bf16[384,128]{1,0:T(8,128)(2,1)S(1)}, u32[]{:S(2)}, u32[]{:S(2)}) collective-permute-start(bf16[384,128]{1,0:T(8,128)(2,1)S(1)} %get-tuple-element.99), channel_id=1, source_target_pairs={{0,2},{1,3},{2,0},{3,1},{4,6},{5,7},{6,4},{7,5},{8,10},{9,11},{10,... | collective-permute-start | bytes 294920 | tf_op jit(solution)/shard_map/ppermute | solution.py:423
  67.7 6.2 %collective-permute-start.14 = (bf16[128,256]{1,0:T(8,128)(2,1)S(1)}, bf16[128,256]{1,0:T(8,128)(2,1)S(1)}, u32[]{:S(2)}, u32[]{:S(2)}) collective-permute-start(bf16[128,256]{1,0:T(8,128)(2,1)S(1)} %get-tuple-element.102), channel_id=1, source_target_pairs={{4,8},{12,16},{20,24},{28,32},{36,40},{44,48},{52,56},{60,64},{68,... | collective-permute-start | bytes 196616 | tf_op jit(solution)/shard_map/ppermute | solution.py:561
  105.1 5.1 %collective-permute-start.15 = (bf16[64,48,128]{2,1,0:T(8,128)(2,1)S(1)}, bf16[64,48,128]{2,1,0:T(8,128)(2,1)S(1)}, u32[]{:S(2)}, u32[]{:S(2)}) collective-permute-start(bf16[64,48,128]{2,1,0:T(8,128)(2,1)S(1)} %all_to_all.11.mine_ref), channel_id=1, source_target_pairs={{0,4},{4,0},{1,5},{5,1},{2,6},{6,2},{3,7},{7,3},{8,12},{12,8},{9,1... | collective-permute-start | bytes 2359304 | tf_op jit(solution)/shard_map/ppermute | solution.py:423

commit v6 on v5

--- a/solution.py
+++ b/solution.py
@@ -117,18 +117,19 @@
     second_ref[...] = (mine[half:] + far_ref[...].astype(F32)).astype(BF)
 
 
-def own_kernel(own_ref, src_ref, target_ref, w1_ref, part_ref):
+def own_kernel(own_ref, src_ref, target_ref, w1_ref, part_ref, left_ref):
     nodes, feature = own_ref.shape
     for at in range(0, src_ref.shape[1], CHUNK):
         here = slice(at, at + CHUNK)
         left = dot(pick_matrix(src_ref[:, here], nodes), own_ref[...]).astype(BF)
+        left_ref[here, :] = left
         right = dot(pick_matrix(target_ref[:, here], nodes), own_ref[...]).astype(BF)
         part_ref[here, :] = dot(left, w1_ref[0:feature, :]) + dot(right, w1_ref[feature:, :])
 
 
 def fine_forward_kernel(
-    part_ref, own_ref, ra, rb, rw, re, src_ref, target_ref, place_ref,
-    w1_ref, w2_ref, gain_ref, assign_ref, slope_ref, acc_out, summed_ref, pooled_ref, table, acc,
+    part_ref, left_ref, own_ref, ra, rb, rw, re, src_ref, target_ref, place_ref,
+    w1_ref, w2_ref, gain_ref, assign_ref, slope_ref, acc_out, summed_ref, pooled_ref, pair_ref, table, acc,
 ):
     nodes, feature = own_ref.shape
     rim = ra.shape[0]
@@ -145,6 +146,7 @@
         here = slice(at, at + CHUNK)
         picks = pick_matrix(src_ref[:, here] - nodes, 4 * rim)
         left = dot(picks, table[nodes:, :]).astype(BF)
+        pair_ref[here, :] = left + left_ref[here, :]
         preact = part_ref[here, :] + dot(left, w1_ref[0:feature, :])
         hidden, slope = activations(preact)
         slope_ref[here, :] = slope
@@ -233,9 +235,9 @@
 
 
 def fine_backward_kernel(
-    grad_fine_ref, summed_ref, slope_ref, acc_ref, table_ref, src_ref, target_ref,
+    grad_fine_ref, summed_ref, slope_ref, acc_ref, left_ref, own_ref, src_ref, target_ref,
     place_ref, w1_ref, w2_ref, gain_ref, coarse_ref,
-    local_ref, give_ref, keep_ref, ghost_b, ghost_w, ghost_e, by_src, by_dst, ghost,
+    local_ref, give_ref, keep_ref, ghost_b, ghost_w, ghost_e, by_src, by_dst, ghost, grad_left,
 ):
     nodes, feature = grad_fine_ref.shape
     rim = ghost_b.shape[0]
@@ -247,21 +249,24 @@
         target = target_ref[:, here]
         grad_message = dot(pick_matrix(target, nodes), grad_summed).astype(BF)
         grad_preact = (dot_rt(grad_message, w2_ref[...]) * slope_ref[here, :]).astype(BF)
-        part_src = dot(sum_matrix(src_ref[:, here], table_ref.shape[0]), grad_preact)
+        back = dot_rt(grad_preact, w1_ref[0:feature, :]).astype(BF)
+        part_src = dot(sum_matrix(src_ref[:, here], by_src.shape[0]), back)
+        part_left = dot_lt(left_ref[here, :], grad_preact)
         part_dst = dot(sum_matrix(target, nodes), grad_preact)
         if at == 0:
             by_src[...] = part_src
+            grad_left[...] = part_left
             by_dst[...] = part_dst
         else:
             by_src[...] += part_src
+            grad_left[...] += part_left
             by_dst[...] += part_dst
-    grad_table = dot_rt(by_src[...].astype(BF), w1_ref[0:feature, :])
     local_ref[...] = (
         grad_fine
-        + grad_table[0:nodes, :]
+        + by_src[0:nodes, :]
         + dot_rt(by_dst[...].astype(BF), w1_ref[feature:, :])
     )
-    ghost[...] = grad_table[nodes:, :].astype(BF)
+    ghost[...] = by_src[nodes:, :].astype(BF)
     to_core = ghost[pl.ds(pl.multiple_of(rim * (1 - core), rim), rim), :]
     give_ref[1920 : 1920 + rim, :] = to_core[:, 0:128]
     give_ref[1920 + rim :, :] = to_core[:, 128:256]
@@ -271,8 +276,8 @@
         out[rim:, :] = ghost[at : at + rim, 128:256]
     for out, half in ((give_ref, 1 - core), (keep_ref, core)):
         part = pl.ds(pl.multiple_of(half * 256, 256), 256)
-        first = dot_lt(table_ref[...], by_src[:, part].astype(BF)).astype(out.dtype)
-        second = dot_lt(table_ref[0:nodes, :], by_dst[:, part].astype(BF)).astype(out.dtype)
+        first = grad_left[:, part].astype(out.dtype)
+        second = dot_lt(own_ref[...], by_dst[:, part].astype(BF)).astype(out.dtype)
         third = dot_lt(acc_ref[:, part], grad_summed).astype(out.dtype)
         for k in range(2):
             lanes = slice(128 * k, 128 * k + 128)
@@ -468,11 +473,11 @@
     from_west, from_east = send(rim, "x", 1), send(rim, "x", 3)
     from_a = send(rim, "core", 1)
     from_b = lax.ppermute(rim, ROW, between)
-    part, csrc_in, cdst_in, cw1_in, cw2_in, cgain_in, cot_in = run(
+    part, left, csrc_in, cdst_in, cw1_in, cw2_in, cgain_in, cot_in = run(
         own_kernel,
-        [((edges, hidden), F32)],
+        [((edges, hidden), F32), ((edges, feature), BF)],
         [own_in, src_in, target, w1_in],
-        inner=(0,),
+        inner=(0, 1),
         ahead=[coarse_src, coarse_dst, coarse_w1, coarse_w2, coarse_gain, cot],
         limit=LIMITS[0],
         work=1.1,
@@ -481,21 +486,21 @@
     (pair,) = run(add_kernel, [((CNODE + 32, feature), BF)], [pack, pack_got], inner=(0,))
     pair, part = lax.optimization_barrier((pair, part))
     pair_got = lax.ppermute(pair, "x", far)
-    slope, acc, summed, pooled, table = run(
+    slope, acc, summed, pooled, left = run(
         fine_forward_kernel,
         [
             ((edges, hidden), F32),
             ((nodes, hidden), BF),
             ((nodes, feature), F32),
             ((CNODE, feature), BF),
-            ((nodes + 4 * rim_count, feature), BF),
-        ],
-        [
-            part, own_in, from_a, from_b, from_west, from_east, src_in, target, place,
+            ((edges, feature), BF),
+        ],
+        [
+            part, left, own_in, from_a, from_b, from_west, from_east, src_in, target, place,
             w1_in, w2_in, gain_in, assign_in,
         ],
-        [((nodes, hidden), F32)],
-        scalars=(8,),
+        [((nodes + 4 * rim_count, feature), BF), ((nodes, hidden), F32)],
+        scalars=(9,),
         inner=(0, 1, 2, 3, 4),
         limit=LIMITS[1],
         work=1.6,
@@ -544,21 +549,23 @@
             ((2 * rim_count, 128), BF),
         ],
         [
-            grad_fine, summed, slope, acc, table, src_in, target, place,
+            grad_fine, summed, slope, acc, left, own_in, src_in, target, place,
             w1_in, w2_in, gain_in, coarse_pack,
         ],
         [
-            ((nodes + 4 * rim_count, hidden), F32),
+            ((nodes + 4 * rim_count, feature), F32),
             ((nodes, hidden), F32),
             ((4 * rim_count, feature), BF),
-        ],
-        scalars=(7,),
+            ((feature, hidden), F32),
+        ],
+        scalars=(8,),
         inner=(0, 1, 2, 3, 4, 5),
         limit=LIMITS[3],
         work=2.8,
     )
     from_core = send(give, "core", 1)
     from_b = lax.ppermute(ghost_b, ROW, between)
+    keep, from_b = lax.optimization_barrier((keep, from_b))
     total, coarse_total, to_east, to_cross, to_west = run(
         split_kernel,
         [
@@ -584,7 +591,6 @@
     both = jnp.concatenate(
         [total.reshape(16, 24, 128), coarse_total.reshape(16, 24, 128)], axis=1
     ).astype(BF)
-    both, from_b = lax.optimization_barrier((both, from_b))
     both = lax.all_to_all(both, PLANE, 0, 0, tiled=True)
     both = jnp.sum(both.astype(F32), axis=0).astype(BF)
     copies = jnp.broadcast_to(both[None], (64,) + both.shape)

time: 113 us -> 115 us (1.018)
  blocking collectives: 31.1 us -> 32.7 us
    ppermute x1, waiting for transfers between devices: 0.01 us -> 3.69 us  [shards(): from_b = lax.ppermute(ghost_b, ROW, between)]
    ppermute x8, waiting for transfers between devices: 7.95 us -> 4.98 us  [send(): lax.ppermute(value, axis, [(i, (i + step) % size) for i in range(size)])]
    all_to_all x1, blocking collectives: 11.3 us -> 13.4 us  [shards(): both = lax.all_to_all(both, PLANE, 0, 0, tiled=True)]
where the time goes in v6:
time: 115 us
  Pallas kernels  35.8 us (31%)
  blocking collectives  32.7 us (28%)
  starting transfers between devices  24.7 us (21%)
  waiting for transfers between devices  19.8 us (17%)
  between operations  1.42 us (1%)
    pallas_call x10, Pallas kernels, run(): pl.pallas_call(body if copies else kernel, out_shape=shapes, in_specs=[pl...  35.8 us
    all_to_all x1, blocking collectives, shards(): mine = lax.all_to_all(copies, CHIPS, 0, 0, tiled=True)  19.3 us
    ppermute x8, starting transfers between devices, send(): lax.ppermute(value, axis, [(i, (i + step) % size) for i in range(size)])  17.5 us
    all_to_all x1, blocking collectives, shards(): both = lax.all_to_all(both, PLANE, 0, 0, tiled=True)  13.4 us
    ppermute x2, waiting for transfers between devices, shards(): got = [lax.ppermute(first, 'x', far), lax.ppermute(second, 'x', near)]  5.08 us
    ppermute x8, waiting for transfers between devices, send(): lax.ppermute(value, axis, [(i, (i + step) % size) for i in range(size)])  4.98 us
    ppermute x1, waiting for transfers between devices, shards(): from_b = lax.ppermute(ghost_b, ROW, between)  3.69 us
    ppermute x1, waiting for transfers between devices, shards(): lax.ppermute(pooled[half_rows:], 'x', far)  2.71 us
  transfers between devices with their start and end apart: 16, of which 8 were waited for; matrix products, arithmetic and copies ran while one was open for 0% of the time, Pallas kernels for 8%

profile of v6, /device:TPU:1, one launch (start us, length us, event | category | flops | bytes accessed | tf_op | source)
XLA Modules:
  0.0 114.8 jit_solution(6629851176351227899)
XLA Ops:
  1.3 0.1 pad_add_fusion.refs_5_.place_ref
  1.4 2.4 %shard_map.182 = (bf16[128,256]{1,0:T(8,128)(2,1)S(1)}, bf16[544,256]{1,0:T(8,128)(2,1)S(1)}, s32[1,2048]{1,0:T(1,128)S(1)}, bf16[512,256]{1,0:T(8,128)(2,1)S(1)...) custom-call(bf16[512,256]{1,0:T(8,128)(2,1)} %bitcast.15, ...), custom_call_target="tpu_custom_call" | custom-call | flops 200000000 | bytes 1947664 | tf_op jit(solution)/shard_map/pallas_call | solution.py:406
  3.8 2.1 %collective-permute-start = (bf16[544,256]{1,0:T(8,128)(2,1)S(1)}, bf16[544,256]{1,0:T(8,128)(2,1)S(1)}, u32[]{:S(2)}, u32[]{:S(2)}) collective-permute-start(bf16[544,256]{1,0:T(8,128)(2,1)S(1)} %get-tuple-element.68.mine_ref), channel_id=1, source_target_pairs={{0,1},{1,0},{2,3},{3,2},{4,5},{5,4},{6,7},{7,6},{8,9},{9,8},{10,11... | collective-permute-start | bytes 835592 | tf_op jit(solution)/shard_map/ppermute | solution.py:472
  5.9 1.0 collective-permute-start.1
  6.9 1.2 %collective-permute-start.2 = (bf16[128,256]{1,0:T(8,128)(2,1)S(1)}, bf16[128,256]{1,0:T(8,128)(2,1)S(1)}, u32[]{:S(2)}, u32[]{:S(2)}) collective-permute-start(bf16[128,256]{1,0:T(8,128)(2,1)S(1)} %get-tuple-element.73), channel_id=1, source_target_pairs={{4,8},{12,16},{20,24},{28,32},{36,40},{44,48},{52,56},{60,64},{68,... | collective-permute-start | bytes 196616 | tf_op jit(solution)/shard_map/ppermute | solution.py:475
  8.1 0.3 collective-permute-start.3
  8.3 2.4 %collective-permute-start.4 = (bf16[128,256]{1,0:T(8,128)(2,1)S(1)}, bf16[128,256]{1,0:T(8,128)(2,1)S(1)}, u32[]{:S(2)}, u32[]{:S(2)}) collective-permute-start(bf16[128,256]{1,0:T(8,128)(2,1)S(1)} %get-tuple-element.73), channel_id=1, source_target_pairs={{0,3},{1,0},{2,1},{3,2},{4,7},{5,4},{6,5},{7,6},{8,11},{9,8},{10,9... | collective-permute-start | bytes 196616 | tf_op jit(solution)/shard_map/ppermute | solution.py:428
  10.7 2.6 %shard_map.183 = (f32[2048,512]{1,0:T(8,128)S(1)}, bf16[2048,256]{1,0:T(8,128)(2,1)S(1)}, s32[1,3072]{1,0:T(1,128)S(1)}, s32[1,3072]{1,0:T(1,128)S(1)}, bf16[512...) custom-call(bf16[512,256]{1,0:T(8,128)(2,1)S(1)} %get-tuple-element.63, ...), custom_call_target="tpu_custom_call" | custom-call | flops 2200000000 | bytes 7119872 | tf_op jit(solution)/shard_map/pallas_call | solution.py:406
  13.4 0.0 collective-permute-done.got_ref
  13.4 0.1 shard_map.184.g0
  13.5 1.4 %collective-permute-start.5 = (bf16[544,256]{1,0:T(8,128)(2,1)S(1)}, bf16[544,256]{1,0:T(8,128)(2,1)S(1)}, u32[]{:S(2)}, u32[]{:S(2)}) collective-permute-start(bf16[544,256]{1,0:T(8,128)(2,1)S(1)} %shard_map.184.g0), channel_id=1, source_target_pairs={{1,2},{2,1},{3,0},{0,3},{5,6},{6,5},{7,4},{4,7},{9,10},{10,9},{11,... | collective-permute-start | bytes 835592 | tf_op jit(solution)/shard_map/ppermute | solution.py:488
  14.9 0.0 collective-permute-done.1.ra
  14.9 0.0 collective-permute-done.2.rb
  14.9 0.0 collective-permute-done.3.rw
  14.9 0.0 collective-permute-done.4.re
  14.9 5.2 %shard_map.185 = (f32[2048,512]{1,0:T(8,128)S(1)}, bf16[512,512]{1,0:T(8,128)(2,1)S(1)}, f32[512,256]{1,0:T(8,128)S(1)}, bf16[512,256]{1,0:T(8,128)(2,1)S(1)}, bf16[2048,256]{1,0:T(8,128)(2,1)S(1)}) custom-call(f32[2048,512]{1,0:T(8,128)S(1)} %get-tuple-element.71.part_ref, bf16[2048,256]{1,0:T(8,128)(2,1)S(1)} %get-tuple-element.72.left_ref, ...), custom_call_target="tpu_custom_call" | custom-call | flops 3200000000 | bytes 13126672 | tf_op jit(solution)/shard_map/pallas_call | solution.py:406
  20.1 0.8 collective-permute-done.5.g1
  20.9 0.1 collective-permute-start.6
  21.0 1.5 %collective-permute-start.7 = (bf16[256,256]{1,0:T(8,128)(2,1)S(1)}, bf16[256,256]{1,0:T(8,128)(2,1)S(1)}, u32[]{:S(2)}, u32[]{:S(2)}) collective-permute-start(bf16[256,256]{1,0:T(8,128)(2,1)S(1)} %get-tuple-element.115), channel_id=1, source_target_pairs={{1,2},{2,1},{3,0},{0,3},{5,6},{6,5},{7,4},{4,7},{9,10},{10,9},{11,... | collective-permute-start | bytes 393224 | tf_op jit(solution)/shard_map/ppermute | solution.py:512
  22.5 2.6 %collective-permute-done.6.near_ref = bf16[256,256]{1,0:T(8,128)(2,1)S(1)} collective-permute-done((bf16[256,256]{1,0:T(8,128)(2,1)S(1)}, bf16[256,256]{1,0:T(8,128)(2,1)S(1)}, u32[]{:S(2)}, u32[]{:S(2)}) %collective-permute-start.6) | collective-permute-done | bytes 131104 | tf_op jit(solution)/shard_map/ppermute | solution.py:511
  25.1 2.7 %collective-permute-done.7.far_ref = bf16[256,256]{1,0:T(8,128)(2,1)S(1)} collective-permute-done((bf16[256,256]{1,0:T(8,128)(2,1)S(1)}, bf16[256,256]{1,0:T(8,128)(2,1)S(1)}, u32[]{:S(2)}, u32[]{:S(2)}) %collective-permute-start.7) | collective-permute-done | bytes 131104 | tf_op jit(solution)/shard_map/ppermute | solution.py:512
  27.8 0.1 shard_map.186
  27.9 0.9 collective-permute-start.8
  28.8 0.0 collective-permute-start.9
  28.8 4.2 %collective-permute-done.8.p1 = bf16[256,256]{1,0:T(8,128)(2,1)S(1)} collective-permute-done((bf16[256,256]{1,0:T(8,128)(2,1)S(1)}, bf16[256,256]{1,0:T(8,128)(2,1)S(1)}, u32[]{:S(2)}, u32[]{:S(2)}) %collective-permute-start.8) | collective-permute-done | bytes 131104 | tf_op jit(solution)/shard_map/ppermute | solution.py:517
  33.0 0.9 collective-permute-done.9.q1
  33.8 14.1 %shard_map.187 = (f32[512,256]{1,0:T(8,128)S(1)}, f32[2,384,128]{2,1,0:T(8,128)S(1)}) custom-call(bf16[256,256]{1,0:T(8,128)(2,1)S(1)} %get-tuple-element.80.p0, bf16[256,256]{1,0:T(8,128)(2,1)S(1)} %collective-permute-done.8.p1, bf16[256,256]{1,0:T(8,128)(2,1)S(1)} %get-tuple-element.81.q0, bf16[256,256]{1,0:T(8,128)(2,1)S(1)} %collective-permute-done.9.q1, ...), custom_call_target="tpu_custom_call" | custom-call | flops 10000000000 | bytes 3075088 | tf_op jit(solution)/shard_map/pallas_call | solution.py:406
  47.9 6.5 %shard_map.188 = (f32[512,256]{1,0:T(8,128)S(1)}, bf16[2176,128]{1,0:T(8,128)(2,1)S(1)}, f32[1920,128]{1,0:T(8,128)S(1)}, bf16[128,256]{1,0:T(8,128)(2,1)S(1)}, ...) custom-call(f32[512,256]{1,0:T(8,128)S(1)} %get-tuple-element.89.grad_fine_ref, ...), custom_call_target="tpu_custom_call" | custom-call | flops 5600000000 | bytes 10535952 | tf_op jit(solution)/shard_map/pallas_call | solution.py:406
  54.4 7.6 %collective-permute-start.11 = (bf16[2176,128]{1,0:T(8,128)(2,1)S(1)}, bf16[2176,128]{1,0:T(8,128)(2,1)S(1)}, u32[]{:S(2)}, u32[]{:S(2)}) collective-permute-start(bf16[2176,128]{1,0:T(8,128)(2,1)S(1)} %get-tuple-element.98), channel_id=1, source_target_pairs={{0,4},{4,0},{1,5},{5,1},{2,6},{6,2},{3,7},{7,3},{8,12},{12,8},{9,1... | collective-permute-start | bytes 1671176 | tf_op jit(solution)/shard_map/ppermute | solution.py:428
  62.1 0.0 collective-permute-start.10
  62.1 3.7 %collective-permute-done.10.from_b = bf16[128,256]{1,0:T(8,128)(2,1)S(1)} collective-permute-done((bf16[128,256]{1,0:T(8,128)(2,1)S(1)}, bf16[128,256]{1,0:T(8,128)(2,1)S(1)}, u32[]{:S(2)}, u32[]{:S(2)}) %collective-permute-start.10) | collective-permute-done | bytes 65568 | tf_op jit(solution)/shard_map/ppermute | solution.py:567
  65.8 0.0 collective-permute-done.11.got_ref.from_core
  65.8 0.7 shard_map.189
  66.4 0.1 collective-permute-start.12
  66.5 2.7 %collective-permute-start.14 = (bf16[640,128]{1,0:T(8,128)(2,1)S(1)}, bf16[640,128]{1,0:T(8,128)(2,1)S(1)}, u32[]{:S(2)}, u32[]{:S(2)}) collective-permute-start(bf16[640,128]{1,0:T(8,128)(2,1)S(1)} %get-tuple-element.104), channel_id=1, source_target_pairs={{0,3},{1,0},{2,1},{3,2},{4,7},{5,4},{6,5},{7,6},{8,11},{9,8},{10,9... | collective-permute-start | bytes 491528 | tf_op jit(solution)/shard_map/ppermute | solution.py:428
  69.2 0.3 collective-permute-start.13
  69.4 4.7 %collective-permute-done.13 = bf16[384,128]{1,0:T(8,128)(2,1)S(1)} collective-permute-done((bf16[384,128]{1,0:T(8,128)(2,1)S(1)}, bf16[384,128]{1,0:T(8,128)(2,1)S(1)}, u32[]{:S(2)}, u32[]{:S(2)}) %collective-permute-start.13) | collective-permute-done | bytes 98336 | tf_op jit(solution)/shard_map/ppermute | solution.py:428
  74.2 0.0 collective-permute-done.12.from_west
  74.2 0.0 collective-permute-done.14.from_east
  74.2 0.1 add_convert_fusion
  74.3 13.4 %all_to_all.10 = bf16[16,48,128]{2,1,0:T(8,128)(2,1)S(1)} all-to-all(bf16[16,48,128]{2,1,0:T(8,128)(2,1)S(1)} %pad_maximum_fusion), channel_id=1, replica_groups=mesh['z'=4,'y'=4,'core'=2,'x'=4] {'z','y'}, dimensions={0} | all-to-all | bytes 393216 | tf_op jit(solution)/shard_map/all_to_all | solution.py:594
  87.7 0.1 broadcast_in_dim.17
  87.8 19.3 %all_to_all.11.mine_ref = bf16[64,48,128]{2,1,0:T(8,128)(2,1)S(1)} all-to-all(bf16[64,48,128]{2,1,0:T(8,128)(2,1)S(1)} %broadcast_in_dim.17), channel_id=1, replica_groups=mesh['z'=4,'y'=4,'core'=2,'x'=4] {'z','y','x'}, dimensions={0} | all-to-all | bytes 1572864 | tf_op jit(solution)/shard_map/all_to_all | solution.py:597
  107.1 3.2 %collective-permute-start.15 = (bf16[64,48,128]{2,1,0:T(8,128)(2,1)S(1)}, bf16[64,48,128]{2,1,0:T(8,128)(2,1)S(1)}, u32[]{:S(2)}, u32[]{:S(2)}) collective-permute-start(bf16[64,48,128]{2,1,0:T(8,128)(2,1)S(1)} %all_to_all.11.mine_ref), channel_id=1, source_target_pairs={{0,4},{4,0},{1,5},{5,1},{2,6},{6,2},{3,7},{7,3},{8,12},{12,8},{9,1... | collective-permute-start | bytes 2359304 | tf_op jit(solution)/shard_map/ppermute | solution.py:428
  110.3 1.7 %shard_map.190 = f32[512,256]{1,0:T(8,128)} custom-call(f32[512,256]{1,0:T(8,128)S(1)} %get-tuple-element.107.local_ref, bf16[2176,128]{1,0:T(8,128)(2,1)S(1)} %collective-permute-done.11.got_ref.from_core, bf16[128,256]{1,0:T(8,128)(2,1)S(1)} %collective-permute-done.10.from_b, bf16[640,128]{1,0:T(8,128)(2,1)S(1)} %collective-permute-done.12.from_west, ...), custom_call_target="tpu_custom_call" | custom-call | flops 200000000 | bytes 1999376 | tf_op jit(solution)/shard_map/pallas_call | solution.py:406
  112.0 0.3 collective-permute-done.15.other_ref
  112.2 2.5 %shard_map.191 = (f32[512,512]{1,0:T(8,128)}, f32[512,256]{1,0:T(8,128)}, f32[512,512]{1,0:T(8,128)}, f32[512,256]{1,0:T(8,128)}) custom-call(bf16[64,48,128]{2,1,0:T(8,128)(2,1)S(1)} %all_to_all.11.mine_ref, bf16[64,48,128]{2,1,0:T(8,128)(2,1)S(1)} %collective-permute-done.15.other_ref, s32[4]{0:T(128)S(1)} %pad_add_fusion.refs_5_.place_ref), custom_call_target="tpu_custom_call" | custom-call | flops 200000000 | bytes 4718608 | tf_op jit(solution)/shard_map/pallas_call | solution.py:406
  (4 shorter events, 0.1 us)
Async XLA Ops:
  3.8 9.6 %collective-permute-start = (bf16[544,256]{1,0:T(8,128)(2,1)S(1)}, bf16[544,256]{1,0:T(8,128)(2,1)S(1)}, u32[]{:S(2)}, u32[]{:S(2)}) collective-permute-start(bf16[544,256]{1,0:T(8,128)(2,1)S(1)} %get-tuple-element.68.mine_ref), channel_id=1, source_target_pairs={{0,1},{1,0},{2,3},{3,2},{4,5},{5,4},{6,7},{7,6},{8,9},{9,8},{10,11... | collective-permute-start | bytes 835592 | tf_op jit(solution)/shard_map/ppermute | solution.py:472
  5.9 9.0 %collective-permute-start.1 = (bf16[128,256]{1,0:T(8,128)(2,1)S(1)}, bf16[128,256]{1,0:T(8,128)(2,1)S(1)}, u32[]{:S(2)}, u32[]{:S(2)}) collective-permute-start(bf16[128,256]{1,0:T(8,128)(2,1)S(1)} %get-tuple-element.73), channel_id=1, source_target_pairs={{0,4},{4,0},{1,5},{5,1},{2,6},{6,2},{3,7},{7,3},{8,12},{12,8},{9,1... | collective-permute-start | bytes 196616 | tf_op jit(solution)/shard_map/ppermute | solution.py:428
  6.9 8.0 %collective-permute-start.2 = (bf16[128,256]{1,0:T(8,128)(2,1)S(1)}, bf16[128,256]{1,0:T(8,128)(2,1)S(1)}, u32[]{:S(2)}, u32[]{:S(2)}) collective-permute-start(bf16[128,256]{1,0:T(8,128)(2,1)S(1)} %get-tuple-element.73), channel_id=1, source_target_pairs={{4,8},{12,16},{20,24},{28,32},{36,40},{44,48},{52,56},{60,64},{68,... | collective-permute-start | bytes 196616 | tf_op jit(solution)/shard_map/ppermute | solution.py:475
  8.1 6.8 %collective-permute-start.3 = (bf16[128,256]{1,0:T(8,128)(2,1)S(1)}, bf16[128,256]{1,0:T(8,128)(2,1)S(1)}, u32[]{:S(2)}, u32[]{:S(2)}) collective-permute-start(bf16[128,256]{1,0:T(8,128)(2,1)S(1)} %get-tuple-element.73), channel_id=1, source_target_pairs={{0,1},{1,2},{2,3},{3,0},{4,5},{5,6},{6,7},{7,4},{8,9},{9,10},{10,1... | collective-permute-start | bytes 196616 | tf_op jit(solution)/shard_map/ppermute | solution.py:428
  8.3 6.6 %collective-permute-start.4 = (bf16[128,256]{1,0:T(8,128)(2,1)S(1)}, bf16[128,256]{1,0:T(8,128)(2,1)S(1)}, u32[]{:S(2)}, u32[]{:S(2)}) collective-permute-start(bf16[128,256]{1,0:T(8,128)(2,1)S(1)} %get-tuple-element.73), channel_id=1, source_target_pairs={{0,3},{1,0},{2,1},{3,2},{4,7},{5,4},{6,5},{7,6},{8,11},{9,8},{10,9... | collective-permute-start | bytes 196616 | tf_op jit(solution)/shard_map/ppermute | solution.py:428
  13.5 7.4 %collective-permute-start.5 = (bf16[544,256]{1,0:T(8,128)(2,1)S(1)}, bf16[544,256]{1,0:T(8,128)(2,1)S(1)}, u32[]{:S(2)}, u32[]{:S(2)}) collective-permute-start(bf16[544,256]{1,0:T(8,128)(2,1)S(1)} %shard_map.184.g0), channel_id=1, source_target_pairs={{1,2},{2,1},{3,0},{0,3},{5,6},{6,5},{7,4},{4,7},{9,10},{10,9},{11,... | collective-permute-start | bytes 835592 | tf_op jit(solution)/shard_map/ppermute | solution.py:488
  20.9 4.2 %collective-permute-start.6 = (bf16[256,256]{1,0:T(8,128)(2,1)S(1)}, bf16[256,256]{1,0:T(8,128)(2,1)S(1)}, u32[]{:S(2)}, u32[]{:S(2)}) collective-permute-start(bf16[256,256]{1,0:T(8,128)(2,1)S(1)} %get-tuple-element.116), channel_id=1, source_target_pairs={{0,1},{1,0},{2,3},{3,2},{4,5},{5,4},{6,7},{7,6},{8,9},{9,8},{10,11... | collective-permute-start | bytes 393224 | tf_op jit(solution)/shard_map/ppermute | solution.py:511
  21.0 6.8 %collective-permute-start.7 = (bf16[256,256]{1,0:T(8,128)(2,1)S(1)}, bf16[256,256]{1,0:T(8,128)(2,1)S(1)}, u32[]{:S(2)}, u32[]{:S(2)}) collective-permute-start(bf16[256,256]{1,0:T(8,128)(2,1)S(1)} %get-tuple-element.115), channel_id=1, source_target_pairs={{1,2},{2,1},{3,0},{0,3},{5,6},{6,5},{7,4},{4,7},{9,10},{10,9},{11,... | collective-permute-start | bytes 393224 | tf_op jit(solution)/shard_map/ppermute | solution.py:512
  27.9 5.1 %collective-permute-start.8 = (bf16[256,256]{1,0:T(8,128)(2,1)S(1)}, bf16[256,256]{1,0:T(8,128)(2,1)S(1)}, u32[]{:S(2)}, u32[]{:S(2)}) collective-permute-start(bf16[256,256]{1,0:T(8,128)(2,1)S(1)} %get-tuple-element.80.p0), channel_id=1, source_target_pairs={{1,2},{2,1},{3,0},{0,3},{5,6},{6,5},{7,4},{4,7},{9,10},{10,9},{11,... | collective-permute-start | bytes 393224 | tf_op jit(solution)/shard_map/ppermute | solution.py:517
  28.8 5.1 %collective-permute-start.9 = (bf16[256,256]{1,0:T(8,128)(2,1)S(1)}, bf16[256,256]{1,0:T(8,128)(2,1)S(1)}, u32[]{:S(2)}, u32[]{:S(2)}) collective-permute-start(bf16[256,256]{1,0:T(8,128)(2,1)S(1)} %get-tuple-element.81.q0), channel_id=1, source_target_pairs={{0,1},{1,0},{2,3},{3,2},{4,5},{5,4},{6,7},{7,6},{8,9},{9,8},{10,11... | collective-permute-start | bytes 393224 | tf_op jit(solution)/shard_map/ppermute | solution.py:517
  54.4 11.3 %collective-permute-start.11 = (bf16[2176,128]{1,0:T(8,128)(2,1)S(1)}, bf16[2176,128]{1,0:T(8,128)(2,1)S(1)}, u32[]{:S(2)}, u32[]{:S(2)}) collective-permute-start(bf16[2176,128]{1,0:T(8,128)(2,1)S(1)} %get-tuple-element.98), channel_id=1, source_target_pairs={{0,4},{4,0},{1,5},{5,1},{2,6},{6,2},{3,7},{7,3},{8,12},{12,8},{9,1... | collective-permute-start | bytes 1671176 | tf_op jit(solution)/shard_map/ppermute | solution.py:428
  62.1 3.7 %collective-permute-start.10 = (bf16[128,256]{1,0:T(8,128)(2,1)S(1)}, bf16[128,256]{1,0:T(8,128)(2,1)S(1)}, u32[]{:S(2)}, u32[]{:S(2)}) collective-permute-start(bf16[128,256]{1,0:T(8,128)(2,1)S(1)} %get-tuple-element.96), channel_id=1, source_target_pairs={{4,8},{12,16},{20,24},{28,32},{36,40},{44,48},{52,56},{60,64},{68,... | collective-permute-start | bytes 196616 | tf_op jit(solution)/shard_map/ppermute | solution.py:567
  66.4 7.7 %collective-permute-start.12 = (bf16[640,128]{1,0:T(8,128)(2,1)S(1)}, bf16[640,128]{1,0:T(8,128)(2,1)S(1)}, u32[]{:S(2)}, u32[]{:S(2)}) collective-permute-start(bf16[640,128]{1,0:T(8,128)(2,1)S(1)} %get-tuple-element.102), channel_id=1, source_target_pairs={{0,1},{1,2},{2,3},{3,0},{4,5},{5,6},{6,7},{7,4},{8,9},{9,10},{10,1... | collective-permute-start | bytes 491528 | tf_op jit(solution)/shard_map/ppermute | solution.py:428
  66.5 7.7 %collective-permute-start.14 = (bf16[640,128]{1,0:T(8,128)(2,1)S(1)}, bf16[640,128]{1,0:T(8,128)(2,1)S(1)}, u32[]{:S(2)}, u32[]{:S(2)}) collective-permute-start(bf16[640,128]{1,0:T(8,128)(2,1)S(1)} %get-tuple-element.104), channel_id=1, source_target_pairs={{0,3},{1,0},{2,1},{3,2},{4,7},{5,4},{6,5},{7,6},{8,11},{9,8},{10,9... | collective-permute-start | bytes 491528 | tf_op jit(solution)/shard_map/ppermute | solution.py:428
  69.2 5.0 %collective-permute-start.13 = (bf16[384,128]{1,0:T(8,128)(2,1)S(1)}, bf16[384,128]{1,0:T(8,128)(2,1)S(1)}, u32[]{:S(2)}, u32[]{:S(2)}) collective-permute-start(bf16[384,128]{1,0:T(8,128)(2,1)S(1)} %get-tuple-element.103), channel_id=1, source_target_pairs={{0,2},{1,3},{2,0},{3,1},{4,6},{5,7},{6,4},{7,5},{8,10},{9,11},{10,... | collective-permute-start | bytes 294920 | tf_op jit(solution)/shard_map/ppermute | solution.py:428
  107.1 5.1 %collective-permute-start.15 = (bf16[64,48,128]{2,1,0:T(8,128)(2,1)S(1)}, bf16[64,48,128]{2,1,0:T(8,128)(2,1)S(1)}, u32[]{:S(2)}, u32[]{:S(2)}) collective-permute-start(bf16[64,48,128]{2,1,0:T(8,128)(2,1)S(1)} %all_to_all.11.mine_ref), channel_id=1, source_target_pairs={{0,4},{4,0},{1,5},{5,1},{2,6},{6,2},{3,7},{7,3},{8,12},{12,8},{9,1... | collective-permute-start | bytes 2359304 | tf_op jit(solution)/shard_map/ppermute | solution.py:428

commit v7 on v6

--- a/solution.py
+++ b/solution.py
@@ -161,9 +161,8 @@
     summed_ref[...] = summed
     _, normed = norm_of(summed)
     fine_new = own_ref[...].astype(F32) + normed * gain_ref[...]
-    high, low = halves(fine_new)
     pool = sum_matrix(assign_ref[...], CNODE)
-    pooled_ref[...] = (dot(pool, high) + dot(pool, low)).astype(BF)
+    pooled_ref[...] = dot(pool, fine_new.astype(BF)).astype(BF)
 
 
 def coarse_kernel(
@@ -220,9 +219,8 @@
         + dot_rt(by_src[...].astype(BF), w1_ref[0:feature, :])
         + dot_rt(by_dst[...].astype(BF), w1_ref[feature:, :])
     )
-    high, low = halves(grad_c0 * weight)
-    spread = pick_matrix(assign_ref[...], CNODE)
-    grad_fine_ref[...] = cot_ref[...].astype(F32) + dot(spread, high) + dot(spread, low)
+    spread = dot(pick_matrix(assign_ref[...], CNODE), (grad_c0 * weight).astype(BF))
+    grad_fine_ref[...] = cot_ref[...].astype(F32) + spread
     own = pl.ds(pl.multiple_of(place_ref[0] * 128, 128), 128)
     for half, rows in enumerate((by_src, by_dst)):
         pack_ref[half, 0:256, :] = dot_lt(table[...], rows[:, own].astype(BF))
@@ -455,7 +453,7 @@
     own, place = lax.optimization_barrier((own, place.astype(jnp.int32)))
     wide = 2 * feature
 
-    rim, pack, target, own_in, src_in, w1_in, w2_in, gain_in, assign_in, export_in = run(
+    rim, pack, target, own_in, src_in, w1_in = run(
         start_kernel,
         [
             ((rim_count, feature), BF),
@@ -466,19 +464,25 @@
         scalars=(5,),
         late=(0, 1, 2, 3, 4),
         inner=(0, 1, 2),
-        ahead=[own, src, fine_w1, fine_w2, fine_gain, assign, export],
+        ahead=[own, src, fine_w1],
     )
     near, far = [(0, 1), (1, 0), (2, 3), (3, 2)], [(1, 2), (2, 1), (3, 0), (0, 3)]
     pack_got = lax.ppermute(pack, "x", near)
     from_west, from_east = send(rim, "x", 1), send(rim, "x", 3)
     from_a = send(rim, "core", 1)
     from_b = lax.ppermute(rim, ROW, between)
-    part, left, csrc_in, cdst_in, cw1_in, cw2_in, cgain_in, cot_in = run(
+    (
+        part, left, csrc_in, cdst_in, cw1_in, cw2_in, cgain_in, cot_in,
+        w2_in, gain_in, assign_in, export_in,
+    ) = run(
         own_kernel,
         [((edges, hidden), F32), ((edges, feature), BF)],
         [own_in, src_in, target, w1_in],
         inner=(0, 1),
-        ahead=[coarse_src, coarse_dst, coarse_w1, coarse_w2, coarse_gain, cot],
+        ahead=[
+            coarse_src, coarse_dst, coarse_w1, coarse_w2, coarse_gain, cot,
+            fine_w2, fine_gain, assign, export,
+        ],
         limit=LIMITS[0],
         work=1.1,
     )
@@ -565,7 +569,6 @@
     )
     from_core = send(give, "core", 1)
     from_b = lax.ppermute(ghost_b, ROW, between)
-    keep, from_b = lax.optimization_barrier((keep, from_b))
     total, coarse_total, to_east, to_cross, to_west = run(
         split_kernel,
         [
@@ -591,6 +594,7 @@
     both = jnp.concatenate(
         [total.reshape(16, 24, 128), coarse_total.reshape(16, 24, 128)], axis=1
     ).astype(BF)
+    both, from_b = lax.optimization_barrier((both, from_b))
     both = lax.all_to_all(both, PLANE, 0, 0, tiled=True)
     both = jnp.sum(both.astype(F32), axis=0).astype(BF)
     copies = jnp.broadcast_to(both[None], (64,) + both.shape)

time: 115 us -> 113 us (0.983)
  blocking collectives: 32.7 us -> 29.7 us
    ppermute x1, waiting for transfers between devices: 3.69 us -> 0.01 us  [shards(): from_b = lax.ppermute(ghost_b, ROW, between)]
    all_to_all x1, blocking collectives: 13.4 us -> 10.2 us  [shards(): both = lax.all_to_all(both, PLANE, 0, 0, tiled=True)]
    ppermute x8, waiting for transfers between devices: 4.98 us -> 7.95 us  [send(): lax.ppermute(value, axis, [(i, (i + step) % size) for i in range(size)])]
  transfers between devices with their start and end apart: 16 -> 16, of which waited for: 8 -> 8; matrix products, arithmetic and copies ran while one was open for 0% -> 0% of each run, Pallas kernels for 8% -> 9%
where the time goes in v7:
time: 113 us; the launch traced here: 112 us
  Pallas kernels  36.1 us (32%)
  blocking collectives  29.7 us (26%)
  starting transfers between devices  24.8 us (22%)
  waiting for transfers between devices  19.9 us (18%)
  between operations  1.43 us (1%)
    pallas_call x10, Pallas kernels, run(): pl.pallas_call(body if copies else kernel, out_shape=shapes, in_specs=[pl...  36.1 us
    all_to_all x1, blocking collectives, shards(): mine = lax.all_to_all(copies, CHIPS, 0, 0, tiled=True)  19.6 us
    ppermute x8, starting transfers between devices, send(): lax.ppermute(value, axis, [(i, (i + step) % size) for i in range(size)])  18.5 us
    all_to_all x1, blocking collectives, shards(): both = lax.all_to_all(both, PLANE, 0, 0, tiled=True)  10.2 us
    ppermute x8, waiting for transfers between devices, send(): lax.ppermute(value, axis, [(i, (i + step) % size) for i in range(size)])  7.95 us
    ppermute x2, waiting for transfers between devices, shards(): got = [lax.ppermute(first, 'x', far), lax.ppermute(second, 'x', near)]  4.84 us
    ppermute x1, waiting for transfers between devices, shards(): lax.ppermute(pooled[:half_rows], 'x', near)  2.99 us
    ppermute x1, waiting for transfers between devices, shards(): lax.ppermute(pooled[half_rows:], 'x', far)  2.65 us
  transfers between devices with their start and end apart: 16, of which 8 were waited for; matrix products, arithmetic and copies ran while one was open for 0% of the time, Pallas kernels for 9%

profile of v7, /device:TPU:1, one launch (start us, length us, event | category | flops | bytes accessed | tf_op | source)
XLA Modules:
  0.0 112.3 jit_solution(4630565810816964410)
XLA Ops:
  1.3 0.1 pad_add_fusion.refs_5_.place_ref
  1.4 2.4 %shard_map.182 = (bf16[128,256]{1,0:T(8,128)(2,1)S(1)}, bf16[544,256]{1,0:T(8,128)(2,1)S(1)}, s32[1,2048]{1,0:T(1,128)S(1)}, bf16[512,256]{1,0:T(8,128)(2,1)S(1)...) custom-call(bf16[512,256]{1,0:T(8,128)(2,1)} %bitcast.15, s32[1,128]{1,0:T(1,128)} %bitcast.26, ...), custom_call_target="tpu_custom_call" | custom-call | flops 200000000 | bytes 1681936 | tf_op jit(solution)/shard_map/pallas_call | solution.py:404
  3.8 2.1 %collective-permute-start = (bf16[544,256]{1,0:T(8,128)(2,1)S(1)}, bf16[544,256]{1,0:T(8,128)(2,1)S(1)}, u32[]{:S(2)}, u32[]{:S(2)}) collective-permute-start(bf16[544,256]{1,0:T(8,128)(2,1)S(1)} %get-tuple-element.68.mine_ref), channel_id=1, source_target_pairs={{0,1},{1,0},{2,3},{3,2},{4,5},{5,4},{6,7},{7,6},{8,9},{9,8},{10,11... | collective-permute-start | bytes 835592 | tf_op jit(solution)/shard_map/ppermute | solution.py:470
  5.9 1.0 collective-permute-start.1
  6.8 1.2 %collective-permute-start.2 = (bf16[128,256]{1,0:T(8,128)(2,1)S(1)}, bf16[128,256]{1,0:T(8,128)(2,1)S(1)}, u32[]{:S(2)}, u32[]{:S(2)}) collective-permute-start(bf16[128,256]{1,0:T(8,128)(2,1)S(1)} %get-tuple-element.73), channel_id=1, source_target_pairs={{4,8},{12,16},{20,24},{28,32},{36,40},{44,48},{52,56},{60,64},{68,... | collective-permute-start | bytes 196616 | tf_op jit(solution)/shard_map/ppermute | solution.py:473
  8.0 0.3 collective-permute-start.3
  8.3 2.4 %collective-permute-start.4 = (bf16[128,256]{1,0:T(8,128)(2,1)S(1)}, bf16[128,256]{1,0:T(8,128)(2,1)S(1)}, u32[]{:S(2)}, u32[]{:S(2)}) collective-permute-start(bf16[128,256]{1,0:T(8,128)(2,1)S(1)} %get-tuple-element.73), channel_id=1, source_target_pairs={{0,3},{1,0},{2,1},{3,2},{4,7},{5,4},{6,5},{7,6},{8,11},{9,8},{10,9... | collective-permute-start | bytes 196616 | tf_op jit(solution)/shard_map/ppermute | solution.py:426
  10.7 3.4 %shard_map.183 = (f32[2048,512]{1,0:T(8,128)S(1)}, bf16[2048,256]{1,0:T(8,128)(2,1)S(1)}, s32[1,3072]{1,0:T(1,128)S(1)}, s32[1,3072]{1,0:T(1,128)S(1)}, bf16[512...) custom-call(bf16[512,256]{1,0:T(8,128)(2,1)S(1)} %get-tuple-element., ...), custom_call_target="tpu_custom_call" | custom-call | flops 2200000000 | bytes 7385600 | tf_op jit(solution)/shard_map/pallas_call | solution.py:404
  14.2 0.0 collective-permute-done.got_ref
  14.2 0.1 shard_map.184.g0
  14.2 0.7 collective-permute-start.5
  14.9 0.0 collective-permute-done.1.ra
  14.9 0.0 collective-permute-done.2.rb
  14.9 0.0 collective-permute-done.3.rw
  14.9 0.0 collective-permute-done.4.re
  14.9 4.8 %shard_map.185 = (f32[2048,512]{1,0:T(8,128)S(1)}, bf16[512,512]{1,0:T(8,128)(2,1)S(1)}, f32[512,256]{1,0:T(8,128)S(1)}, bf16[512,256]{1,0:T(8,128)(2,1)S(1)}, bf16[2048,256]{1,0:T(8,128)(2,1)S(1)}) custom-call(f32[2048,512]{1,0:T(8,128)S(1)} %get-tuple-element.71.part_ref, bf16[2048,256]{1,0:T(8,128)(2,1)S(1)} %get-tuple-element.72.left_ref, ...), custom_call_target="tpu_custom_call" | custom-call | flops 3200000000 | bytes 13126672 | tf_op jit(solution)/shard_map/pallas_call | solution.py:404
  19.8 1.4 %collective-permute-done.5.g1 = bf16[544,256]{1,0:T(8,128)(2,1)S(1)} collective-permute-done((bf16[544,256]{1,0:T(8,128)(2,1)S(1)}, bf16[544,256]{1,0:T(8,128)(2,1)S(1)}, u32[]{:S(2)}, u32[]{:S(2)}) %collective-permute-start.5) | collective-permute-done | bytes 278560 | tf_op jit(solution)/shard_map/ppermute | solution.py:492
  21.2 0.1 collective-permute-start.6
  21.3 1.1 collective-permute-start.7
  22.4 3.0 %collective-permute-done.6.near_ref = bf16[256,256]{1,0:T(8,128)(2,1)S(1)} collective-permute-done((bf16[256,256]{1,0:T(8,128)(2,1)S(1)}, bf16[256,256]{1,0:T(8,128)(2,1)S(1)}, u32[]{:S(2)}, u32[]{:S(2)}) %collective-permute-start.6) | collective-permute-done | bytes 131104 | tf_op jit(solution)/shard_map/ppermute | solution.py:515
  25.4 2.7 %collective-permute-done.7.far_ref = bf16[256,256]{1,0:T(8,128)(2,1)S(1)} collective-permute-done((bf16[256,256]{1,0:T(8,128)(2,1)S(1)}, bf16[256,256]{1,0:T(8,128)(2,1)S(1)}, u32[]{:S(2)}, u32[]{:S(2)}) %collective-permute-start.7) | collective-permute-done | bytes 131104 | tf_op jit(solution)/shard_map/ppermute | solution.py:516
  28.1 0.1 shard_map.186
  28.1 1.2 %collective-permute-start.8 = (bf16[256,256]{1,0:T(8,128)(2,1)S(1)}, bf16[256,256]{1,0:T(8,128)(2,1)S(1)}, u32[]{:S(2)}, u32[]{:S(2)}) collective-permute-start(bf16[256,256]{1,0:T(8,128)(2,1)S(1)} %get-tuple-element.80.p0), channel_id=1, source_target_pairs={{1,2},{2,1},{3,0},{0,3},{5,6},{6,5},{7,4},{4,7},{9,10},{10,9},{11,... | collective-permute-start | bytes 393224 | tf_op jit(solution)/shard_map/ppermute | solution.py:521
  29.3 0.0 collective-permute-start.9
  29.3 3.9 %collective-permute-done.8.p1 = bf16[256,256]{1,0:T(8,128)(2,1)S(1)} collective-permute-done((bf16[256,256]{1,0:T(8,128)(2,1)S(1)}, bf16[256,256]{1,0:T(8,128)(2,1)S(1)}, u32[]{:S(2)}, u32[]{:S(2)}) %collective-permute-start.8) | collective-permute-done | bytes 131104 | tf_op jit(solution)/shard_map/ppermute | solution.py:521
  33.3 0.9 collective-permute-done.9.q1
  34.2 14.0 %shard_map.187 = (f32[512,256]{1,0:T(8,128)S(1)}, f32[2,384,128]{2,1,0:T(8,128)S(1)}) custom-call(bf16[256,256]{1,0:T(8,128)(2,1)S(1)} %get-tuple-element.80.p0, bf16[256,256]{1,0:T(8,128)(2,1)S(1)} %collective-permute-done.8.p1, bf16[256,256]{1,0:T(8,128)(2,1)S(1)} %get-tuple-element.81.q0, bf16[256,256]{1,0:T(8,128)(2,1)S(1)} %collective-permute-done.9.q1, ...), custom_call_target="tpu_custom_call" | custom-call | flops 10000000000 | bytes 3075088 | tf_op jit(solution)/shard_map/pallas_call | solution.py:404
  48.1 6.5 %shard_map.188 = (f32[512,256]{1,0:T(8,128)S(1)}, bf16[2176,128]{1,0:T(8,128)(2,1)S(1)}, f32[1920,128]{1,0:T(8,128)S(1)}, bf16[128,256]{1,0:T(8,128)(2,1)S(1)}, ...) custom-call(f32[512,256]{1,0:T(8,128)S(1)} %get-tuple-element.89.grad_fine_ref, ...), custom_call_target="tpu_custom_call" | custom-call | flops 5600000000 | bytes 10535952 | tf_op jit(solution)/shard_map/pallas_call | solution.py:404
  54.6 8.1 %collective-permute-start.10 = (bf16[2176,128]{1,0:T(8,128)(2,1)S(1)}, bf16[2176,128]{1,0:T(8,128)(2,1)S(1)}, u32[]{:S(2)}, u32[]{:S(2)}) collective-permute-start(bf16[2176,128]{1,0:T(8,128)(2,1)S(1)} %get-tuple-element.96), channel_id=1, source_target_pairs={{0,4},{4,0},{1,5},{5,1},{2,6},{6,2},{3,7},{7,3},{8,12},{12,8},{9,1... | collective-permute-start | bytes 1671176 | tf_op jit(solution)/shard_map/ppermute | solution.py:426
  62.7 1.6 %collective-permute-done.10.got_ref.from_core = bf16[2176,128]{1,0:T(8,128)(2,1)S(1)} collective-permute-done((bf16[2176,128]{1,0:T(8,128)(2,1)S(1)}, bf16[2176,128]{1,0:T(8,128)(2,1)S(1)}, u32[]{:S(2)}, u32[]{:S(2)}) %collective-permute-start.10) | collective-permute-done | bytes 557088 | tf_op jit(solution)/shard_map/ppermute | solution.py:426
  64.3 0.7 shard_map.189
  65.0 0.1 collective-permute-start.11
  65.0 2.7 %collective-permute-start.13 = (bf16[640,128]{1,0:T(8,128)(2,1)S(1)}, bf16[640,128]{1,0:T(8,128)(2,1)S(1)}, u32[]{:S(2)}, u32[]{:S(2)}) collective-permute-start(bf16[640,128]{1,0:T(8,128)(2,1)S(1)} %get-tuple-element.102), channel_id=1, source_target_pairs={{0,3},{1,0},{2,1},{3,2},{4,7},{5,4},{6,5},{7,6},{8,11},{9,8},{10,9... | collective-permute-start | bytes 491528 | tf_op jit(solution)/shard_map/ppermute | solution.py:426
  67.7 0.3 collective-permute-start.12
  68.0 0.0 collective-permute-start.14
  68.0 6.1 %collective-permute-done.12 = bf16[384,128]{1,0:T(8,128)(2,1)S(1)} collective-permute-done((bf16[384,128]{1,0:T(8,128)(2,1)S(1)}, bf16[384,128]{1,0:T(8,128)(2,1)S(1)}, u32[]{:S(2)}, u32[]{:S(2)}) %collective-permute-start.12) | collective-permute-done | bytes 98336 | tf_op jit(solution)/shard_map/ppermute | solution.py:426
  74.1 0.0 collective-permute-done.11.from_west
  74.1 0.0 collective-permute-done.13.from_east
  74.1 0.1 add_convert_fusion
  74.2 0.0 collective-permute-done.14.from_b
  74.2 10.2 %all_to_all.10 = bf16[16,48,128]{2,1,0:T(8,128)(2,1)S(1)} all-to-all(bf16[16,48,128]{2,1,0:T(8,128)(2,1)S(1)} %pad_maximum_fusion), channel_id=1, replica_groups=mesh['z'=4,'y'=4,'core'=2,'x'=4] {'z','y'}, dimensions={0} | all-to-all | bytes 393216 | tf_op jit(solution)/shard_map/all_to_all | solution.py:598
  84.4 0.1 broadcast_in_dim.17
  84.5 19.6 %all_to_all.11.mine_ref = bf16[64,48,128]{2,1,0:T(8,128)(2,1)S(1)} all-to-all(bf16[64,48,128]{2,1,0:T(8,128)(2,1)S(1)} %broadcast_in_dim.17), channel_id=1, replica_groups=mesh['z'=4,'y'=4,'core'=2,'x'=4] {'z','y','x'}, dimensions={0} | all-to-all | bytes 1572864 | tf_op jit(solution)/shard_map/all_to_all | solution.py:601
  104.1 3.7 %collective-permute-start.15 = (bf16[64,48,128]{2,1,0:T(8,128)(2,1)S(1)}, bf16[64,48,128]{2,1,0:T(8,128)(2,1)S(1)}, u32[]{:S(2)}, u32[]{:S(2)}) collective-permute-start(bf16[64,48,128]{2,1,0:T(8,128)(2,1)S(1)} %all_to_all.11.mine_ref), channel_id=1, source_target_pairs={{0,4},{4,0},{1,5},{5,1},{2,6},{6,2},{3,7},{7,3},{8,12},{12,8},{9,1... | collective-permute-start | bytes 2359304 | tf_op jit(solution)/shard_map/ppermute | solution.py:426
  107.8 1.7 %shard_map.190 = f32[512,256]{1,0:T(8,128)} custom-call(f32[512,256]{1,0:T(8,128)S(1)} %get-tuple-element.107.local_ref, bf16[2176,128]{1,0:T(8,128)(2,1)S(1)} %collective-permute-done.10.got_ref.from_core, bf16[128,256]{1,0:T(8,128)(2,1)S(1)} %collective-permute-done.14.from_b, bf16[640,128]{1,0:T(8,128)(2,1)S(1)} %collective-permute-done.11.from_west, ...), custom_call_target="tpu_custom_call" | custom-call | flops 200000000 | bytes 1999376 | tf_op jit(solution)/shard_map/pallas_call | solution.py:404
  109.5 0.3 collective-permute-done.15.other_ref
  109.7 2.5 %shard_map.191 = (f32[512,512]{1,0:T(8,128)}, f32[512,256]{1,0:T(8,128)}, f32[512,512]{1,0:T(8,128)}, f32[512,256]{1,0:T(8,128)}) custom-call(bf16[64,48,128]{2,1,0:T(8,128)(2,1)S(1)} %all_to_all.11.mine_ref, bf16[64,48,128]{2,1,0:T(8,128)(2,1)S(1)} %collective-permute-done.15.other_ref, s32[4]{0:T(128)S(1)} %pad_add_fusion.refs_5_.place_ref), custom_call_target="tpu_custom_call" | custom-call | flops 200000000 | bytes 4718608 | tf_op jit(solution)/shard_map/pallas_call | solution.py:404
  (4 shorter events, 0.1 us)
Async XLA Ops:
  3.8 10.4 %collective-permute-start = (bf16[544,256]{1,0:T(8,128)(2,1)S(1)}, bf16[544,256]{1,0:T(8,128)(2,1)S(1)}, u32[]{:S(2)}, u32[]{:S(2)}) collective-permute-start(bf16[544,256]{1,0:T(8,128)(2,1)S(1)} %get-tuple-element.68.mine_ref), channel_id=1, source_target_pairs={{0,1},{1,0},{2,3},{3,2},{4,5},{5,4},{6,7},{7,6},{8,9},{9,8},{10,11... | collective-permute-start | bytes 835592 | tf_op jit(solution)/shard_map/ppermute | solution.py:470
  5.9 9.1 %collective-permute-start.1 = (bf16[128,256]{1,0:T(8,128)(2,1)S(1)}, bf16[128,256]{1,0:T(8,128)(2,1)S(1)}, u32[]{:S(2)}, u32[]{:S(2)}) collective-permute-start(bf16[128,256]{1,0:T(8,128)(2,1)S(1)} %get-tuple-element.73), channel_id=1, source_target_pairs={{0,4},{4,0},{1,5},{5,1},{2,6},{6,2},{3,7},{7,3},{8,12},{12,8},{9,1... | collective-permute-start | bytes 196616 | tf_op jit(solution)/shard_map/ppermute | solution.py:426
  6.8 8.1 %collective-permute-start.2 = (bf16[128,256]{1,0:T(8,128)(2,1)S(1)}, bf16[128,256]{1,0:T(8,128)(2,1)S(1)}, u32[]{:S(2)}, u32[]{:S(2)}) collective-permute-start(bf16[128,256]{1,0:T(8,128)(2,1)S(1)} %get-tuple-element.73), channel_id=1, source_target_pairs={{4,8},{12,16},{20,24},{28,32},{36,40},{44,48},{52,56},{60,64},{68,... | collective-permute-start | bytes 196616 | tf_op jit(solution)/shard_map/ppermute | solution.py:473
  8.0 6.9 %collective-permute-start.3 = (bf16[128,256]{1,0:T(8,128)(2,1)S(1)}, bf16[128,256]{1,0:T(8,128)(2,1)S(1)}, u32[]{:S(2)}, u32[]{:S(2)}) collective-permute-start(bf16[128,256]{1,0:T(8,128)(2,1)S(1)} %get-tuple-element.73), channel_id=1, source_target_pairs={{0,1},{1,2},{2,3},{3,0},{4,5},{5,6},{6,7},{7,4},{8,9},{9,10},{10,1... | collective-permute-start | bytes 196616 | tf_op jit(solution)/shard_map/ppermute | solution.py:426
  8.3 6.7 %collective-permute-start.4 = (bf16[128,256]{1,0:T(8,128)(2,1)S(1)}, bf16[128,256]{1,0:T(8,128)(2,1)S(1)}, u32[]{:S(2)}, u32[]{:S(2)}) collective-permute-start(bf16[128,256]{1,0:T(8,128)(2,1)S(1)} %get-tuple-element.73), channel_id=1, source_target_pairs={{0,3},{1,0},{2,1},{3,2},{4,7},{5,4},{6,5},{7,6},{8,11},{9,8},{10,9... | collective-permute-start | bytes 196616 | tf_op jit(solution)/shard_map/ppermute | solution.py:426
  14.2 7.0 %collective-permute-start.5 = (bf16[544,256]{1,0:T(8,128)(2,1)S(1)}, bf16[544,256]{1,0:T(8,128)(2,1)S(1)}, u32[]{:S(2)}, u32[]{:S(2)}) collective-permute-start(bf16[544,256]{1,0:T(8,128)(2,1)S(1)} %shard_map.184.g0), channel_id=1, source_target_pairs={{1,2},{2,1},{3,0},{0,3},{5,6},{6,5},{7,4},{4,7},{9,10},{10,9},{11,... | collective-permute-start | bytes 835592 | tf_op jit(solution)/shard_map/ppermute | solution.py:492
  21.2 4.2 %collective-permute-start.6 = (bf16[256,256]{1,0:T(8,128)(2,1)S(1)}, bf16[256,256]{1,0:T(8,128)(2,1)S(1)}, u32[]{:S(2)}, u32[]{:S(2)}) collective-permute-start(bf16[256,256]{1,0:T(8,128)(2,1)S(1)} %get-tuple-element.116), channel_id=1, source_target_pairs={{0,1},{1,0},{2,3},{3,2},{4,5},{5,4},{6,7},{7,6},{8,9},{9,8},{10,11... | collective-permute-start | bytes 393224 | tf_op jit(solution)/shard_map/ppermute | solution.py:515
  21.3 6.8 %collective-permute-start.7 = (bf16[256,256]{1,0:T(8,128)(2,1)S(1)}, bf16[256,256]{1,0:T(8,128)(2,1)S(1)}, u32[]{:S(2)}, u32[]{:S(2)}) collective-permute-start(bf16[256,256]{1,0:T(8,128)(2,1)S(1)} %get-tuple-element.115), channel_id=1, source_target_pairs={{1,2},{2,1},{3,0},{0,3},{5,6},{6,5},{7,4},{4,7},{9,10},{10,9},{11,... | collective-permute-start | bytes 393224 | tf_op jit(solution)/shard_map/ppermute | solution.py:516
  28.1 5.1 %collective-permute-start.8 = (bf16[256,256]{1,0:T(8,128)(2,1)S(1)}, bf16[256,256]{1,0:T(8,128)(2,1)S(1)}, u32[]{:S(2)}, u32[]{:S(2)}) collective-permute-start(bf16[256,256]{1,0:T(8,128)(2,1)S(1)} %get-tuple-element.80.p0), channel_id=1, source_target_pairs={{1,2},{2,1},{3,0},{0,3},{5,6},{6,5},{7,4},{4,7},{9,10},{10,9},{11,... | collective-permute-start | bytes 393224 | tf_op jit(solution)/shard_map/ppermute | solution.py:521
  29.3 4.8 %collective-permute-start.9 = (bf16[256,256]{1,0:T(8,128)(2,1)S(1)}, bf16[256,256]{1,0:T(8,128)(2,1)S(1)}, u32[]{:S(2)}, u32[]{:S(2)}) collective-permute-start(bf16[256,256]{1,0:T(8,128)(2,1)S(1)} %get-tuple-element.81.q0), channel_id=1, source_target_pairs={{0,1},{1,0},{2,3},{3,2},{4,5},{5,4},{6,7},{7,6},{8,9},{9,8},{10,11... | collective-permute-start | bytes 393224 | tf_op jit(solution)/shard_map/ppermute | solution.py:521
  54.6 9.7 %collective-permute-start.10 = (bf16[2176,128]{1,0:T(8,128)(2,1)S(1)}, bf16[2176,128]{1,0:T(8,128)(2,1)S(1)}, u32[]{:S(2)}, u32[]{:S(2)}) collective-permute-start(bf16[2176,128]{1,0:T(8,128)(2,1)S(1)} %get-tuple-element.96), channel_id=1, source_target_pairs={{0,4},{4,0},{1,5},{5,1},{2,6},{6,2},{3,7},{7,3},{8,12},{12,8},{9,1... | collective-permute-start | bytes 1671176 | tf_op jit(solution)/shard_map/ppermute | solution.py:426
  65.0 9.1 %collective-permute-start.11 = (bf16[640,128]{1,0:T(8,128)(2,1)S(1)}, bf16[640,128]{1,0:T(8,128)(2,1)S(1)}, u32[]{:S(2)}, u32[]{:S(2)}) collective-permute-start(bf16[640,128]{1,0:T(8,128)(2,1)S(1)} %get-tuple-element.100), channel_id=1, source_target_pairs={{0,1},{1,2},{2,3},{3,0},{4,5},{5,6},{6,7},{7,4},{8,9},{9,10},{10,1... | collective-permute-start | bytes 491528 | tf_op jit(solution)/shard_map/ppermute | solution.py:426
  65.0 9.1 %collective-permute-start.13 = (bf16[640,128]{1,0:T(8,128)(2,1)S(1)}, bf16[640,128]{1,0:T(8,128)(2,1)S(1)}, u32[]{:S(2)}, u32[]{:S(2)}) collective-permute-start(bf16[640,128]{1,0:T(8,128)(2,1)S(1)} %get-tuple-element.102), channel_id=1, source_target_pairs={{0,3},{1,0},{2,1},{3,2},{4,7},{5,4},{6,5},{7,6},{8,11},{9,8},{10,9... | collective-permute-start | bytes 491528 | tf_op jit(solution)/shard_map/ppermute | solution.py:426
  67.7 6.4 %collective-permute-start.12 = (bf16[384,128]{1,0:T(8,128)(2,1)S(1)}, bf16[384,128]{1,0:T(8,128)(2,1)S(1)}, u32[]{:S(2)}, u32[]{:S(2)}) collective-permute-start(bf16[384,128]{1,0:T(8,128)(2,1)S(1)} %get-tuple-element.101), channel_id=1, source_target_pairs={{0,2},{1,3},{2,0},{3,1},{4,6},{5,7},{6,4},{7,5},{8,10},{9,11},{10,... | collective-permute-start | bytes 294920 | tf_op jit(solution)/shard_map/ppermute | solution.py:426
  68.0 6.2 %collective-permute-start.14 = (bf16[128,256]{1,0:T(8,128)(2,1)S(1)}, bf16[128,256]{1,0:T(8,128)(2,1)S(1)}, u32[]{:S(2)}, u32[]{:S(2)}) collective-permute-start(bf16[128,256]{1,0:T(8,128)(2,1)S(1)} %get-tuple-element.104), channel_id=1, source_target_pairs={{4,8},{12,16},{20,24},{28,32},{36,40},{44,48},{52,56},{60,64},{68,... | collective-permute-start | bytes 196616 | tf_op jit(solution)/shard_map/ppermute | solution.py:571
  104.1 5.7 %collective-permute-start.15 = (bf16[64,48,128]{2,1,0:T(8,128)(2,1)S(1)}, bf16[64,48,128]{2,1,0:T(8,128)(2,1)S(1)}, u32[]{:S(2)}, u32[]{:S(2)}) collective-permute-start(bf16[64,48,128]{2,1,0:T(8,128)(2,1)S(1)} %all_to_all.11.mine_ref), channel_id=1, source_target_pairs={{0,4},{4,0},{1,5},{5,1},{2,6},{6,2},{3,7},{7,3},{8,12},{12,8},{9,1... | collective-permute-start | bytes 2359304 | tf_op jit(solution)/shard_map/ppermute | solution.py:426

commit v8 on v6

--- a/solution.py
+++ b/solution.py
@@ -110,11 +110,9 @@
     out_ref[CNODE + 16 : CNODE + 32, :] = packed[:, 256:]
 
 
-def pair_kernel(mine_ref, near_ref, far_ref, first_ref, second_ref):
-    half = near_ref.shape[0]
-    mine = mine_ref[...].astype(F32)
-    first_ref[...] = (mine[0:half] + near_ref[...].astype(F32)).astype(BF)
-    second_ref[...] = (mine[half:] + far_ref[...].astype(F32)).astype(BF)
+def pair_kernel(upper_ref, near_ref, lower_ref, far_ref, first_ref, second_ref):
+    first_ref[...] = (upper_ref[...].astype(F32) + near_ref[...].astype(F32)).astype(BF)
+    second_ref[...] = (lower_ref[...].astype(F32) + far_ref[...].astype(F32)).astype(BF)
 
 
 def own_kernel(own_ref, src_ref, target_ref, w1_ref, part_ref, left_ref):
@@ -129,7 +127,7 @@
 
 def fine_forward_kernel(
     part_ref, left_ref, own_ref, ra, rb, rw, re, src_ref, target_ref, place_ref,
-    w1_ref, w2_ref, gain_ref, assign_ref, slope_ref, acc_out, summed_ref, pooled_ref, pair_ref, table, acc,
+    w1_ref, w2_ref, gain_ref, assign_ref, slope_ref, acc_out, summed_ref, upper_ref, lower_ref, pair_ref, table, acc,
 ):
     nodes, feature = own_ref.shape
     rim = ra.shape[0]
@@ -161,9 +159,10 @@
     summed_ref[...] = summed
     _, normed = norm_of(summed)
     fine_new = own_ref[...].astype(F32) + normed * gain_ref[...]
-    high, low = halves(fine_new)
     pool = sum_matrix(assign_ref[...], CNODE)
-    pooled_ref[...] = (dot(pool, high) + dot(pool, low)).astype(BF)
+    pooled = dot(pool, fine_new.astype(BF)).astype(BF)
+    upper_ref[...] = pooled[0 : CNODE // 2, :]
+    lower_ref[...] = pooled[CNODE // 2 :, :]
 
 
 def coarse_kernel(
@@ -220,9 +219,8 @@
         + dot_rt(by_src[...].astype(BF), w1_ref[0:feature, :])
         + dot_rt(by_dst[...].astype(BF), w1_ref[feature:, :])
     )
-    high, low = halves(grad_c0 * weight)
-    spread = pick_matrix(assign_ref[...], CNODE)
-    grad_fine_ref[...] = cot_ref[...].astype(F32) + dot(spread, high) + dot(spread, low)
+    spread = dot(pick_matrix(assign_ref[...], CNODE), (grad_c0 * weight).astype(BF))
+    grad_fine_ref[...] = cot_ref[...].astype(F32) + spread
     own = pl.ds(pl.multiple_of(place_ref[0] * 128, 128), 128)
     for half, rows in enumerate((by_src, by_dst)):
         pack_ref[half, 0:256, :] = dot_lt(table[...], rows[:, own].astype(BF))
@@ -486,13 +484,14 @@
     (pair,) = run(add_kernel, [((CNODE + 32, feature), BF)], [pack, pack_got], inner=(0,))
     pair, part = lax.optimization_barrier((pair, part))
     pair_got = lax.ppermute(pair, "x", far)
-    slope, acc, summed, pooled, left = run(
+    slope, acc, summed, upper, lower, left = run(
         fine_forward_kernel,
         [
             ((edges, hidden), F32),
             ((nodes, hidden), BF),
             ((nodes, feature), F32),
-            ((CNODE, feature), BF),
+            ((CNODE // 2, feature), BF),
+            ((CNODE // 2, feature), BF),
             ((edges, feature), BF),
         ],
         [
@@ -501,18 +500,18 @@
         ],
         [((nodes + 4 * rim_count, feature), BF), ((nodes, hidden), F32)],
         scalars=(9,),
-        inner=(0, 1, 2, 3, 4),
+        inner=(0, 1, 2, 3, 4, 5),
         limit=LIMITS[1],
         work=1.6,
     )
-    pooled, pair_got = lax.optimization_barrier((pooled, pair_got))
-    half_rows = CNODE // 2
-    got = [
-        lax.ppermute(pooled[:half_rows], "x", near),
-        lax.ppermute(pooled[half_rows:], "x", far),
-    ]
+    upper, lower, pair_got = lax.optimization_barrier((upper, lower, pair_got))
+    near_got = lax.ppermute(upper, "x", near)
+    far_got = lax.ppermute(lower, "x", far)
     first, second = run(
-        pair_kernel, [((half_rows, feature), BF)] * 2, [pooled, *got], inner=(0, 1)
+        pair_kernel,
+        [((CNODE // 2, feature), BF)] * 2,
+        [upper, near_got, lower, far_got],
+        inner=(0, 1),
     )
     got = [lax.ppermute(first, "x", far), lax.ppermute(second, "x", near)]
 
@@ -565,7 +564,6 @@
     )
     from_core = send(give, "core", 1)
     from_b = lax.ppermute(ghost_b, ROW, between)
-    keep, from_b = lax.optimization_barrier((keep, from_b))
     total, coarse_total, to_east, to_cross, to_west = run(
         split_kernel,
         [
@@ -591,6 +589,7 @@
     both = jnp.concatenate(
         [total.reshape(16, 24, 128), coarse_total.reshape(16, 24, 128)], axis=1
     ).astype(BF)
+    both, from_b = lax.optimization_barrier((both, from_b))
     both = lax.all_to_all(both, PLANE, 0, 0, tiled=True)
     both = jnp.sum(both.astype(F32), axis=0).astype(BF)
     copies = jnp.broadcast_to(both[None], (64,) + both.shape)

time: 115 us -> 112 us (0.974)
  blocking collectives: 32.7 us -> 31.1 us
    ppermute x1, waiting for transfers between devices: 3.69 us -> 0.01 us  [shards(): from_b = lax.ppermute(ghost_b, ROW, between)]
    ppermute x8, waiting for transfers between devices: 4.98 us -> 7.86 us  [send(): lax.ppermute(value, axis, [(i, (i + step) % size) for i in range(size)])]
    all_to_all x1, blocking collectives: 13.4 us -> 11.5 us  [shards(): both = lax.all_to_all(both, PLANE, 0, 0, tiled=True)]
where the time goes in v8:
time: 112 us
  Pallas kernels  35.3 us (32%)
  blocking collectives  31.1 us (28%)
  starting transfers between devices  24.5 us (22%)
  waiting for transfers between devices  19.5 us (17%)
  between operations  1.42 us (1%)
    pallas_call x10, Pallas kernels, run(): pl.pallas_call(body if copies else kernel, out_shape=shapes, in_specs=[pl...  35.3 us
    all_to_all x1, blocking collectives, shards(): mine = lax.all_to_all(copies, CHIPS, 0, 0, tiled=True)  19.6 us
    ppermute x8, starting transfers between devices, send(): lax.ppermute(value, axis, [(i, (i + step) % size) for i in range(size)])  17.2 us
    all_to_all x1, blocking collectives, shards(): both = lax.all_to_all(both, PLANE, 0, 0, tiled=True)  11.5 us
    ppermute x8, waiting for transfers between devices, send(): lax.ppermute(value, axis, [(i, (i + step) % size) for i in range(size)])  7.86 us
    ppermute x2, waiting for transfers between devices, shards(): got = [lax.ppermute(first, 'x', far), lax.ppermute(second, 'x', near)]  5.22 us
    ppermute x1, waiting for transfers between devices, shards(): near_got = lax.ppermute(upper, 'x', near)  2.68 us
    ppermute x1, waiting for transfers between devices, shards(): far_got = lax.ppermute(lower, 'x', far)  2.59 us
  transfers between devices with their start and end apart: 16, of which 8 were waited for; matrix products, arithmetic and copies ran while one was open for 0% of the time, Pallas kernels for 8%

profile of v8, /device:TPU:1, one launch (start us, length us, event | category | flops | bytes accessed | tf_op | source)
XLA Modules:
  0.0 112.1 jit_solution(14595649137832001285)
XLA Ops:
  1.3 0.1 pad_add_fusion.refs_5_.place_ref
  1.4 2.4 %shard_map.182 = (bf16[128,256]{1,0:T(8,128)(2,1)S(1)}, bf16[544,256]{1,0:T(8,128)(2,1)S(1)}, s32[1,2048]{1,0:T(1,128)S(1)}, bf16[512,256]{1,0:T(8,128)(2,1)S(1)...) custom-call(bf16[512,256]{1,0:T(8,128)(2,1)} %bitcast.15, ...), custom_call_target="tpu_custom_call" | custom-call | flops 200000000 | bytes 1947664 | tf_op jit(solution)/shard_map/pallas_call | solution.py:404
  3.8 2.1 %collective-permute-start = (bf16[544,256]{1,0:T(8,128)(2,1)S(1)}, bf16[544,256]{1,0:T(8,128)(2,1)S(1)}, u32[]{:S(2)}, u32[]{:S(2)}) collective-permute-start(bf16[544,256]{1,0:T(8,128)(2,1)S(1)} %get-tuple-element.70.mine_ref), channel_id=1, source_target_pairs={{0,1},{1,0},{2,3},{3,2},{4,5},{5,4},{6,7},{7,6},{8,9},{9,8},{10,11... | collective-permute-start | bytes 835592 | tf_op jit(solution)/shard_map/ppermute | solution.py:470
  5.9 1.0 collective-permute-start.1
  6.9 1.2 %collective-permute-start.2 = (bf16[128,256]{1,0:T(8,128)(2,1)S(1)}, bf16[128,256]{1,0:T(8,128)(2,1)S(1)}, u32[]{:S(2)}, u32[]{:S(2)}) collective-permute-start(bf16[128,256]{1,0:T(8,128)(2,1)S(1)} %get-tuple-element.75), channel_id=1, source_target_pairs={{4,8},{12,16},{20,24},{28,32},{36,40},{44,48},{52,56},{60,64},{68,... | collective-permute-start | bytes 196616 | tf_op jit(solution)/shard_map/ppermute | solution.py:473
  8.1 0.3 collective-permute-start.3
  8.3 2.4 %collective-permute-start.4 = (bf16[128,256]{1,0:T(8,128)(2,1)S(1)}, bf16[128,256]{1,0:T(8,128)(2,1)S(1)}, u32[]{:S(2)}, u32[]{:S(2)}) collective-permute-start(bf16[128,256]{1,0:T(8,128)(2,1)S(1)} %get-tuple-element.75), channel_id=1, source_target_pairs={{0,3},{1,0},{2,1},{3,2},{4,7},{5,4},{6,5},{7,6},{8,11},{9,8},{10,9... | collective-permute-start | bytes 196616 | tf_op jit(solution)/shard_map/ppermute | solution.py:426
  10.7 2.6 %shard_map.183 = (f32[2048,512]{1,0:T(8,128)S(1)}, bf16[2048,256]{1,0:T(8,128)(2,1)S(1)}, s32[1,3072]{1,0:T(1,128)S(1)}, s32[1,3072]{1,0:T(1,128)S(1)}, bf16[512...) custom-call(bf16[512,256]{1,0:T(8,128)(2,1)S(1)} %get-tuple-element.65, ...), custom_call_target="tpu_custom_call" | custom-call | flops 2200000000 | bytes 7119872 | tf_op jit(solution)/shard_map/pallas_call | solution.py:404
  13.4 0.0 collective-permute-done.got_ref
  13.4 0.1 shard_map.184.g0
  13.5 1.4 %collective-permute-start.5 = (bf16[544,256]{1,0:T(8,128)(2,1)S(1)}, bf16[544,256]{1,0:T(8,128)(2,1)S(1)}, u32[]{:S(2)}, u32[]{:S(2)}) collective-permute-start(bf16[544,256]{1,0:T(8,128)(2,1)S(1)} %shard_map.184.g0), channel_id=1, source_target_pairs={{1,2},{2,1},{3,0},{0,3},{5,6},{6,5},{7,4},{4,7},{9,10},{10,9},{11,... | collective-permute-start | bytes 835592 | tf_op jit(solution)/shard_map/ppermute | solution.py:486
  14.9 0.0 collective-permute-done.1.ra
  14.9 0.0 collective-permute-done.2.rb
  14.9 0.0 collective-permute-done.3.rw
  14.9 0.0 collective-permute-done.4.re
  14.9 4.8 %shard_map.185 = (f32[2048,512]{1,0:T(8,128)S(1)}, bf16[512,512]{1,0:T(8,128)(2,1)S(1)}, f32[512,256]{1,0:T(8,128)S(1)}, bf16[256,256]{1,0:T(8,128)(2,1)S(1)}, b...) custom-call(f32[2048,512]{1,0:T(8,128)S(1)} %get-tuple-element.73.part_ref, ...), custom_call_target="tpu_custom_call" | custom-call | flops 3200000000 | bytes 13126672 | tf_op jit(solution)/shard_map/pallas_call | solution.py:404
  19.7 1.1 collective-permute-done.5.g1
  20.9 0.0 collective-permute-start.6
  20.9 1.4 %collective-permute-start.7 = (bf16[256,256]{1,0:T(8,128)(2,1)S(1)}, bf16[256,256]{1,0:T(8,128)(2,1)S(1)}, u32[]{:S(2)}, u32[]{:S(2)}) collective-permute-start(bf16[256,256]{1,0:T(8,128)(2,1)S(1)} %get-tuple-element.83.lower_ref), channel_id=1, source_target_pairs={{1,2},{2,1},{3,0},{0,3},{5,6},{6,5},{7,4},{4,7},{9,10},{10,9},{11,... | collective-permute-start | bytes 393224 | tf_op jit(solution)/shard_map/ppermute | solution.py:509
  22.3 2.7 %collective-permute-done.6.near_ref = bf16[256,256]{1,0:T(8,128)(2,1)S(1)} collective-permute-done((bf16[256,256]{1,0:T(8,128)(2,1)S(1)}, bf16[256,256]{1,0:T(8,128)(2,1)S(1)}, u32[]{:S(2)}, u32[]{:S(2)}) %collective-permute-start.6) | collective-permute-done | bytes 131104 | tf_op jit(solution)/shard_map/ppermute | solution.py:508
  25.0 2.6 %collective-permute-done.7.far_ref = bf16[256,256]{1,0:T(8,128)(2,1)S(1)} collective-permute-done((bf16[256,256]{1,0:T(8,128)(2,1)S(1)}, bf16[256,256]{1,0:T(8,128)(2,1)S(1)}, u32[]{:S(2)}, u32[]{:S(2)}) %collective-permute-start.7) | collective-permute-done | bytes 131104 | tf_op jit(solution)/shard_map/ppermute | solution.py:509
  27.6 0.1 shard_map.186
  27.6 1.2 %collective-permute-start.8 = (bf16[256,256]{1,0:T(8,128)(2,1)S(1)}, bf16[256,256]{1,0:T(8,128)(2,1)S(1)}, u32[]{:S(2)}, u32[]{:S(2)}) collective-permute-start(bf16[256,256]{1,0:T(8,128)(2,1)S(1)} %get-tuple-element.84.p0), channel_id=1, source_target_pairs={{1,2},{2,1},{3,0},{0,3},{5,6},{6,5},{7,4},{4,7},{9,10},{10,9},{11,... | collective-permute-start | bytes 393224 | tf_op jit(solution)/shard_map/ppermute | solution.py:516
  28.9 0.0 collective-permute-start.9
  28.9 3.9 %collective-permute-done.8.p1 = bf16[256,256]{1,0:T(8,128)(2,1)S(1)} collective-permute-done((bf16[256,256]{1,0:T(8,128)(2,1)S(1)}, bf16[256,256]{1,0:T(8,128)(2,1)S(1)}, u32[]{:S(2)}, u32[]{:S(2)}) %collective-permute-start.8) | collective-permute-done | bytes 131104 | tf_op jit(solution)/shard_map/ppermute | solution.py:516
  32.7 1.3 %collective-permute-done.9.q1 = bf16[256,256]{1,0:T(8,128)(2,1)S(1)} collective-permute-done((bf16[256,256]{1,0:T(8,128)(2,1)S(1)}, bf16[256,256]{1,0:T(8,128)(2,1)S(1)}, u32[]{:S(2)}, u32[]{:S(2)}) %collective-permute-start.9) | collective-permute-done | bytes 131104 | tf_op jit(solution)/shard_map/ppermute | solution.py:516
  34.1 14.0 %shard_map.187 = (f32[512,256]{1,0:T(8,128)S(1)}, f32[2,384,128]{2,1,0:T(8,128)S(1)}) custom-call(bf16[256,256]{1,0:T(8,128)(2,1)S(1)} %get-tuple-element.84.p0, bf16[256,256]{1,0:T(8,128)(2,1)S(1)} %collective-permute-done.8.p1, bf16[256,256]{1,0:T(8,128)(2,1)S(1)} %get-tuple-element.85.q0, bf16[256,256]{1,0:T(8,128)(2,1)S(1)} %collective-permute-done.9.q1, ...), custom_call_target="tpu_custom_call" | custom-call | flops 10000000000 | bytes 3075088 | tf_op jit(solution)/shard_map/pallas_call | solution.py:404
  48.1 6.5 %shard_map.188 = (f32[512,256]{1,0:T(8,128)S(1)}, bf16[2176,128]{1,0:T(8,128)(2,1)S(1)}, f32[1920,128]{1,0:T(8,128)S(1)}, bf16[128,256]{1,0:T(8,128)(2,1)S(1)}, ...) custom-call(f32[512,256]{1,0:T(8,128)S(1)} %get-tuple-element.93.grad_fine_ref, ...), custom_call_target="tpu_custom_call" | custom-call | flops 5600000000 | bytes 10535952 | tf_op jit(solution)/shard_map/pallas_call | solution.py:404
  54.6 7.4 %collective-permute-start.10 = (bf16[2176,128]{1,0:T(8,128)(2,1)S(1)}, bf16[2176,128]{1,0:T(8,128)(2,1)S(1)}, u32[]{:S(2)}, u32[]{:S(2)}) collective-permute-start(bf16[2176,128]{1,0:T(8,128)(2,1)S(1)} %get-tuple-element.100), channel_id=1, source_target_pairs={{0,4},{4,0},{1,5},{5,1},{2,6},{6,2},{3,7},{7,3},{8,12},{12,8},{9,1... | collective-permute-start | bytes 1671176 | tf_op jit(solution)/shard_map/ppermute | solution.py:426
  61.9 1.6 %collective-permute-done.10.got_ref.from_core = bf16[2176,128]{1,0:T(8,128)(2,1)S(1)} collective-permute-done((bf16[2176,128]{1,0:T(8,128)(2,1)S(1)}, bf16[2176,128]{1,0:T(8,128)(2,1)S(1)}, u32[]{:S(2)}, u32[]{:S(2)}) %collective-permute-start.10) | collective-permute-done | bytes 557088 | tf_op jit(solution)/shard_map/ppermute | solution.py:426
  63.5 0.7 shard_map.189
  64.2 0.1 collective-permute-start.11
  64.3 2.7 %collective-permute-start.13 = (bf16[640,128]{1,0:T(8,128)(2,1)S(1)}, bf16[640,128]{1,0:T(8,128)(2,1)S(1)}, u32[]{:S(2)}, u32[]{:S(2)}) collective-permute-start(bf16[640,128]{1,0:T(8,128)(2,1)S(1)} %get-tuple-element.106), channel_id=1, source_target_pairs={{0,3},{1,0},{2,1},{3,2},{4,7},{5,4},{6,5},{7,6},{8,11},{9,8},{10,9... | collective-permute-start | bytes 491528 | tf_op jit(solution)/shard_map/ppermute | solution.py:426
  66.9 0.1 collective-permute-start.12
  67.0 0.0 collective-permute-start.14
  67.0 6.0 %collective-permute-done.12 = bf16[384,128]{1,0:T(8,128)(2,1)S(1)} collective-permute-done((bf16[384,128]{1,0:T(8,128)(2,1)S(1)}, bf16[384,128]{1,0:T(8,128)(2,1)S(1)}, u32[]{:S(2)}, u32[]{:S(2)}) %collective-permute-start.12) | collective-permute-done | bytes 98336 | tf_op jit(solution)/shard_map/ppermute | solution.py:426
  73.0 0.0 collective-permute-done.11.from_west
  73.0 0.0 collective-permute-done.13.from_east
  73.1 0.1 add_convert_fusion
  73.1 0.0 collective-permute-done.14.from_b
  73.2 11.5 %all_to_all.10 = bf16[16,48,128]{2,1,0:T(8,128)(2,1)S(1)} all-to-all(bf16[16,48,128]{2,1,0:T(8,128)(2,1)S(1)} %pad_maximum_fusion), channel_id=1, replica_groups=mesh['z'=4,'y'=4,'core'=2,'x'=4] {'z','y'}, dimensions={0} | all-to-all | bytes 393216 | tf_op jit(solution)/shard_map/all_to_all | solution.py:593
  84.7 0.1 broadcast_in_dim.17
  84.8 19.6 %all_to_all.11.mine_ref = bf16[64,48,128]{2,1,0:T(8,128)(2,1)S(1)} all-to-all(bf16[64,48,128]{2,1,0:T(8,128)(2,1)S(1)} %broadcast_in_dim.17), channel_id=1, replica_groups=mesh['z'=4,'y'=4,'core'=2,'x'=4] {'z','y','x'}, dimensions={0} | all-to-all | bytes 1572864 | tf_op jit(solution)/shard_map/all_to_all | solution.py:596
  104.4 3.3 %collective-permute-start.15 = (bf16[64,48,128]{2,1,0:T(8,128)(2,1)S(1)}, bf16[64,48,128]{2,1,0:T(8,128)(2,1)S(1)}, u32[]{:S(2)}, u32[]{:S(2)}) collective-permute-start(bf16[64,48,128]{2,1,0:T(8,128)(2,1)S(1)} %all_to_all.11.mine_ref), channel_id=1, source_target_pairs={{0,4},{4,0},{1,5},{5,1},{2,6},{6,2},{3,7},{7,3},{8,12},{12,8},{9,1... | collective-permute-start | bytes 2359304 | tf_op jit(solution)/shard_map/ppermute | solution.py:426
  107.7 1.7 %shard_map.190 = f32[512,256]{1,0:T(8,128)} custom-call(f32[512,256]{1,0:T(8,128)S(1)} %get-tuple-element.111.local_ref, bf16[2176,128]{1,0:T(8,128)(2,1)S(1)} %collective-permute-done.10.got_ref.from_core, bf16[128,256]{1,0:T(8,128)(2,1)S(1)} %collective-permute-done.14.from_b, bf16[640,128]{1,0:T(8,128)(2,1)S(1)} %collective-permute-done.11.from_west, ...), custom_call_target="tpu_custom_call" | custom-call | flops 200000000 | bytes 1999376 | tf_op jit(solution)/shard_map/pallas_call | solution.py:404
  109.3 0.3 collective-permute-done.15.other_ref
  109.6 2.5 %shard_map.191 = (f32[512,512]{1,0:T(8,128)}, f32[512,256]{1,0:T(8,128)}, f32[512,512]{1,0:T(8,128)}, f32[512,256]{1,0:T(8,128)}) custom-call(bf16[64,48,128]{2,1,0:T(8,128)(2,1)S(1)} %all_to_all.11.mine_ref, bf16[64,48,128]{2,1,0:T(8,128)(2,1)S(1)} %collective-permute-done.15.other_ref, s32[4]{0:T(128)S(1)} %pad_add_fusion.refs_5_.place_ref), custom_call_target="tpu_custom_call" | custom-call | flops 200000000 | bytes 4718608 | tf_op jit(solution)/shard_map/pallas_call | solution.py:404
  (3 shorter events, 0.1 us)
Async XLA Ops:
  3.8 9.6 %collective-permute-start = (bf16[544,256]{1,0:T(8,128)(2,1)S(1)}, bf16[544,256]{1,0:T(8,128)(2,1)S(1)}, u32[]{:S(2)}, u32[]{:S(2)}) collective-permute-start(bf16[544,256]{1,0:T(8,128)(2,1)S(1)} %get-tuple-element.70.mine_ref), channel_id=1, source_target_pairs={{0,1},{1,0},{2,3},{3,2},{4,5},{5,4},{6,7},{7,6},{8,9},{9,8},{10,11... | collective-permute-start | bytes 835592 | tf_op jit(solution)/shard_map/ppermute | solution.py:470
  5.9 9.0 %collective-permute-start.1 = (bf16[128,256]{1,0:T(8,128)(2,1)S(1)}, bf16[128,256]{1,0:T(8,128)(2,1)S(1)}, u32[]{:S(2)}, u32[]{:S(2)}) collective-permute-start(bf16[128,256]{1,0:T(8,128)(2,1)S(1)} %get-tuple-element.75), channel_id=1, source_target_pairs={{0,4},{4,0},{1,5},{5,1},{2,6},{6,2},{3,7},{7,3},{8,12},{12,8},{9,1... | collective-permute-start | bytes 196616 | tf_op jit(solution)/shard_map/ppermute | solution.py:426
  6.9 8.0 %collective-permute-start.2 = (bf16[128,256]{1,0:T(8,128)(2,1)S(1)}, bf16[128,256]{1,0:T(8,128)(2,1)S(1)}, u32[]{:S(2)}, u32[]{:S(2)}) collective-permute-start(bf16[128,256]{1,0:T(8,128)(2,1)S(1)} %get-tuple-element.75), channel_id=1, source_target_pairs={{4,8},{12,16},{20,24},{28,32},{36,40},{44,48},{52,56},{60,64},{68,... | collective-permute-start | bytes 196616 | tf_op jit(solution)/shard_map/ppermute | solution.py:473
  8.1 6.8 %collective-permute-start.3 = (bf16[128,256]{1,0:T(8,128)(2,1)S(1)}, bf16[128,256]{1,0:T(8,128)(2,1)S(1)}, u32[]{:S(2)}, u32[]{:S(2)}) collective-permute-start(bf16[128,256]{1,0:T(8,128)(2,1)S(1)} %get-tuple-element.75), channel_id=1, source_target_pairs={{0,1},{1,2},{2,3},{3,0},{4,5},{5,6},{6,7},{7,4},{8,9},{9,10},{10,1... | collective-permute-start | bytes 196616 | tf_op jit(solution)/shard_map/ppermute | solution.py:426
  8.3 6.6 %collective-permute-start.4 = (bf16[128,256]{1,0:T(8,128)(2,1)S(1)}, bf16[128,256]{1,0:T(8,128)(2,1)S(1)}, u32[]{:S(2)}, u32[]{:S(2)}) collective-permute-start(bf16[128,256]{1,0:T(8,128)(2,1)S(1)} %get-tuple-element.75), channel_id=1, source_target_pairs={{0,3},{1,0},{2,1},{3,2},{4,7},{5,4},{6,5},{7,6},{8,11},{9,8},{10,9... | collective-permute-start | bytes 196616 | tf_op jit(solution)/shard_map/ppermute | solution.py:426
  13.5 7.4 %collective-permute-start.5 = (bf16[544,256]{1,0:T(8,128)(2,1)S(1)}, bf16[544,256]{1,0:T(8,128)(2,1)S(1)}, u32[]{:S(2)}, u32[]{:S(2)}) collective-permute-start(bf16[544,256]{1,0:T(8,128)(2,1)S(1)} %shard_map.184.g0), channel_id=1, source_target_pairs={{1,2},{2,1},{3,0},{0,3},{5,6},{6,5},{7,4},{4,7},{9,10},{10,9},{11,... | collective-permute-start | bytes 835592 | tf_op jit(solution)/shard_map/ppermute | solution.py:486
  20.9 4.1 %collective-permute-start.6 = (bf16[256,256]{1,0:T(8,128)(2,1)S(1)}, bf16[256,256]{1,0:T(8,128)(2,1)S(1)}, u32[]{:S(2)}, u32[]{:S(2)}) collective-permute-start(bf16[256,256]{1,0:T(8,128)(2,1)S(1)} %get-tuple-element.82.upper_ref), channel_id=1, source_target_pairs={{0,1},{1,0},{2,3},{3,2},{4,5},{5,4},{6,7},{7,6},{8,9},{9,8},{10,11... | collective-permute-start | bytes 393224 | tf_op jit(solution)/shard_map/ppermute | solution.py:508
  20.9 6.7 %collective-permute-start.7 = (bf16[256,256]{1,0:T(8,128)(2,1)S(1)}, bf16[256,256]{1,0:T(8,128)(2,1)S(1)}, u32[]{:S(2)}, u32[]{:S(2)}) collective-permute-start(bf16[256,256]{1,0:T(8,128)(2,1)S(1)} %get-tuple-element.83.lower_ref), channel_id=1, source_target_pairs={{1,2},{2,1},{3,0},{0,3},{5,6},{6,5},{7,4},{4,7},{9,10},{10,9},{11,... | collective-permute-start | bytes 393224 | tf_op jit(solution)/shard_map/ppermute | solution.py:509
  27.6 5.1 %collective-permute-start.8 = (bf16[256,256]{1,0:T(8,128)(2,1)S(1)}, bf16[256,256]{1,0:T(8,128)(2,1)S(1)}, u32[]{:S(2)}, u32[]{:S(2)}) collective-permute-start(bf16[256,256]{1,0:T(8,128)(2,1)S(1)} %get-tuple-element.84.p0), channel_id=1, source_target_pairs={{1,2},{2,1},{3,0},{0,3},{5,6},{6,5},{7,4},{4,7},{9,10},{10,9},{11,... | collective-permute-start | bytes 393224 | tf_op jit(solution)/shard_map/ppermute | solution.py:516
  28.9 5.2 %collective-permute-start.9 = (bf16[256,256]{1,0:T(8,128)(2,1)S(1)}, bf16[256,256]{1,0:T(8,128)(2,1)S(1)}, u32[]{:S(2)}, u32[]{:S(2)}) collective-permute-start(bf16[256,256]{1,0:T(8,128)(2,1)S(1)} %get-tuple-element.85.q0), channel_id=1, source_target_pairs={{0,1},{1,0},{2,3},{3,2},{4,5},{5,4},{6,7},{7,6},{8,9},{9,8},{10,11... | collective-permute-start | bytes 393224 | tf_op jit(solution)/shard_map/ppermute | solution.py:516
  54.6 9.0 %collective-permute-start.10 = (bf16[2176,128]{1,0:T(8,128)(2,1)S(1)}, bf16[2176,128]{1,0:T(8,128)(2,1)S(1)}, u32[]{:S(2)}, u32[]{:S(2)}) collective-permute-start(bf16[2176,128]{1,0:T(8,128)(2,1)S(1)} %get-tuple-element.100), channel_id=1, source_target_pairs={{0,4},{4,0},{1,5},{5,1},{2,6},{6,2},{3,7},{7,3},{8,12},{12,8},{9,1... | collective-permute-start | bytes 1671176 | tf_op jit(solution)/shard_map/ppermute | solution.py:426
  64.2 8.9 %collective-permute-start.11 = (bf16[640,128]{1,0:T(8,128)(2,1)S(1)}, bf16[640,128]{1,0:T(8,128)(2,1)S(1)}, u32[]{:S(2)}, u32[]{:S(2)}) collective-permute-start(bf16[640,128]{1,0:T(8,128)(2,1)S(1)} %get-tuple-element.104), channel_id=1, source_target_pairs={{0,1},{1,2},{2,3},{3,0},{4,5},{5,6},{6,7},{7,4},{8,9},{9,10},{10,1... | collective-permute-start | bytes 491528 | tf_op jit(solution)/shard_map/ppermute | solution.py:426
  64.3 8.8 %collective-permute-start.13 = (bf16[640,128]{1,0:T(8,128)(2,1)S(1)}, bf16[640,128]{1,0:T(8,128)(2,1)S(1)}, u32[]{:S(2)}, u32[]{:S(2)}) collective-permute-start(bf16[640,128]{1,0:T(8,128)(2,1)S(1)} %get-tuple-element.106), channel_id=1, source_target_pairs={{0,3},{1,0},{2,1},{3,2},{4,7},{5,4},{6,5},{7,6},{8,11},{9,8},{10,9... | collective-permute-start | bytes 491528 | tf_op jit(solution)/shard_map/ppermute | solution.py:426
  66.9 6.1 %collective-permute-start.12 = (bf16[384,128]{1,0:T(8,128)(2,1)S(1)}, bf16[384,128]{1,0:T(8,128)(2,1)S(1)}, u32[]{:S(2)}, u32[]{:S(2)}) collective-permute-start(bf16[384,128]{1,0:T(8,128)(2,1)S(1)} %get-tuple-element.105), channel_id=1, source_target_pairs={{0,2},{1,3},{2,0},{3,1},{4,6},{5,7},{6,4},{7,5},{8,10},{9,11},{10,... | collective-permute-start | bytes 294920 | tf_op jit(solution)/shard_map/ppermute | solution.py:426
  67.0 6.1 %collective-permute-start.14 = (bf16[128,256]{1,0:T(8,128)(2,1)S(1)}, bf16[128,256]{1,0:T(8,128)(2,1)S(1)}, u32[]{:S(2)}, u32[]{:S(2)}) collective-permute-start(bf16[128,256]{1,0:T(8,128)(2,1)S(1)} %get-tuple-element.108), channel_id=1, source_target_pairs={{4,8},{12,16},{20,24},{28,32},{36,40},{44,48},{52,56},{60,64},{68,... | collective-permute-start | bytes 196616 | tf_op jit(solution)/shard_map/ppermute | solution.py:566
  104.4 5.2 %collective-permute-start.15 = (bf16[64,48,128]{2,1,0:T(8,128)(2,1)S(1)}, bf16[64,48,128]{2,1,0:T(8,128)(2,1)S(1)}, u32[]{:S(2)}, u32[]{:S(2)}) collective-permute-start(bf16[64,48,128]{2,1,0:T(8,128)(2,1)S(1)} %all_to_all.11.mine_ref), channel_id=1, source_target_pairs={{0,4},{4,0},{1,5},{5,1},{2,6},{6,2},{3,7},{7,3},{8,12},{12,8},{9,1... | collective-permute-start | bytes 2359304 | tf_op jit(solution)/shard_map/ppermute | solution.py:426

commit v9 on v8

--- a/solution.py
+++ b/solution.py
@@ -12,7 +12,8 @@
 EPS = 1e-05
 CNODE = 512
 CHUNK = 1024
-LIMITS = (20, 20, 36, 22)
+FINE_CHUNK = 2048
+LIMITS = (28, 28, 36, 30)
 BF = jnp.bfloat16
 F32 = jnp.float32
 
@@ -117,8 +118,8 @@
 
 def own_kernel(own_ref, src_ref, target_ref, w1_ref, part_ref, left_ref):
     nodes, feature = own_ref.shape
-    for at in range(0, src_ref.shape[1], CHUNK):
-        here = slice(at, at + CHUNK)
+    for at in range(0, src_ref.shape[1], FINE_CHUNK):
+        here = slice(at, at + FINE_CHUNK)
         left = dot(pick_matrix(src_ref[:, here], nodes), own_ref[...]).astype(BF)
         left_ref[here, :] = left
         right = dot(pick_matrix(target_ref[:, here], nodes), own_ref[...]).astype(BF)
@@ -140,8 +141,8 @@
     east = re[...].astype(F32) * jnp.where(col < 3, 1.0, 0.0)
     table[nodes + 2 * rim : nodes + 3 * rim, :] = west.astype(BF)
     table[nodes + 3 * rim :, :] = east.astype(BF)
-    for at in range(0, src_ref.shape[1], CHUNK):
-        here = slice(at, at + CHUNK)
+    for at in range(0, src_ref.shape[1], FINE_CHUNK):
+        here = slice(at, at + FINE_CHUNK)
         picks = pick_matrix(src_ref[:, here] - nodes, 4 * rim)
         left = dot(picks, table[nodes:, :]).astype(BF)
         pair_ref[here, :] = left + left_ref[here, :]
@@ -242,8 +243,8 @@
     core = place_ref[1]
     grad_fine = grad_fine_ref[...]
     grad_summed = summed_grad(grad_fine, gain_ref[...], summed_ref[...])
-    for at in range(0, src_ref.shape[1], CHUNK):
-        here = slice(at, at + CHUNK)
+    for at in range(0, src_ref.shape[1], FINE_CHUNK):
+        here = slice(at, at + FINE_CHUNK)
         target = target_ref[:, here]
         grad_message = dot(pick_matrix(target, nodes), grad_summed).astype(BF)
         grad_preact = (dot_rt(grad_message, w2_ref[...]) * slope_ref[here, :]).astype(BF)

time: 112 us -> 113 us (level)
  no operation moved by 1% of the time
where the time goes in v9:
time: 113 us; the launch traced here: 112 us
  Pallas kernels  35.8 us (32%)
  blocking collectives  31 us (27%)
  starting transfers between devices  24.5 us (22%)
  waiting for transfers between devices  19.4 us (17%)
  between operations  1.42 us (1%)
    pallas_call x10, Pallas kernels, run(): pl.pallas_call(body if copies else kernel, out_shape=shapes, in_specs=[pl...  35.8 us
    all_to_all x1, blocking collectives, shards(): mine = lax.all_to_all(copies, CHIPS, 0, 0, tiled=True)  19.8 us
    ppermute x8, starting transfers between devices, send(): lax.ppermute(value, axis, [(i, (i + step) % size) for i in range(size)])  17.2 us
    all_to_all x1, blocking collectives, shards(): both = lax.all_to_all(both, PLANE, 0, 0, tiled=True)  11.2 us
    ppermute x8, waiting for transfers between devices, send(): lax.ppermute(value, axis, [(i, (i + step) % size) for i in range(size)])  7.8 us
    ppermute x2, waiting for transfers between devices, shards(): got = [lax.ppermute(first, 'x', far), lax.ppermute(second, 'x', near)]  5.28 us
    ppermute x1, waiting for transfers between devices, shards(): near_got = lax.ppermute(upper, 'x', near)  2.74 us
    ppermute x1, waiting for transfers between devices, shards(): far_got = lax.ppermute(lower, 'x', far)  2.59 us
  transfers between devices with their start and end apart: 16, of which 8 were waited for; matrix products, arithmetic and copies ran while one was open for 0% of the time, Pallas kernels for 8%

profile of v9, /device:TPU:1, one launch (start us, length us, event | category | flops | bytes accessed | tf_op | source)
XLA Modules:
  0.0 112.4 jit_solution(8703326539522468636)
XLA Ops:
  1.3 0.1 pad_add_fusion.refs_5_.place_ref
  1.4 2.4 %shard_map.182 = (bf16[128,256]{1,0:T(8,128)(2,1)S(1)}, bf16[544,256]{1,0:T(8,128)(2,1)S(1)}, s32[1,2048]{1,0:T(1,128)S(1)}, bf16[512,256]{1,0:T(8,128)(2,1)S(1)...) custom-call(bf16[512,256]{1,0:T(8,128)(2,1)} %bitcast.15, ...), custom_call_target="tpu_custom_call" | custom-call | flops 200000000 | bytes 1947664 | tf_op jit(solution)/shard_map/pallas_call | solution.py:405
  3.8 2.1 %collective-permute-start = (bf16[544,256]{1,0:T(8,128)(2,1)S(1)}, bf16[544,256]{1,0:T(8,128)(2,1)S(1)}, u32[]{:S(2)}, u32[]{:S(2)}) collective-permute-start(bf16[544,256]{1,0:T(8,128)(2,1)S(1)} %get-tuple-element.70.mine_ref), channel_id=1, source_target_pairs={{0,1},{1,0},{2,3},{3,2},{4,5},{5,4},{6,7},{7,6},{8,9},{9,8},{10,11... | collective-permute-start | bytes 835592 | tf_op jit(solution)/shard_map/ppermute | solution.py:471
  5.9 1.0 collective-permute-start.1
  6.9 1.2 %collective-permute-start.2 = (bf16[128,256]{1,0:T(8,128)(2,1)S(1)}, bf16[128,256]{1,0:T(8,128)(2,1)S(1)}, u32[]{:S(2)}, u32[]{:S(2)}) collective-permute-start(bf16[128,256]{1,0:T(8,128)(2,1)S(1)} %get-tuple-element.75), channel_id=1, source_target_pairs={{4,8},{12,16},{20,24},{28,32},{36,40},{44,48},{52,56},{60,64},{68,... | collective-permute-start | bytes 196616 | tf_op jit(solution)/shard_map/ppermute | solution.py:474
  8.1 0.3 collective-permute-start.3
  8.3 2.4 %collective-permute-start.4 = (bf16[128,256]{1,0:T(8,128)(2,1)S(1)}, bf16[128,256]{1,0:T(8,128)(2,1)S(1)}, u32[]{:S(2)}, u32[]{:S(2)}) collective-permute-start(bf16[128,256]{1,0:T(8,128)(2,1)S(1)} %get-tuple-element.75), channel_id=1, source_target_pairs={{0,3},{1,0},{2,1},{3,2},{4,7},{5,4},{6,5},{7,6},{8,11},{9,8},{10,9... | collective-permute-start | bytes 196616 | tf_op jit(solution)/shard_map/ppermute | solution.py:427
  10.7 2.7 %shard_map.183 = (f32[2048,512]{1,0:T(8,128)S(1)}, bf16[2048,256]{1,0:T(8,128)(2,1)S(1)}, s32[1,3072]{1,0:T(1,128)S(1)}, s32[1,3072]{1,0:T(1,128)S(1)}, bf16[512...) custom-call(bf16[512,256]{1,0:T(8,128)(2,1)S(1)} %get-tuple-element.65, ...), custom_call_target="tpu_custom_call" | custom-call | flops 2200000000 | bytes 7119872 | tf_op jit(solution)/shard_map/pallas_call | solution.py:405
  13.4 0.0 collective-permute-done.got_ref
  13.4 0.1 shard_map.184.g0
  13.5 1.3 %collective-permute-start.5 = (bf16[544,256]{1,0:T(8,128)(2,1)S(1)}, bf16[544,256]{1,0:T(8,128)(2,1)S(1)}, u32[]{:S(2)}, u32[]{:S(2)}) collective-permute-start(bf16[544,256]{1,0:T(8,128)(2,1)S(1)} %shard_map.184.g0), channel_id=1, source_target_pairs={{1,2},{2,1},{3,0},{0,3},{5,6},{6,5},{7,4},{4,7},{9,10},{10,9},{11,... | collective-permute-start | bytes 835592 | tf_op jit(solution)/shard_map/ppermute | solution.py:487
  14.9 0.0 collective-permute-done.1.ra
  14.9 0.0 collective-permute-done.2.rb
  14.9 0.0 collective-permute-done.3.rw
  14.9 0.0 collective-permute-done.4.re
  14.9 5.0 %shard_map.185 = (f32[2048,512]{1,0:T(8,128)S(1)}, bf16[512,512]{1,0:T(8,128)(2,1)S(1)}, f32[512,256]{1,0:T(8,128)S(1)}, bf16[256,256]{1,0:T(8,128)(2,1)S(1)}, b...) custom-call(f32[2048,512]{1,0:T(8,128)S(1)} %get-tuple-element.73.part_ref, ...), custom_call_target="tpu_custom_call" | custom-call | flops 3200000000 | bytes 13126672 | tf_op jit(solution)/shard_map/pallas_call | solution.py:405
  19.9 1.0 collective-permute-done.5.g1
  20.9 0.0 collective-permute-start.6
  20.9 1.4 %collective-permute-start.7 = (bf16[256,256]{1,0:T(8,128)(2,1)S(1)}, bf16[256,256]{1,0:T(8,128)(2,1)S(1)}, u32[]{:S(2)}, u32[]{:S(2)}) collective-permute-start(bf16[256,256]{1,0:T(8,128)(2,1)S(1)} %get-tuple-element.83.lower_ref), channel_id=1, source_target_pairs={{1,2},{2,1},{3,0},{0,3},{5,6},{6,5},{7,4},{4,7},{9,10},{10,9},{11,... | collective-permute-start | bytes 393224 | tf_op jit(solution)/shard_map/ppermute | solution.py:510
  22.3 2.7 %collective-permute-done.6.near_ref = bf16[256,256]{1,0:T(8,128)(2,1)S(1)} collective-permute-done((bf16[256,256]{1,0:T(8,128)(2,1)S(1)}, bf16[256,256]{1,0:T(8,128)(2,1)S(1)}, u32[]{:S(2)}, u32[]{:S(2)}) %collective-permute-start.6) | collective-permute-done | bytes 131104 | tf_op jit(solution)/shard_map/ppermute | solution.py:509
  25.0 2.6 %collective-permute-done.7.far_ref = bf16[256,256]{1,0:T(8,128)(2,1)S(1)} collective-permute-done((bf16[256,256]{1,0:T(8,128)(2,1)S(1)}, bf16[256,256]{1,0:T(8,128)(2,1)S(1)}, u32[]{:S(2)}, u32[]{:S(2)}) %collective-permute-start.7) | collective-permute-done | bytes 131104 | tf_op jit(solution)/shard_map/ppermute | solution.py:510
  27.6 0.1 shard_map.186
  27.7 1.3 %collective-permute-start.8 = (bf16[256,256]{1,0:T(8,128)(2,1)S(1)}, bf16[256,256]{1,0:T(8,128)(2,1)S(1)}, u32[]{:S(2)}, u32[]{:S(2)}) collective-permute-start(bf16[256,256]{1,0:T(8,128)(2,1)S(1)} %get-tuple-element.84.p0), channel_id=1, source_target_pairs={{1,2},{2,1},{3,0},{0,3},{5,6},{6,5},{7,4},{4,7},{9,10},{10,9},{11,... | collective-permute-start | bytes 393224 | tf_op jit(solution)/shard_map/ppermute | solution.py:517
  29.0 0.0 collective-permute-start.9
  29.0 3.8 %collective-permute-done.8.p1 = bf16[256,256]{1,0:T(8,128)(2,1)S(1)} collective-permute-done((bf16[256,256]{1,0:T(8,128)(2,1)S(1)}, bf16[256,256]{1,0:T(8,128)(2,1)S(1)}, u32[]{:S(2)}, u32[]{:S(2)}) %collective-permute-start.8) | collective-permute-done | bytes 131104 | tf_op jit(solution)/shard_map/ppermute | solution.py:517
  32.8 1.5 %collective-permute-done.9.q1 = bf16[256,256]{1,0:T(8,128)(2,1)S(1)} collective-permute-done((bf16[256,256]{1,0:T(8,128)(2,1)S(1)}, bf16[256,256]{1,0:T(8,128)(2,1)S(1)}, u32[]{:S(2)}, u32[]{:S(2)}) %collective-permute-start.9) | collective-permute-done | bytes 131104 | tf_op jit(solution)/shard_map/ppermute | solution.py:517
  34.3 13.9 %shard_map.187 = (f32[512,256]{1,0:T(8,128)S(1)}, f32[2,384,128]{2,1,0:T(8,128)S(1)}) custom-call(bf16[256,256]{1,0:T(8,128)(2,1)S(1)} %get-tuple-element.84.p0, bf16[256,256]{1,0:T(8,128)(2,1)S(1)} %collective-permute-done.8.p1, bf16[256,256]{1,0:T(8,128)(2,1)S(1)} %get-tuple-element.85.q0, bf16[256,256]{1,0:T(8,128)(2,1)S(1)} %collective-permute-done.9.q1, ...), custom_call_target="tpu_custom_call" | custom-call | flops 10000000000 | bytes 3075088 | tf_op jit(solution)/shard_map/pallas_call | solution.py:405
  48.2 6.8 %shard_map.188 = (f32[512,256]{1,0:T(8,128)S(1)}, bf16[2176,128]{1,0:T(8,128)(2,1)S(1)}, f32[1920,128]{1,0:T(8,128)S(1)}, bf16[128,256]{1,0:T(8,128)(2,1)S(1)}, ...) custom-call(f32[512,256]{1,0:T(8,128)S(1)} %get-tuple-element.93.grad_fine_ref, ...), custom_call_target="tpu_custom_call" | custom-call | flops 5600000000 | bytes 10535952 | tf_op jit(solution)/shard_map/pallas_call | solution.py:405
  55.0 7.3 %collective-permute-start.10 = (bf16[2176,128]{1,0:T(8,128)(2,1)S(1)}, bf16[2176,128]{1,0:T(8,128)(2,1)S(1)}, u32[]{:S(2)}, u32[]{:S(2)}) collective-permute-start(bf16[2176,128]{1,0:T(8,128)(2,1)S(1)} %get-tuple-element.100), channel_id=1, source_target_pairs={{0,4},{4,0},{1,5},{5,1},{2,6},{6,2},{3,7},{7,3},{8,12},{12,8},{9,1... | collective-permute-start | bytes 1671176 | tf_op jit(solution)/shard_map/ppermute | solution.py:427
  62.3 1.6 %collective-permute-done.10.got_ref.from_core = bf16[2176,128]{1,0:T(8,128)(2,1)S(1)} collective-permute-done((bf16[2176,128]{1,0:T(8,128)(2,1)S(1)}, bf16[2176,128]{1,0:T(8,128)(2,1)S(1)}, u32[]{:S(2)}, u32[]{:S(2)}) %collective-permute-start.10) | collective-permute-done | bytes 557088 | tf_op jit(solution)/shard_map/ppermute | solution.py:427
  63.9 0.7 shard_map.189
  64.6 0.1 collective-permute-start.11
  64.6 2.7 %collective-permute-start.13 = (bf16[640,128]{1,0:T(8,128)(2,1)S(1)}, bf16[640,128]{1,0:T(8,128)(2,1)S(1)}, u32[]{:S(2)}, u32[]{:S(2)}) collective-permute-start(bf16[640,128]{1,0:T(8,128)(2,1)S(1)} %get-tuple-element.106), channel_id=1, source_target_pairs={{0,3},{1,0},{2,1},{3,2},{4,7},{5,4},{6,5},{7,6},{8,11},{9,8},{10,9... | collective-permute-start | bytes 491528 | tf_op jit(solution)/shard_map/ppermute | solution.py:427
  67.3 0.0 collective-permute-start.12
  67.3 0.0 collective-permute-start.14
  67.3 5.9 %collective-permute-done.12 = bf16[384,128]{1,0:T(8,128)(2,1)S(1)} collective-permute-done((bf16[384,128]{1,0:T(8,128)(2,1)S(1)}, bf16[384,128]{1,0:T(8,128)(2,1)S(1)}, u32[]{:S(2)}, u32[]{:S(2)}) %collective-permute-start.12) | collective-permute-done | bytes 98336 | tf_op jit(solution)/shard_map/ppermute | solution.py:427
  73.3 0.0 collective-permute-done.11.from_west
  73.3 0.0 collective-permute-done.13.from_east
  73.3 0.1 add_convert_fusion
  73.4 0.0 collective-permute-done.14.from_b
  73.4 11.2 %all_to_all.10 = bf16[16,48,128]{2,1,0:T(8,128)(2,1)S(1)} all-to-all(bf16[16,48,128]{2,1,0:T(8,128)(2,1)S(1)} %pad_maximum_fusion), channel_id=1, replica_groups=mesh['z'=4,'y'=4,'core'=2,'x'=4] {'z','y'}, dimensions={0} | all-to-all | bytes 393216 | tf_op jit(solution)/shard_map/all_to_all | solution.py:594
  84.6 0.1 broadcast_in_dim.17
  84.7 19.8 %all_to_all.11.mine_ref = bf16[64,48,128]{2,1,0:T(8,128)(2,1)S(1)} all-to-all(bf16[64,48,128]{2,1,0:T(8,128)(2,1)S(1)} %broadcast_in_dim.17), channel_id=1, replica_groups=mesh['z'=4,'y'=4,'core'=2,'x'=4] {'z','y','x'}, dimensions={0} | all-to-all | bytes 1572864 | tf_op jit(solution)/shard_map/all_to_all | solution.py:597
  104.5 3.4 %collective-permute-start.15 = (bf16[64,48,128]{2,1,0:T(8,128)(2,1)S(1)}, bf16[64,48,128]{2,1,0:T(8,128)(2,1)S(1)}, u32[]{:S(2)}, u32[]{:S(2)}) collective-permute-start(bf16[64,48,128]{2,1,0:T(8,128)(2,1)S(1)} %all_to_all.11.mine_ref), channel_id=1, source_target_pairs={{0,4},{4,0},{1,5},{5,1},{2,6},{6,2},{3,7},{7,3},{8,12},{12,8},{9,1... | collective-permute-start | bytes 2359304 | tf_op jit(solution)/shard_map/ppermute | solution.py:427
  107.9 1.7 %shard_map.190 = f32[512,256]{1,0:T(8,128)} custom-call(f32[512,256]{1,0:T(8,128)S(1)} %get-tuple-element.111.local_ref, bf16[2176,128]{1,0:T(8,128)(2,1)S(1)} %collective-permute-done.10.got_ref.from_core, bf16[128,256]{1,0:T(8,128)(2,1)S(1)} %collective-permute-done.14.from_b, bf16[640,128]{1,0:T(8,128)(2,1)S(1)} %collective-permute-done.11.from_west, ...), custom_call_target="tpu_custom_call" | custom-call | flops 200000000 | bytes 1999376 | tf_op jit(solution)/shard_map/pallas_call | solution.py:405
  109.6 0.3 collective-permute-done.15.other_ref
  109.9 2.5 %shard_map.191 = (f32[512,512]{1,0:T(8,128)}, f32[512,256]{1,0:T(8,128)}, f32[512,512]{1,0:T(8,128)}, f32[512,256]{1,0:T(8,128)}) custom-call(bf16[64,48,128]{2,1,0:T(8,128)(2,1)S(1)} %all_to_all.11.mine_ref, bf16[64,48,128]{2,1,0:T(8,128)(2,1)S(1)} %collective-permute-done.15.other_ref, s32[4]{0:T(128)S(1)} %pad_add_fusion.refs_5_.place_ref), custom_call_target="tpu_custom_call" | custom-call | flops 200000000 | bytes 4718608 | tf_op jit(solution)/shard_map/pallas_call | solution.py:405
  (3 shorter events, 0.1 us)
Async XLA Ops:
  3.8 9.6 %collective-permute-start = (bf16[544,256]{1,0:T(8,128)(2,1)S(1)}, bf16[544,256]{1,0:T(8,128)(2,1)S(1)}, u32[]{:S(2)}, u32[]{:S(2)}) collective-permute-start(bf16[544,256]{1,0:T(8,128)(2,1)S(1)} %get-tuple-element.70.mine_ref), channel_id=1, source_target_pairs={{0,1},{1,0},{2,3},{3,2},{4,5},{5,4},{6,7},{7,6},{8,9},{9,8},{10,11... | collective-permute-start | bytes 835592 | tf_op jit(solution)/shard_map/ppermute | solution.py:471
  5.9 9.0 %collective-permute-start.1 = (bf16[128,256]{1,0:T(8,128)(2,1)S(1)}, bf16[128,256]{1,0:T(8,128)(2,1)S(1)}, u32[]{:S(2)}, u32[]{:S(2)}) collective-permute-start(bf16[128,256]{1,0:T(8,128)(2,1)S(1)} %get-tuple-element.75), channel_id=1, source_target_pairs={{0,4},{4,0},{1,5},{5,1},{2,6},{6,2},{3,7},{7,3},{8,12},{12,8},{9,1... | collective-permute-start | bytes 196616 | tf_op jit(solution)/shard_map/ppermute | solution.py:427
  6.9 8.0 %collective-permute-start.2 = (bf16[128,256]{1,0:T(8,128)(2,1)S(1)}, bf16[128,256]{1,0:T(8,128)(2,1)S(1)}, u32[]{:S(2)}, u32[]{:S(2)}) collective-permute-start(bf16[128,256]{1,0:T(8,128)(2,1)S(1)} %get-tuple-element.75), channel_id=1, source_target_pairs={{4,8},{12,16},{20,24},{28,32},{36,40},{44,48},{52,56},{60,64},{68,... | collective-permute-start | bytes 196616 | tf_op jit(solution)/shard_map/ppermute | solution.py:474
  8.1 6.8 %collective-permute-start.3 = (bf16[128,256]{1,0:T(8,128)(2,1)S(1)}, bf16[128,256]{1,0:T(8,128)(2,1)S(1)}, u32[]{:S(2)}, u32[]{:S(2)}) collective-permute-start(bf16[128,256]{1,0:T(8,128)(2,1)S(1)} %get-tuple-element.75), channel_id=1, source_target_pairs={{0,1},{1,2},{2,3},{3,0},{4,5},{5,6},{6,7},{7,4},{8,9},{9,10},{10,1... | collective-permute-start | bytes 196616 | tf_op jit(solution)/shard_map/ppermute | solution.py:427
  8.3 6.6 %collective-permute-start.4 = (bf16[128,256]{1,0:T(8,128)(2,1)S(1)}, bf16[128,256]{1,0:T(8,128)(2,1)S(1)}, u32[]{:S(2)}, u32[]{:S(2)}) collective-permute-start(bf16[128,256]{1,0:T(8,128)(2,1)S(1)} %get-tuple-element.75), channel_id=1, source_target_pairs={{0,3},{1,0},{2,1},{3,2},{4,7},{5,4},{6,5},{7,6},{8,11},{9,8},{10,9... | collective-permute-start | bytes 196616 | tf_op jit(solution)/shard_map/ppermute | solution.py:427
  13.5 7.4 %collective-permute-start.5 = (bf16[544,256]{1,0:T(8,128)(2,1)S(1)}, bf16[544,256]{1,0:T(8,128)(2,1)S(1)}, u32[]{:S(2)}, u32[]{:S(2)}) collective-permute-start(bf16[544,256]{1,0:T(8,128)(2,1)S(1)} %shard_map.184.g0), channel_id=1, source_target_pairs={{1,2},{2,1},{3,0},{0,3},{5,6},{6,5},{7,4},{4,7},{9,10},{10,9},{11,... | collective-permute-start | bytes 835592 | tf_op jit(solution)/shard_map/ppermute | solution.py:487
  20.9 4.1 %collective-permute-start.6 = (bf16[256,256]{1,0:T(8,128)(2,1)S(1)}, bf16[256,256]{1,0:T(8,128)(2,1)S(1)}, u32[]{:S(2)}, u32[]{:S(2)}) collective-permute-start(bf16[256,256]{1,0:T(8,128)(2,1)S(1)} %get-tuple-element.82.upper_ref), channel_id=1, source_target_pairs={{0,1},{1,0},{2,3},{3,2},{4,5},{5,4},{6,7},{7,6},{8,9},{9,8},{10,11... | collective-permute-start | bytes 393224 | tf_op jit(solution)/shard_map/ppermute | solution.py:509
  20.9 6.7 %collective-permute-start.7 = (bf16[256,256]{1,0:T(8,128)(2,1)S(1)}, bf16[256,256]{1,0:T(8,128)(2,1)S(1)}, u32[]{:S(2)}, u32[]{:S(2)}) collective-permute-start(bf16[256,256]{1,0:T(8,128)(2,1)S(1)} %get-tuple-element.83.lower_ref), channel_id=1, source_target_pairs={{1,2},{2,1},{3,0},{0,3},{5,6},{6,5},{7,4},{4,7},{9,10},{10,9},{11,... | collective-permute-start | bytes 393224 | tf_op jit(solution)/shard_map/ppermute | solution.py:510
  27.7 5.1 %collective-permute-start.8 = (bf16[256,256]{1,0:T(8,128)(2,1)S(1)}, bf16[256,256]{1,0:T(8,128)(2,1)S(1)}, u32[]{:S(2)}, u32[]{:S(2)}) collective-permute-start(bf16[256,256]{1,0:T(8,128)(2,1)S(1)} %get-tuple-element.84.p0), channel_id=1, source_target_pairs={{1,2},{2,1},{3,0},{0,3},{5,6},{6,5},{7,4},{4,7},{9,10},{10,9},{11,... | collective-permute-start | bytes 393224 | tf_op jit(solution)/shard_map/ppermute | solution.py:517
  29.0 5.3 %collective-permute-start.9 = (bf16[256,256]{1,0:T(8,128)(2,1)S(1)}, bf16[256,256]{1,0:T(8,128)(2,1)S(1)}, u32[]{:S(2)}, u32[]{:S(2)}) collective-permute-start(bf16[256,256]{1,0:T(8,128)(2,1)S(1)} %get-tuple-element.85.q0), channel_id=1, source_target_pairs={{0,1},{1,0},{2,3},{3,2},{4,5},{5,4},{6,7},{7,6},{8,9},{9,8},{10,11... | collective-permute-start | bytes 393224 | tf_op jit(solution)/shard_map/ppermute | solution.py:517
  55.0 8.9 %collective-permute-start.10 = (bf16[2176,128]{1,0:T(8,128)(2,1)S(1)}, bf16[2176,128]{1,0:T(8,128)(2,1)S(1)}, u32[]{:S(2)}, u32[]{:S(2)}) collective-permute-start(bf16[2176,128]{1,0:T(8,128)(2,1)S(1)} %get-tuple-element.100), channel_id=1, source_target_pairs={{0,4},{4,0},{1,5},{5,1},{2,6},{6,2},{3,7},{7,3},{8,12},{12,8},{9,1... | collective-permute-start | bytes 1671176 | tf_op jit(solution)/shard_map/ppermute | solution.py:427
  64.6 8.7 %collective-permute-start.11 = (bf16[640,128]{1,0:T(8,128)(2,1)S(1)}, bf16[640,128]{1,0:T(8,128)(2,1)S(1)}, u32[]{:S(2)}, u32[]{:S(2)}) collective-permute-start(bf16[640,128]{1,0:T(8,128)(2,1)S(1)} %get-tuple-element.104), channel_id=1, source_target_pairs={{0,1},{1,2},{2,3},{3,0},{4,5},{5,6},{6,7},{7,4},{8,9},{9,10},{10,1... | collective-permute-start | bytes 491528 | tf_op jit(solution)/shard_map/ppermute | solution.py:427
  64.6 8.7 %collective-permute-start.13 = (bf16[640,128]{1,0:T(8,128)(2,1)S(1)}, bf16[640,128]{1,0:T(8,128)(2,1)S(1)}, u32[]{:S(2)}, u32[]{:S(2)}) collective-permute-start(bf16[640,128]{1,0:T(8,128)(2,1)S(1)} %get-tuple-element.106), channel_id=1, source_target_pairs={{0,3},{1,0},{2,1},{3,2},{4,7},{5,4},{6,5},{7,6},{8,11},{9,8},{10,9... | collective-permute-start | bytes 491528 | tf_op jit(solution)/shard_map/ppermute | solution.py:427
  67.3 6.0 %collective-permute-start.12 = (bf16[384,128]{1,0:T(8,128)(2,1)S(1)}, bf16[384,128]{1,0:T(8,128)(2,1)S(1)}, u32[]{:S(2)}, u32[]{:S(2)}) collective-permute-start(bf16[384,128]{1,0:T(8,128)(2,1)S(1)} %get-tuple-element.105), channel_id=1, source_target_pairs={{0,2},{1,3},{2,0},{3,1},{4,6},{5,7},{6,4},{7,5},{8,10},{9,11},{10,... | collective-permute-start | bytes 294920 | tf_op jit(solution)/shard_map/ppermute | solution.py:427
  67.3 6.1 %collective-permute-start.14 = (bf16[128,256]{1,0:T(8,128)(2,1)S(1)}, bf16[128,256]{1,0:T(8,128)(2,1)S(1)}, u32[]{:S(2)}, u32[]{:S(2)}) collective-permute-start(bf16[128,256]{1,0:T(8,128)(2,1)S(1)} %get-tuple-element.108), channel_id=1, source_target_pairs={{4,8},{12,16},{20,24},{28,32},{36,40},{44,48},{52,56},{60,64},{68,... | collective-permute-start | bytes 196616 | tf_op jit(solution)/shard_map/ppermute | solution.py:567
  104.5 5.3 %collective-permute-start.15 = (bf16[64,48,128]{2,1,0:T(8,128)(2,1)S(1)}, bf16[64,48,128]{2,1,0:T(8,128)(2,1)S(1)}, u32[]{:S(2)}, u32[]{:S(2)}) collective-permute-start(bf16[64,48,128]{2,1,0:T(8,128)(2,1)S(1)} %all_to_all.11.mine_ref), channel_id=1, source_target_pairs={{0,4},{4,0},{1,5},{5,1},{2,6},{6,2},{3,7},{7,3},{8,12},{12,8},{9,1... | collective-permute-start | bytes 2359304 | tf_op jit(solution)/shard_map/ppermute | solution.py:427
